TPU v7x, 32 devices: a whole 2x2x4 slice. The times are simulated.
32 devices in a mesh: seq: 8 (over z, x), fsdp: 4 (over y, core).
Axes of the slice: x: 2, y: 2, z: 4, core: 2. Of those that a mesh axis runs over, the one named last changes fastest.
Arguments:
- layer_input: bfloat16 [4, 1024, 2880], P('fsdp', 'seq'), may hold values from -6 to 6
- attn_gain: bfloat16 [2880], P('fsdp'), may hold values from 0.25 to 1.75
- query_matrix: bfloat16 [2880, 4096], P(None, ('seq', 'fsdp')), may hold values from -0.109375 to 0.109375
- query_bias_vector: bfloat16 [4096], P(('seq', 'fsdp')), may hold values from -3 to 3
- key_matrix: bfloat16 [2880, 512], P(None, ('seq', 'fsdp')), may hold values from -0.109375 to 0.109375
- key_bias_vector: bfloat16 [512], P(('seq', 'fsdp')), may hold values from -3 to 3
- value_matrix: bfloat16 [2880, 512], P(None, ('seq', 'fsdp')), may hold values from -0.109375 to 0.109375
- value_bias_vector: bfloat16 [512], P(('seq', 'fsdp')), may hold values from -1.75 to 1.75
- sink_logit_values: bfloat16 [64], P('fsdp'), may hold values from -4 to 4
- output_matrix: bfloat16 [4096, 2880], P(('seq', 'fsdp')), may hold values from -0.375 to 0.375
- output_bias_vector: bfloat16 [2880], P('fsdp'), may hold values from -1.75 to 1.75
- ffn_gain: bfloat16 [2880], P('fsdp'), may hold values from 0.25 to 1.75
- router_weight: bfloat16 [2880, 8], P('fsdp'), may hold values from -0.0546875 to 0.0546875
- router_bias: bfloat16 [8], P('fsdp'), may hold values from -1.5 to 1.5
- expert_gate_up: bfloat16 [8, 2, 2880, 2880], P('seq', None, None, 'fsdp'), may hold values from -0.109375 to 0.109375
- expert_gate_up_bias: bfloat16 [8, 2, 2880], P('seq', None, 'fsdp'), may hold values from -1.25 to 1.25
- expert_down: bfloat16 [8, 2880, 2880], P('seq', 'fsdp'), may hold values from -0.21875 to 0.21875
- expert_down_bias: bfloat16 [8, 2880], P(None, 'fsdp'), may hold values from -1.25 to 1.25
- route_ids: int32 [4, 1024, 4], P('fsdp', 'seq'), may hold values from 0 to 7, all different within a row; in each aligned block of 128 rows (0 to 127, 128 to 255, ..., all dimensions but the last counted through in order) at most 80 rows name the same one
- doc_lengths: int32 [4, 3], replicated, may hold values from 1 to 960, 1024 in all within a row
- out_cotangent: bfloat16 [4, 1024, 2880], P('fsdp', 'seq'), may hold values from -6 to 6
Outputs:
- layer_output: bfloat16 [4, 1024, 2880], P('fsdp', 'seq')
- input_grad: float32 [4, 1024, 2880], P('fsdp', 'seq')
- attn_gain_grad: float32 [2880], P('fsdp')
- query_weight_grad: float32 [2880, 4096], P(None, ('seq', 'fsdp'))
- query_bias_grad: float32 [4096], P(('seq', 'fsdp'))
- key_weight_grad: float32 [2880, 512], P(None, ('seq', 'fsdp'))
- key_bias_grad: float32 [512], P(('seq', 'fsdp'))
- value_weight_grad: float32 [2880, 512], P(None, ('seq', 'fsdp'))
- value_bias_grad: float32 [512], P(('seq', 'fsdp'))
- sink_grad: float32 [64], P('fsdp')
- output_weight_grad: float32 [4096, 2880], P(('seq', 'fsdp'))
- output_bias_grad: float32 [2880], P('fsdp')
- ffn_gain_grad: float32 [2880], P('fsdp')
- router_weight_grad: float32 [2880, 8], P('fsdp')
- router_bias_grad: float32 [8], P('fsdp')
- expert_gate_up_grad: float32 [8, 2, 2880, 2880], P('seq', None, None, 'fsdp')
- expert_gate_up_bias_grad: float32 [8, 2, 2880], P('seq', None, 'fsdp')
- expert_down_grad: float32 [8, 2880, 2880], P('seq', 'fsdp')
- expert_down_bias_grad: float32 [8, 2880], P(None, 'fsdp')
Inputs may be any that keep to these rules, and one draw needn't show every extreme that they name: `route_ids`: in the 128 rows of one device no expert is named more than 80 times; some expert is named exactly 80 times. `doc_lengths`: each row sums to 1024; its largest entry is 960.
All inputs are finite; a program needn't handle non-finite values.
Results may differ from a plain program's by a relative error of at most 0.024.
Values may be sent and summed in bfloat16 or wider, within the bound.
No kernel may reach another device: no remote copies, remote signals or barrier semaphores. Data moves between devices by JAX's collectives and lax.ppermute only.
A program may use at most 384 MiB of HBM per device.

v0:
```python
import jax
import jax.numpy as jnp
from jax import lax
from jax.sharding import PartitionSpec as P

QUERY_HEADS = 64
KEY_VALUE_HEADS = 8
HEAD_DIM = 64
WINDOW_LENGTH = 128


ROPE_BASE = 150000.0
NORM_EPS = 1e-05
GLU_ALPHA = 1.702
GLU_LIMIT = 7.0
EXACT_PRECISION = lax.Precision.HIGHEST


def from_behind(block, axis, distance):
    devices = range(lax.axis_size(axis))
    route = [(i - distance, i) for i in devices if i - distance in devices]
    return lax.ppermute(block, axis, route)


def rms_scale(values):
    return lax.rsqrt(jnp.mean(values * values, axis=-1, keepdims=True) + NORM_EPS)


def rope_tables(positions):
    frequency = ROPE_BASE ** (-jnp.arange(HEAD_DIM // 2, dtype=jnp.float32) * 2.0 / HEAD_DIM)
    angles = positions.astype(jnp.float32)[:, None] * frequency[None, :]
    return (jnp.cos(angles), jnp.sin(angles))


def apply_rotary(values, cosine_values, sine_values, direction):
    half_size = values.shape[-1] // 2
    first_half = values[..., :half_size]
    second = values[..., half_size:]
    cosine_b = cosine_values[:, None, :]
    sine_b = direction * sine_values[:, None, :]
    return jnp.concatenate(
        [first_half * cosine_b - second * sine_b, second * cosine_b + first_half * sine_b], axis=-1
    )


def swiglu(gate_pre, up_pre):
    gate_soft = GLU_LIMIT - jax.nn.softplus(GLU_LIMIT - gate_pre)
    up_soft = GLU_LIMIT * jnp.tanh(up_pre / GLU_LIMIT)
    return (up_soft + 1.0) * gate_soft * jax.nn.sigmoid(GLU_ALPHA * gate_soft)


def contract_last(left, right, matmul_precision=None):
    return lax.dot_general(
        left,
        right,
        (((1,), (1,)), ((), ())),
        precision=matmul_precision,
        preferred_element_type=jnp.float32,
    )


def contract_first(left, right, matmul_precision=None):
    return lax.dot_general(
        left,
        right,
        (((0,), (0,)), ((), ())),
        precision=matmul_precision,
        preferred_element_type=jnp.float32,
    )


def masked_scores(query_grid, key_all, allowed):
    scores = (
        jnp.einsum("nqhgd,nkhd->nhgqk", query_grid, key_all, preferred_element_type=jnp.float32)
        * 0.125
    )
    return jnp.where(allowed[:, None, None], scores, -1e30)


def fan_out(rows_buffer, copies):
    row_count = rows_buffer.shape[0]
    spread = jnp.broadcast_to(rows_buffer[:, None], (row_count, copies) + rows_buffer.shape[1:])
    return spread.reshape((row_count * copies,) + rows_buffer.shape[1:])


def to_experts(buffer):
    return lax.all_to_all(buffer, ("seq", "fsdp"), split_axis=0, concat_axis=0, tiled=True)


def from_experts(partials):
    return lax.all_to_all(partials, ("seq", "fsdp"), split_axis=0, concat_axis=0, tiled=True)


def token_columns(
    query_matrix,
    query_bias_vector,
    key_matrix,
    key_bias_vector,
    value_matrix,
    value_bias_vector,
    output_matrix,
):
    return (
        lax.all_gather(query_matrix, ("seq", "fsdp"), axis=1, tiled=True),
        lax.all_gather(query_bias_vector, ("seq", "fsdp"), axis=0, tiled=True),
        lax.all_gather(key_matrix, ("seq", "fsdp"), axis=1, tiled=True),
        lax.all_gather(key_bias_vector, ("seq", "fsdp"), axis=0, tiled=True),
        lax.all_gather(value_matrix, ("seq", "fsdp"), axis=1, tiled=True),
        lax.all_gather(value_bias_vector, ("seq", "fsdp"), axis=0, tiled=True),
        lax.all_gather(output_matrix, ("seq", "fsdp"), axis=0, tiled=True),
    )


def window_mask(doc_rows, positions, key_pos):
    doc_ends = jnp.cumsum(doc_rows, axis=1)
    query_doc = jnp.sum(
        (positions[None, :, None] >= doc_ends[:, None, :]).astype(jnp.int32), axis=2
    )
    key_doc = jnp.sum((key_pos[None, :, None] >= doc_ends[:, None, :]).astype(jnp.int32), axis=2)
    offset = positions[:, None] - key_pos[None, :]
    inside = (key_pos[None, :] >= 0) & (offset >= 0) & (offset <= WINDOW_LENGTH)
    return inside[None] & (query_doc[:, :, None] == key_doc[:, None, :])


def attend(query_grid, keys_own, values_own, sink_logit_grid, allowed):
    sets_count, rows_count, kv_heads, query_groups, head_size = query_grid.shape
    kv_width = kv_heads * head_size
    key_value = jnp.stack(
        [
            keys_own.reshape(sets_count, rows_count, kv_width),
            values_own.reshape(sets_count, rows_count, kv_width),
        ],
        axis=2,
    )
    halo_kv = from_behind(key_value, "seq", 1)
    all_kv = jnp.concatenate([halo_kv, key_value], axis=1)
    keys_count = rows_count + WINDOW_LENGTH
    key_all = all_kv[:, :, 0].reshape(sets_count, keys_count, kv_heads, head_size)
    value_all = all_kv[:, :, 1].reshape(sets_count, keys_count, kv_heads, head_size)
    scores = masked_scores(query_grid, key_all, allowed)
    sink_col = sink_logit_grid[None, :, :, None]
    top_score = jnp.maximum(jnp.max(scores, axis=-1), sink_col)
    exp_scores = jnp.exp(scores - top_score[..., None])
    denominator = jnp.sum(exp_scores, axis=-1) + jnp.exp(sink_col - top_score)
    probabilities = exp_scores / denominator[..., None]
    log_total = top_score + jnp.log(denominator)
    head_output = jnp.einsum(
        "nhgqk,nkhd->nqhgd",
        probabilities.astype(jnp.bfloat16),
        value_all,
        preferred_element_type=jnp.float32,
    )
    head_output = head_output.reshape(
        sets_count, rows_count, kv_heads * query_groups * head_size
    ).astype(jnp.bfloat16)
    return (head_output, key_all, value_all, log_total)


def attend_back(
    query_grid, key_all, value_all, sink_logit_grid, allowed, log_total, grad_heads_grid
):
    sets_count, rows_count, kv_heads, query_groups, head_size = query_grid.shape
    keys_count = key_all.shape[1]
    kv_width = kv_heads * head_size
    scores_again = masked_scores(query_grid, key_all, allowed)
    probs_again = jnp.exp(scores_again - log_total[..., None])
    sink_prob = jnp.exp(sink_logit_grid[None, :, :, None] - log_total)
    grad_probs = jnp.einsum(
        "nqhgd,nkhd->nhgqk", grad_heads_grid, value_all, preferred_element_type=jnp.float32
    )
    row_delta = jnp.sum(probs_again * grad_probs, axis=-1)
    grad_scores = (probs_again * (grad_probs - row_delta[..., None])).astype(jnp.bfloat16)
    sink_grad = -jnp.sum(sink_prob * row_delta, axis=(0, 3)).reshape(kv_heads * query_groups)
    grad_query = (
        jnp.einsum("nhgqk,nkhd->nqhgd", grad_scores, key_all, preferred_element_type=jnp.float32)
        * 0.125
    )
    grad_key = (
        jnp.einsum("nhgqk,nqhgd->nkhd", grad_scores, query_grid, preferred_element_type=jnp.float32)
        * 0.125
    )
    grad_value = jnp.einsum(
        "nhgqk,nqhgd->nkhd",
        probs_again.astype(jnp.bfloat16),
        grad_heads_grid,
        preferred_element_type=jnp.float32,
    )
    grad_kv = jnp.stack(
        [
            grad_key.reshape(sets_count, keys_count, kv_width),
            grad_value.reshape(sets_count, keys_count, kv_width),
        ],
        axis=2,
    )
    from_next = from_behind(grad_kv[:, :WINDOW_LENGTH], "seq", -1)
    own_kv = grad_kv[:, WINDOW_LENGTH:]
    own_kv = jnp.concatenate([own_kv[:, : rows_count - WINDOW_LENGTH], own_kv + from_next], axis=1)
    return (grad_query, own_kv[:, :, 0], own_kv[:, :, 1], sink_grad)


def per_device(
    layer_input,
    attn_gain,
    query_matrix,
    query_bias_vector,
    key_matrix,
    key_bias_vector,
    value_matrix,
    value_bias_vector,
    sink_logit_values,
    output_matrix,
    output_bias_vector,
    ffn_gain,
    router_weight,
    router_bias,
    expert_gate_up,
    expert_gate_up_bias,
    expert_down,
    expert_down_bias,
    route_ids,
    doc_lengths,
    out_cotangent,
):
    seq_count = lax.axis_size("seq")
    fsdp_count = lax.axis_size("fsdp")
    seq_index = lax.axis_index("seq")
    fsdp_index = lax.axis_index("fsdp")
    tokens_here = layer_input.shape[1]
    model_width = layer_input.shape[2]
    choose_count = route_ids.shape[2]
    capacity = max(2, tokens_here * choose_count * 5 // (4 * seq_count))
    query_groups = QUERY_HEADS // KEY_VALUE_HEADS
    (
        attn_gain_all,
        ffn_gain_all,
        out_bias_all,
        sinks_all,
        router_all,
        router_bias_all,
        down_bias_all,
    ) = (
        lax.all_gather(attn_gain, "fsdp", axis=0, tiled=True),
        lax.all_gather(ffn_gain, "fsdp", axis=0, tiled=True),
        lax.all_gather(output_bias_vector, "fsdp", axis=0, tiled=True),
        lax.all_gather(sink_logit_values, "fsdp", axis=0, tiled=True),
        lax.all_gather(router_weight, "fsdp", axis=0, tiled=True),
        lax.all_gather(router_bias, "fsdp", axis=0, tiled=True),
        lax.all_gather(expert_down_bias, "fsdp", axis=1, tiled=True),
    )
    attn_gain_f = attn_gain_all.astype(jnp.float32)
    ffn_gain_f = ffn_gain_all.astype(jnp.float32)
    router_f = router_all.astype(jnp.float32)
    resid_in = layer_input[0].astype(jnp.float32)
    norm_one = rms_scale(resid_in)
    unit_in = resid_in * norm_one
    normalized_input = (unit_in * attn_gain_f).astype(jnp.bfloat16)
    positions = seq_index * tokens_here + jnp.arange(tokens_here, dtype=jnp.int32)
    key_pos = (
        seq_index * tokens_here
        - WINDOW_LENGTH
        + jnp.arange(tokens_here + WINDOW_LENGTH, dtype=jnp.int32)
    )
    cosine_values, sine_values = rope_tables(positions)
    weights_now = token_columns(
        query_matrix,
        query_bias_vector,
        key_matrix,
        key_bias_vector,
        value_matrix,
        value_bias_vector,
        output_matrix,
    )
    rows_in = normalized_input[None]
    doc_rows = lax.dynamic_slice_in_dim(doc_lengths, fsdp_index, 1, 0)
    wq_now, bq_now, wk_now, bk_now, wv_now, bv_now, wo_now = weights_now
    sets_count = rows_in.shape[0]
    heads_here = wq_now.shape[1] // HEAD_DIM
    kv_here = wk_now.shape[1] // HEAD_DIM
    sinks_mine = sinks_all.astype(jnp.float32).reshape(kv_here, query_groups)
    allowed = window_mask(doc_rows, positions, key_pos)
    query_linear = jnp.einsum(
        "ntd,de->nte", rows_in, wq_now, preferred_element_type=jnp.float32
    ) + bq_now.astype(jnp.float32)
    key_linear = jnp.einsum(
        "ntd,de->nte", rows_in, wk_now, preferred_element_type=jnp.float32
    ) + bk_now.astype(jnp.float32)
    value_linear = jnp.einsum(
        "ntd,de->nte", rows_in, wv_now, preferred_element_type=jnp.float32
    ) + bv_now.astype(jnp.float32)
    query_rows = apply_rotary(
        query_linear.reshape(sets_count, tokens_here, heads_here, HEAD_DIM),
        cosine_values,
        sine_values,
        1.0,
    ).astype(jnp.bfloat16)
    keys_own = apply_rotary(
        key_linear.reshape(sets_count, tokens_here, kv_here, HEAD_DIM),
        cosine_values,
        sine_values,
        1.0,
    ).astype(jnp.bfloat16)
    values_own = value_linear.astype(jnp.bfloat16).reshape(
        sets_count, tokens_here, kv_here, HEAD_DIM
    )
    query_grid = query_rows.reshape(sets_count, tokens_here, kv_here, query_groups, HEAD_DIM)
    head_output, key_all, value_all, log_total = attend(
        query_grid, keys_own, values_own, sinks_mine, allowed
    )
    attn_part = jnp.einsum("nte,ed->ntd", head_output, wo_now, preferred_element_type=jnp.float32)
    attn_sum = attn_part[0]
    resid_mid = resid_in + attn_sum + out_bias_all.astype(jnp.float32)
    norm_two = rms_scale(resid_mid)
    unit_mid = resid_mid * norm_two
    normed_mid = (unit_mid * ffn_gain_f).astype(jnp.bfloat16)
    logits = jnp.dot(
        normed_mid, router_all, preferred_element_type=jnp.float32
    ) + router_bias_all.astype(jnp.float32)
    route_here = route_ids[0]
    onehot = (
        route_here[:, :, None] == jnp.arange(seq_count, dtype=jnp.int32)[None, None, :]
    ).astype(jnp.float32)
    picked = jnp.einsum("tke,te->tk", onehot, logits, precision=EXACT_PRECISION)
    gate_probs = jax.nn.softmax(picked, axis=-1)
    pair_onehot = onehot.reshape(tokens_here * choose_count, seq_count)
    pair_int = pair_onehot.astype(jnp.int32)
    before = jnp.cumsum(pair_int, axis=0) - pair_int
    slot_rank = jnp.sum(before * pair_int, axis=1)
    slot_index = route_here.reshape(-1) * capacity + slot_rank
    send_rows = (
        jnp.zeros((seq_count * capacity, model_width), jnp.bfloat16)
        .at[slot_index]
        .set(jnp.repeat(normed_mid, choose_count, axis=0))
    )
    arrived = to_experts(fan_out(send_rows.reshape(seq_count, capacity, model_width), fsdp_count))
    expert_rows = arrived.reshape(-1, model_width)
    gate_w = expert_gate_up[0, 0]
    up_w = expert_gate_up[0, 1]
    gate_pre = jnp.dot(
        expert_rows, gate_w, preferred_element_type=jnp.float32
    ) + expert_gate_up_bias[0, 0].astype(jnp.float32)
    up_pre = jnp.dot(expert_rows, up_w, preferred_element_type=jnp.float32) + expert_gate_up_bias[
        0, 1
    ].astype(jnp.float32)
    hidden = swiglu(gate_pre, up_pre).astype(jnp.bfloat16)
    partial_out = jnp.dot(hidden, expert_down[0], preferred_element_type=jnp.float32)
    returned = from_experts(partial_out.reshape(-1, capacity, model_width))
    summed = (
        jnp.sum(returned.reshape(seq_count, fsdp_count, capacity, model_width), axis=1)
        + down_bias_all.astype(jnp.float32)[:, None, :]
    )
    expert_out = summed.astype(jnp.bfloat16).reshape(seq_count * capacity, model_width)
    pair_out = (
        expert_out[slot_index].astype(jnp.float32).reshape(tokens_here, choose_count, model_width)
    )
    mixture = jnp.einsum("tk,tkd->td", gate_probs, pair_out, precision=EXACT_PRECISION)
    layer_output = (resid_mid + mixture).astype(jnp.bfloat16)[None]
    grad_out = out_cotangent[0].astype(jnp.float32)
    grad_gates = jnp.einsum("td,tkd->tk", grad_out, pair_out, precision=EXACT_PRECISION)
    grad_pairs = (
        (gate_probs[:, :, None] * grad_out[:, None, :])
        .astype(jnp.bfloat16)
        .reshape(tokens_here * choose_count, model_width)
    )
    down_bias_grad = jnp.einsum(
        "pe,pd->ed", pair_onehot, grad_pairs.astype(jnp.float32), precision=EXACT_PRECISION
    )
    grad_buffer = (
        jnp.zeros((seq_count * capacity, model_width), jnp.bfloat16).at[slot_index].set(grad_pairs)
    )
    grad_arrived = to_experts(
        fan_out(grad_buffer.reshape(seq_count, capacity, model_width), fsdp_count)
    )
    grad_arrived = grad_arrived.reshape(-1, model_width)
    grad_hidden = contract_last(grad_arrived, expert_down[0])
    down_grad = contract_first(hidden, grad_arrived)
    _, glu_back = jax.vjp(swiglu, gate_pre, up_pre)
    grad_gate_pre, grad_up_pre = glu_back(grad_hidden)
    grad_gate_low = grad_gate_pre.astype(jnp.bfloat16)
    grad_up_low = grad_up_pre.astype(jnp.bfloat16)
    gate_up_grad = jnp.stack(
        [contract_first(expert_rows, grad_gate_low), contract_first(expert_rows, grad_up_low)],
        axis=0,
    )
    gate_up_bias_grad = jnp.stack(
        [
            jnp.sum(grad_gate_low.astype(jnp.float32), axis=0),
            jnp.sum(grad_up_low.astype(jnp.float32), axis=0),
        ],
        axis=0,
    )
    row_grad_part = contract_last(grad_gate_low, gate_w) + contract_last(grad_up_low, up_w)
    grad_back = from_experts(row_grad_part.reshape(-1, capacity, model_width))
    grad_rows = jnp.sum(
        grad_back.reshape(seq_count, fsdp_count, capacity, model_width), axis=1
    ).astype(jnp.bfloat16)
    grad_rows = grad_rows.reshape(seq_count * capacity, model_width)
    grad_normed_moe = jnp.sum(
        grad_rows[slot_index].astype(jnp.float32).reshape(tokens_here, choose_count, model_width),
        axis=1,
    )
    mean_gate = jnp.sum(gate_probs * grad_gates, axis=-1, keepdims=True)
    grad_picked = gate_probs * (grad_gates - mean_gate)
    grad_logits = jnp.einsum("tke,tk->te", onehot, grad_picked, precision=EXACT_PRECISION)
    router_grad = contract_first(normed_mid.astype(jnp.float32), grad_logits, EXACT_PRECISION)
    router_bias_grad = jnp.sum(grad_logits, axis=0)
    grad_normed_mid = grad_normed_moe + contract_last(grad_logits, router_f, EXACT_PRECISION)
    ffn_gain_grad = jnp.sum(grad_normed_mid * unit_mid, axis=0)
    grad_unit_mid = grad_normed_mid * ffn_gain_f
    grad_mid = (
        norm_two
        * (grad_unit_mid - unit_mid * jnp.mean(grad_unit_mid * unit_mid, axis=-1, keepdims=True))
        + grad_out
    )
    weights_back = token_columns(
        query_matrix,
        query_bias_vector,
        key_matrix,
        key_bias_vector,
        value_matrix,
        value_bias_vector,
        output_matrix,
    )
    wq_back = weights_back[0]
    wk_back = weights_back[2]
    wv_back = weights_back[4]
    wo_back = weights_back[6]
    grad_attn = grad_mid.astype(jnp.bfloat16)
    out_bias_grad = jnp.sum(grad_attn.astype(jnp.float32), axis=0)
    grad_attn_rows = grad_attn[None]
    out_w_grad = jnp.einsum(
        "nte,ntd->ed", head_output, grad_attn_rows, preferred_element_type=jnp.float32
    )
    grad_heads = jnp.einsum(
        "ntd,ed->nte", grad_attn_rows, wo_back, preferred_element_type=jnp.float32
    ).astype(jnp.bfloat16)
    grad_heads_grid = grad_heads.reshape(sets_count, tokens_here, kv_here, query_groups, HEAD_DIM)
    grad_query, grad_key_own, grad_value_own, sink_mine_grad = attend_back(
        query_grid, key_all, value_all, sinks_mine, allowed, log_total, grad_heads_grid
    )
    grad_key_lin = (
        apply_rotary(
            grad_key_own.reshape(sets_count, tokens_here, kv_here, HEAD_DIM),
            cosine_values,
            sine_values,
            -1.0,
        )
        .reshape(sets_count, tokens_here, kv_here * HEAD_DIM)
        .astype(jnp.bfloat16)
    )
    grad_value_lin = grad_value_own.astype(jnp.bfloat16)
    grad_query_lin = (
        apply_rotary(
            grad_query.reshape(sets_count, tokens_here, heads_here, HEAD_DIM),
            cosine_values,
            sine_values,
            -1.0,
        )
        .reshape(sets_count, tokens_here, heads_here * HEAD_DIM)
        .astype(jnp.bfloat16)
    )
    query_w_grad = jnp.einsum(
        "ntd,nte->de", rows_in, grad_query_lin, preferred_element_type=jnp.float32
    )
    key_w_grad = jnp.einsum(
        "ntd,nte->de", rows_in, grad_key_lin, preferred_element_type=jnp.float32
    )
    value_w_grad = jnp.einsum(
        "ntd,nte->de", rows_in, grad_value_lin, preferred_element_type=jnp.float32
    )
    query_b_grad = jnp.sum(grad_query_lin.astype(jnp.float32), axis=(0, 1))
    key_b_grad = jnp.sum(grad_key_lin.astype(jnp.float32), axis=(0, 1))
    value_b_grad = jnp.sum(grad_value_lin.astype(jnp.float32), axis=(0, 1))
    normed_part = (
        jnp.einsum("nte,de->ntd", grad_query_lin, wq_back, preferred_element_type=jnp.float32)
        + jnp.einsum("nte,de->ntd", grad_key_lin, wk_back, preferred_element_type=jnp.float32)
        + jnp.einsum("nte,de->ntd", grad_value_lin, wv_back, preferred_element_type=jnp.float32)
    )
    grad_normed_in = normed_part[0]
    attn_gain_grad = jnp.sum(grad_normed_in * unit_in, axis=0)
    grad_unit_in = grad_normed_in * attn_gain_f
    input_grad = (
        norm_one
        * (grad_unit_in - unit_in * jnp.mean(grad_unit_in * unit_in, axis=-1, keepdims=True))
        + grad_mid
    )
    query_w_own, query_b_own, key_w_own, key_b_own, value_w_own, value_b_own, out_w_own = (
        lax.psum_scatter(query_w_grad, ("seq", "fsdp"), scatter_dimension=1, tiled=True),
        lax.psum_scatter(query_b_grad, ("seq", "fsdp"), scatter_dimension=0, tiled=True),
        lax.psum_scatter(key_w_grad, ("seq", "fsdp"), scatter_dimension=1, tiled=True),
        lax.psum_scatter(key_b_grad, ("seq", "fsdp"), scatter_dimension=0, tiled=True),
        lax.psum_scatter(value_w_grad, ("seq", "fsdp"), scatter_dimension=1, tiled=True),
        lax.psum_scatter(value_b_grad, ("seq", "fsdp"), scatter_dimension=0, tiled=True),
        lax.psum_scatter(out_w_grad, ("seq", "fsdp"), scatter_dimension=0, tiled=True),
    )
    (
        gain_one_sum,
        gain_two_sum,
        out_bias_sum,
        sink_sum,
        router_sum,
        router_bias_sum,
        down_bias_sum,
    ) = lax.psum(
        (
            attn_gain_grad,
            ffn_gain_grad,
            out_bias_grad,
            sink_mine_grad,
            router_grad,
            router_bias_grad,
            down_bias_grad,
        ),
        ("seq", "fsdp"),
    )

    def own_part(whole_array, axis_number):
        piece_size = whole_array.shape[axis_number] // fsdp_count
        return lax.dynamic_slice_in_dim(
            whole_array, fsdp_index * piece_size, piece_size, axis_number
        )

    return (
        layer_output,
        input_grad[None],
        own_part(gain_one_sum, 0),
        query_w_own,
        query_b_own,
        key_w_own,
        key_b_own,
        value_w_own,
        value_b_own,
        own_part(sink_sum, 0),
        out_w_own,
        own_part(out_bias_sum, 0),
        own_part(gain_two_sum, 0),
        own_part(router_sum, 0),
        own_part(router_bias_sum, 0),
        gate_up_grad[None],
        gate_up_bias_grad[None],
        down_grad[None],
        own_part(down_bias_sum, 1),
    )


def solution(mesh):
    return jax.shard_map(
        per_device,
        mesh=mesh,
        in_specs=(
            P("fsdp", "seq", None),
            P("fsdp"),
            P(None, ("seq", "fsdp")),
            P(("seq", "fsdp")),
            P(None, ("seq", "fsdp")),
            P(("seq", "fsdp")),
            P(None, ("seq", "fsdp")),
            P(("seq", "fsdp")),
            P("fsdp"),
            P(("seq", "fsdp"), None),
            P("fsdp"),
            P("fsdp"),
            P("fsdp", None),
            P("fsdp"),
            P("seq", None, None, "fsdp"),
            P("seq", None, "fsdp"),
            P("seq", "fsdp", None),
            P(None, "fsdp"),
            P("fsdp", "seq", None),
            P(),
            P("fsdp", "seq", None),
        ),
        out_specs=(
            P("fsdp", "seq", None),
            P("fsdp", "seq", None),
            P("fsdp"),
            P(None, ("seq", "fsdp")),
            P(("seq", "fsdp")),
            P(None, ("seq", "fsdp")),
            P(("seq", "fsdp")),
            P(None, ("seq", "fsdp")),
            P(("seq", "fsdp")),
            P("fsdp"),
            P(("seq", "fsdp"), None),
            P("fsdp"),
            P("fsdp"),
            P("fsdp", None),
            P("fsdp"),
            P("seq", None, None, "fsdp"),
            P("seq", None, "fsdp"),
            P("seq", "fsdp", None),
            P(None, "fsdp"),
        ),
        check_vma=False,
    )
```

profile of v0, /device:TPU:0, one launch (start us, length us, event | category | flops | bytes accessed | tf_op | source)
XLA Modules:
  0.0 4059.7 jit_solution(3150039189755659501)
XLA Ops:
  18.5 13.5 all-reduce.13
  33.7 40.3 all-reduce.12
  83.3 50.2 %all-gather.10.cloned.1.call-done = bf16[2880,512]{0,1:T(8,128)(2,1)} async-done(((bf16[2880,16]{0,1:T(8,128)(2,1)}), bf16[2880,512]{0,1:T(8,128)(2,1)}) %all-gather.10.cloned.1.call-update) | async-done | bytes 2949136 | tf_op jit(solution)/shard_map/all_gather | solution.py:108
  140.3 38.2 all-gather
  179.3 108.1 %all-gather.12.cloned.1.call-done = bf16[2880,4096]{1,0:T(8,128)(2,1)} async-done(((bf16[2880,128]{1,0:T(8,128)(2,1)}), bf16[2880,4096]{1,0:T(8,128)(2,1)}) %all-gather.12.cloned.1.call-update) | async-done | bytes 23592976 | tf_op jit(solution)/shard_map/all_gather | solution.py:104
  309.5 128.0 %all-gather.14.cloned.1.call-done = bf16[4096,2880]{0,1:T(8,128)(2,1)} async-done(((bf16[128,2880]{0,1:T(8,128)(2,1)}), bf16[4096,2880]{0,1:T(8,128)(2,1)}) %all-gather.14.cloned.1.call-update) | async-done | bytes 23592976 | tf_op jit(solution)/shard_map/all_gather | solution.py:110
  476.6 329.0 %all-to-all-done = bf16[32,80,2880]{2,1,0:T(8,128)(2,1)} async-done(((bf16[32,80,2880]{2,1,0:T(8,128)(2,1)}), bf16[32,80,2880]{2,1,0:T(8,128)(2,1)}, u32[]{:S(2)}, u32[]{:S(2)}) %all-to-all-start) | async-done | bytes 14745632 | tf_op jit(solution)/shard_map/all_to_all | solution.py:87
  805.7 16.2 fusion.22
  821.9 26.6 multiply_convert_fusion.1
  854.6 20.9 fusion.16
  875.5 14.4 all-to-all-start.1
  889.9 169.5 %all-gather.2 = bf16[4,720,8]{1,2,0:T(8,128)(2,1)S(1)} all-gather(bf16[1,720,8]{1,2,0:T(8,128)(2,1)S(1)} %bitcast.305), channel_id=1, replica_groups=mesh['seq'=8,'fsdp'=4] {'fsdp'}, dimensions={0}, use_global_device_ids=true | all-gather | bytes 57600 | tf_op jit(solution)/shard_map/all_gather | solution.py:248
  1062.8 13.0 all-gather.1
  1088.8 455.2 %all-to-all-done.1 = f32[32,80,2880]{2,1,0:T(8,128)} async-done(((f32[32,80,2880]{2,1,0:T(8,128)}), f32[32,80,2880]{2,1,0:T(8,128)}, u32[]{:S(2)}, u32[]{:S(2)}) %all-to-all-start.1) | async-done | bytes 29491232 | tf_op jit(solution)/shard_map/all_to_all | solution.py:91
  1588.8 356.7 %all_to_all.20 = bf16[32,80,2880]{2,1,0:T(8,128)(2,1)} all-to-all(bf16[32,80,2880]{2,1,0:T(8,128)(2,1)S(1)} %bitcast.263), channel_id=1, replica_groups=mesh['seq'=8,'fsdp'=4] {'seq','fsdp'}, dimensions={0} | all-to-all | bytes 29491200 | tf_op jit(solution)/shard_map/all_to_all | solution.py:87
  1945.6 27.2 convert_reduce_fusion
  1972.8 20.2 fusion.20
  1992.9 28.3 convolution_add_fusion
  2021.3 29.9 copy.112
  2066.8 643.1 %all-to-all-done.3 = f32[32,80,2880]{2,1,0:T(8,128)} async-done(((f32[32,80,2880]{2,1,0:T(8,128)}), f32[32,80,2880]{2,1,0:T(8,128)}, u32[]{:S(2)}, u32[]{:S(2)}) %all-to-all-start.3) | async-done | bytes 29491232 | tf_op jit(solution)/shard_map/all_to_all | solution.py:91
  2709.9 13.9 bitcast_reduce_fusion
  2816.0 18.4 fusion.92
  2834.4 19.9 fusion.85
  2854.5 82.0 %all-reduce.16.cloned.1.call-done = (f32[2880,8]{0,1:T(8,128)}, f32[8,2880]{1,0:T(8,128)}) async-done(((f32[2880,8]{0,1:T(8,128)}, f32[8,2880]{1,0:T(8,128)}), (f32[2880,8]{0,1:T(8,128)}, f32[8,2880]{1,0:T(8,128)})) %all-reduce.16.cloned.1.call-update) | async-done | bytes 184336 | tf_op jit(solution)/shard_map/psum | solution.py:503
  2940.0 18.1 convolution_bitcast_fusion
  2958.1 17.2 convolution_bitcast_fusion.1
  2975.3 13.2 maximum_bitcast_fusion
  2988.6 13.9 convolution_bitcast_fusion.2
  3022.0 43.8 %all-reduce.10 = (f32[2880]{0:T(1024)S(1)}, f32[4096]{0:T(1024)S(1)}, f32[512]{0:T(512)S(1)}, f32[512]{0:T(512)S(1)}, f32[64]{0:T(128)S(1)}, /*index=5*/f32[2880]{0:T(1024)S(1)}, f32[2880]{0:T(1024)S(1)}, f32[8]{0:T(128)S(1)}) all-reduce(f32[2880]{0:T(1024)S(1)} %get-tuple-element.21, ...), channel_id=1, replica_groups=mesh['seq'=8,'fsdp'=4] {'seq','fsdp'}, use_global_device_ids=true, to_apply=%region_22.23 | all-reduce | flops 13832 | bytes 110656 | tf_op jit(solution)/shard_map/psum | solution.py:503
  3085.0 143.5 %reduce-scatter.9.cloned.1.call-done = f32[2880,16]{0,1:T(8,128)} async-done(((f32[2880,512]{0,1:T(8,128)}), f32[2880,16]{0,1:T(8,128)}) %reduce-scatter.9.cloned.1.call-update) | async-done | bytes 184336 | tf_op jit(solution)/shard_map/reduce_scatter | solution.py:491
  3228.6 410.2 %reduce-scatter.5.cloned.1.call-done = f32[2880,128]{1,0:T(8,128)} async-done(((f32[2880,4096]{1,0:T(8,128)}), f32[2880,128]{1,0:T(8,128)}) %reduce-scatter.5.cloned.1.call-update) | async-done | bytes 1474576 | tf_op jit(solution)/shard_map/reduce_scatter | solution.py:487
  3638.7 414.2 %reduce-scatter.11.cloned.1.call-done = f32[128,2880]{0,1:T(8,128)} async-done(((f32[4096,2880]{0,1:T(8,128)}), f32[128,2880]{0,1:T(8,128)}) %reduce-scatter.11.cloned.1.call-update) | async-done | bytes 1474576 | tf_op jit(solution)/shard_map/reduce_scatter | solution.py:493
  (345 shorter events, 305.4 us)
Async XLA Ops:
  7.2 71.9 %all-gather.8.cloned.1.call-start = ((), (), s32[]{:S(2)}) async-start(), calls=%async_computation.8 | async-start | bytes 3108864 | tf_op jit(solution)/shard_map/all_gather | solution.py:106
  7.9 125.6 %all-gather.10.cloned.1.call-start = ((), (), s32[]{:S(2)}) async-start(), calls=%async_computation.9 | async-start | bytes 3108864 | tf_op jit(solution)/shard_map/all_gather | solution.py:108
  8.7 124.8 %copy-start.3 = (bf16[1,128,2880]{1,2,0:T(8,128)(2,1)S(1)}, bf16[1,128,2880]{1,2,0:T(8,128)(2,1)}, u32[]{:S(2)}) copy-start(bf16[1,128,2880]{1,2,0:T(8,128)(2,1)} %param.21) | copy-start | bytes 2211844
  8.7 278.7 %all-gather.12.cloned.1.call-start = ((), (), s32[]{:S(2)}) async-start(), calls=%async_computation.10 | async-start | bytes 24330240 | tf_op jit(solution)/shard_map/all_gather | solution.py:104
  9.4 428.1 %all-gather.14.cloned.1.call-start = ((), (), s32[]{:S(2)}) async-start(), calls=%async_computation.11 | async-start | bytes 24330240 | tf_op jit(solution)/shard_map/all_gather | solution.py:110
  32.0 255.4 %copy-start.31 = (f32[2880]{0:T(1024)}, f32[2880]{0:T(1024)S(1)}, u32[]{:S(2)}) copy-start(f32[2880]{0:T(1024)S(1)} %convert_element_type.336) | copy-start | bytes 34564
  78.4 209.1 %copy-start.51 = (f32[128]{0:T(128)}, f32[128]{0:T(128)S(1)}, u32[]{:S(2)}) copy-start(f32[128]{0:T(128)S(1)} %add_rsqrt_fusion.1) | copy-start | bytes 1540
  79.1 222.1 %copy-start.42 = (f32[128,32]{0,1:T(8,128)}, f32[128,32]{0,1:T(8,128)S(1)}, u32[]{:S(2)}) copy-start(f32[128,32]{0,1:T(8,128)S(1)} %get-tuple-element.73) | copy-start | bytes 49156
  137.1 41.7 %collective-permute-start = (bf16[1,128,2,512]{3,1,2,0:T(8,128)(2,1)S(1)}, bf16[1,128,2,512]{3,1,2,0:T(8,128)(2,1)S(1)}, u32[]{:S(2)}, u32[]{:S(2)}) collective-permute-start(bf16[1,128,2,512]{3,1,2,0:T(8,128)(2,1)S(1)} %pad_maximum_fusion.4), channel_id=1, source_target_pairs={{0,4},{4,8},{8,12},{12,16},{16,20},{20,24},{24,28},{1,5},{5,9},{9,... | collective-permute-start | bytes 786440 | tf_op jit(solution)/shard_map/ppermute | solution.py:22
  178.7 128.0 %copy-start.49 = (f32[8,8]{1,0:T(8,128)}, f32[8,8]{1,0:T(8,128)S(1)}, u32[]{:S(2)}) copy-start(f32[8,8]{1,0:T(8,128)S(1)} %reshape.916) | copy-start | bytes 772
  178.7 270.4 %copy-start.46 = (f32[2880]{0:T(1024)}, f32[2880]{0:T(1024)S(1)}, u32[]{:S(2)}) copy-start(f32[2880]{0:T(1024)S(1)} %convert_element_type.352) | copy-start | bytes 34564
  179.1 124.0 %copy-start.27 = (bf16[1,256,1,512]{1,3,2,0:T(8,128)(2,1)}, bf16[1,256,1,512]{1,3,2,0:T(8,128)(2,1)S(1)}, u32[]{:S(2)}) copy-start(bf16[1,256,1,512]{1,3,2,0:T(8,128)(2,1)S(1)} %copy.101) | copy-start | bytes 786436
  179.2 128.5 %copy-start.36 = (bf16[1,256,1,512]{1,3,2,0:T(8,128)(2,1)}, bf16[1,256,1,512]{1,3,2,0:T(8,128)(2,1)S(1)}, u32[]{:S(2)}) copy-start(bf16[1,256,1,512]{1,3,2,0:T(8,128)(2,1)S(1)} %copy.100) | copy-start | bytes 786436
  309.5 139.5 %copy-start.33 = (bf16[8,64,8,128]{3,1,2,0:T(8,128)(2,1)}, bf16[8,64,8,128]{3,1,2,0:T(8,128)(2,1)S(1)}, u32[]{:S(2)}) copy-start(bf16[8,64,8,128]{3,1,2,0:T(8,128)(2,1)S(1)} %fusion.49) | copy-start | bytes 3145732
  472.6 333.1 %all-to-all-start = ((bf16[32,80,2880]{2,1,0:T(8,128)(2,1)}), bf16[32,80,2880]{2,1,0:T(8,128)(2,1)}, u32[]{:S(2)}, u32[]{:S(2)}) async-start(bf16[32,80,2880]{2,1,0:T(8,128)(2,1)} %bitcast.262), calls=%async_computation | async-start | bytes 30146560 | tf_op jit(solution)/shard_map/all_to_all | solution.py:87
  875.5 184.0 %copy-start.14 = (bf16[1,128,2880]{1,2,0:T(8,128)(2,1)S(1)}, bf16[1,128,2880]{1,2,0:T(8,128)(2,1)}, u32[]{:S(2)}) copy-start(bf16[1,128,2880]{1,2,0:T(8,128)(2,1)} %param.41) | copy-start | bytes 2211844
  875.5 187.3 %copy-start.69 = (bf16[8]{0:T(256)(128)(2,1)S(1)}, bf16[8]{0:T(256)(128)(2,1)}, u32[]{:S(2)}) copy-start(bf16[8]{0:T(256)(128)(2,1)} %get-tuple-element.41) | copy-start | bytes 52
  875.5 187.3 %copy-start.62 = (bf16[720,8]{0,1:T(8,128)(2,1)S(1)}, bf16[720,8]{0,1:T(8,128)(2,1)}, u32[]{:S(2)}) copy-start(bf16[720,8]{0,1:T(8,128)(2,1)} %param.33) | copy-start | bytes 34564
  875.5 668.5 %all-to-all-start.1 = ((f32[32,80,2880]{2,1,0:T(8,128)}), f32[32,80,2880]{2,1,0:T(8,128)}, u32[]{:S(2)}, u32[]{:S(2)}) async-start(f32[32,80,2880]{2,1,0:T(8,128)} %fusion.16), calls=%async_computation.1 | async-start | bytes 60293120 | tf_op jit(solution)/shard_map/all_to_all | solution.py:91
  1088.2 469.9 %copy-start.58 = (s32[1024]{0:T(1024)}, s32[1024]{0:T(1024)S(1)}, u32[]{:S(2)}) copy-start(s32[1024]{0:T(1024)S(1)} %pad_clamp_fusion) | copy-start | bytes 12292
  1584.7 360.8 %slice-start.6 = ((s8[4239360]{0:T(1024)(128)(4,1)}), s8[4194304]{0:T(1024)(128)(4,1)S(1)}, s32[]{:S(2)}) async-start(s8[4239360]{0:T(1024)(128)(4,1)} %bitcast.314), calls=%async_computation.23 | async-start | bytes 8388608
  1588.8 356.7 %slice-start.7 = ((s8[4239360]{0:T(1024)(128)(4,1)}), s8[45056]{0:T(1024)(128)(4,1)S(1)}, s32[]{:S(2)}) async-start(s8[4239360]{0:T(1024)(128)(4,1)} %bitcast.314), calls=%async_computation.24 | async-start | bytes 90112
  2051.2 658.7 %all-to-all-start.3 = ((f32[32,80,2880]{2,1,0:T(8,128)}), f32[32,80,2880]{2,1,0:T(8,128)}, u32[]{:S(2)}, u32[]{:S(2)}) async-start(f32[32,80,2880]{2,1,0:T(8,128)} %bitcast.261), calls=%async_computation.3 | async-start | bytes 60293120 | tf_op jit(solution)/shard_map/all_to_all | solution.py:91
  2055.7 880.8 %all-reduce.16.cloned.1.call-start = ((), (), s32[]{:S(2)}) async-start(), calls=%async_computation.16 | async-start | bytes 376832 | tf_op jit(solution)/shard_map/psum | solution.py:503
  2066.8 657.1 %copy-start.59 = (s32[1024]{0:T(1024)S(1)}, s32[1024]{0:T(1024)}, u32[]{:S(2)}) copy-start(s32[1024]{0:T(1024)} %copy-done.58) | copy-start | bytes 12292
  2780.7 18.1 collective-permute-start.1
  2786.1 298.9 %reduce-scatter.7.cloned.1.call-start = ((), (), s32[]{:S(2)}) async-start(), calls=%async_computation.13 | async-start | bytes 6217728 | tf_op jit(solution)/shard_map/reduce_scatter | solution.py:489
  2806.6 422.0 %reduce-scatter.9.cloned.1.call-start = ((), (), s32[]{:S(2)}) async-start(), calls=%async_computation.14 | async-start | bytes 6217728 | tf_op jit(solution)/shard_map/reduce_scatter | solution.py:491
  2811.2 827.6 %reduce-scatter.5.cloned.1.call-start = ((), (), s32[]{:S(2)}) async-start(), calls=%async_computation.12 | async-start | bytes 48660480 | tf_op jit(solution)/shard_map/reduce_scatter | solution.py:487
  2834.4 1218.6 %reduce-scatter.11.cloned.1.call-start = ((), (), s32[]{:S(2)}) async-start(), calls=%async_computation.15 | async-start | bytes 48660480 | tf_op jit(solution)/shard_map/reduce_scatter | solution.py:493
  2854.3 85.0 %copy-start.66 = (f32[720]{0:T(1024)S(1)}, f32[720]{0:T(1024)}, u32[]{:S(2)}) copy-start(f32[720]{0:T(1024)} %get-tuple-element.44) | copy-start | bytes 8644
  3019.2 1033.8 %copy-start.1 = (s32[4,3]{1,0:T(4,128)S(1)}, s32[4,3]{1,0:T(4,128)}, u32[]{:S(2)}) copy-start(s32[4,3]{1,0:T(4,128)} %param.40) | copy-start | bytes 148
  (62 other events, 794.2 us)
Sparse Core Ops, SparseCore 0:
  10.9 62.1 all-gather.7
  76.0 57.4 all-gather.9
  135.0 152.3 all-gather.11
  288.8 148.7 all-gather.13
  2786.3 150.1 all-reduce.15
  2939.2 145.7 reduce-scatter.6
  3087.9 140.6 reduce-scatter.8
  3235.6 403.1 reduce-scatter.4
  3646.9 406.0 reduce-scatter.10
where the time goes:
time: 4070 us; the launch traced here: 4060 us
  waiting for transfers between devices  2790 us (69%)
  blocking collectives  675 us (17%)
  matrix products  331 us (8%)
  local copies, waits for them, and re-layouts  134 us (3%)
  other arithmetic  84.5 us (2%)
    all_to_all x2, waiting for transfers between devices, from_experts(): lax.all_to_all(partials, ('seq', 'fsdp'), split_axis=0, concat_axis=0, ti...  1100 us
    reduce_scatter x1, waiting for transfers between devices, per_device(): lax.psum_scatter(out_w_grad, ('seq', 'fsdp'), scatter_dimension=0, tiled=...  414 us
    reduce_scatter x1, waiting for transfers between devices, per_device(): lax.psum_scatter(query_w_grad, ('seq', 'fsdp'), scatter_dimension=1, tile...  410 us
    all_to_all x1, blocking collectives, to_experts(): lax.all_to_all(buffer, ('seq', 'fsdp'), split_axis=0, concat_axis=0, tile...  357 us
    all_to_all x1, waiting for transfers between devices, to_experts(): lax.all_to_all(buffer, ('seq', 'fsdp'), split_axis=0, concat_axis=0, tile...  329 us
    all_gather x1, blocking collectives, per_device(): lax.all_gather(expert_down_bias, 'fsdp', axis=1, tiled=True)  169 us
    reduce_scatter x1, waiting for transfers between devices, per_device(): lax.psum_scatter(value_w_grad, ('seq', 'fsdp'), scatter_dimension=1, tile...  144 us
    all_gather x1, waiting for transfers between devices, token_columns(): lax.all_gather(output_matrix, ('seq', 'fsdp'), axis=0, tiled=True)  128 us
  transfers between devices with their start and end apart: 14, of which 12 were waited for; matrix products, arithmetic and copies ran while one was open for 5% of the time, Pallas kernels for 0%

commit v1 on v0

v1 whole, which is shorter than its diff:
```python
import jax
import jax.numpy as jnp
from jax import lax
from jax.sharding import PartitionSpec as P

QUERY_HEADS = 64
KEY_VALUE_HEADS = 8
HEAD_DIM = 64
WINDOW_LENGTH = 128


ROPE_BASE = 150000.0
NORM_EPS = 1e-05
GLU_ALPHA = 1.702
GLU_LIMIT = 7.0
EXACT = lax.Precision.HIGHEST
BF = jnp.bfloat16
F32 = jnp.float32


def rms_scale(values):
    return lax.rsqrt(jnp.mean(values * values, axis=-1, keepdims=True) + NORM_EPS)


def rope_tables(positions):
    frequency = ROPE_BASE ** (-jnp.arange(HEAD_DIM // 2, dtype=jnp.float32) * 2.0 / HEAD_DIM)
    angles = positions.astype(jnp.float32)[:, None] * frequency[None, :]
    return (jnp.cos(angles), jnp.sin(angles))


def apply_rotary(values, cosine_values, sine_values, direction):
    half_size = HEAD_DIM // 2
    rows, width = values.shape
    grid = values.reshape(rows, width // HEAD_DIM, HEAD_DIM)
    first_half = grid[..., :half_size]
    second = grid[..., half_size:]
    cosine_b = cosine_values[:, None, :]
    sine_b = direction * sine_values[:, None, :]
    turned = jnp.concatenate(
        [first_half * cosine_b - second * sine_b, second * cosine_b + first_half * sine_b], axis=-1
    )
    return turned.reshape(rows, width)


def swiglu(gate_pre, up_pre):
    gate_soft = GLU_LIMIT - jax.nn.softplus(GLU_LIMIT - gate_pre)
    up_soft = GLU_LIMIT * jnp.tanh(up_pre / GLU_LIMIT)
    return (up_soft + 1.0) * gate_soft * jax.nn.sigmoid(GLU_ALPHA * gate_soft)


def dot(left, right, left_dim, right_dim, precision=None):
    return lax.dot_general(
        left,
        right,
        (((left_dim,), (right_dim,)), ((), ())),
        precision=precision,
        preferred_element_type=jnp.float32,
    )


def gather_seq(block):
    return lax.all_gather(block, "seq", axis=0, tiled=True)


def scatter_seq(partial_rows):
    return lax.psum_scatter(partial_rows, "seq", scatter_dimension=0, tiled=True)


def gather_fsdp(block):
    return lax.all_gather(block, "fsdp", axis=0, tiled=True)


def scatter_fsdp(partial_rows):
    return lax.psum_scatter(partial_rows, "fsdp", scatter_dimension=0, tiled=True)


def split_low(values):
    high = values.astype(BF)
    low = (values - high.astype(F32)).astype(BF)
    return high, low


def with_previous(blocks):
    before = jnp.concatenate([jnp.zeros_like(blocks[:1]), blocks[:-1]], axis=0)
    return jnp.concatenate([before, blocks], axis=1)


def masked_scores(query_grid, key_all, allowed):
    scores = (
        jnp.einsum("nqhgd,nkhd->nhgqk", query_grid, key_all, preferred_element_type=F32) * 0.125
    )
    return jnp.where(allowed[:, None, None], scores, -1e30)


def window_mask(doc_row, block_count, block_rows):
    doc_ends = jnp.cumsum(doc_row)
    starts = jnp.arange(block_count, dtype=jnp.int32)[:, None] * block_rows
    positions = starts + jnp.arange(block_rows, dtype=jnp.int32)[None, :]
    key_pos = starts - block_rows + jnp.arange(2 * block_rows, dtype=jnp.int32)[None, :]
    query_doc = jnp.sum((positions[:, :, None] >= doc_ends).astype(jnp.int32), axis=2)
    key_doc = jnp.sum((key_pos[:, :, None] >= doc_ends).astype(jnp.int32), axis=2)
    offset = positions[:, :, None] - key_pos[:, None, :]
    inside = (key_pos[:, None, :] >= 0) & (offset >= 0) & (offset <= WINDOW_LENGTH)
    return inside & (query_doc[:, :, None] == key_doc[:, None, :])


def per_device(
    layer_input,
    attn_gain,
    query_matrix,
    query_bias_vector,
    key_matrix,
    key_bias_vector,
    value_matrix,
    value_bias_vector,
    sink_logit_values,
    output_matrix,
    output_bias_vector,
    ffn_gain,
    router_weight,
    router_bias,
    expert_gate_up,
    expert_gate_up_bias,
    expert_down,
    expert_down_bias,
    route_ids,
    doc_lengths,
    out_cotangent,
):
    seq_count = lax.axis_size("seq")
    fsdp_count = lax.axis_size("fsdp")
    seq_index = lax.axis_index("seq")
    fsdp_index = lax.axis_index("fsdp")
    tokens_here, width = layer_input.shape[1:]
    choose_count = route_ids.shape[2]
    expert_count = seq_count
    block_rows = WINDOW_LENGTH
    length = seq_count * tokens_here
    block_count = length // block_rows
    capacity = max(2, tokens_here * choose_count * 5 // (4 * expert_count)) * seq_count
    padded = -(-(width + 2 * expert_count) // 128) * 128
    heads_here = QUERY_HEADS // seq_count
    kv_here = max(1, KEY_VALUE_HEADS // seq_count)
    group = heads_here // kv_here
    shared_kv = seq_count > KEY_VALUE_HEADS
    q_width, kv_width = heads_here * HEAD_DIM, kv_here * HEAD_DIM

    rows_x = gather_seq(layer_input[0])
    member_here = jnp.any(
        route_ids[0][:, :, None] == jnp.arange(expert_count, dtype=jnp.int32), axis=1
    )
    cot_here = out_cotangent[0]
    cot_packed = jnp.concatenate(
        [
            cot_here,
            member_here.astype(BF),
            jnp.zeros((tokens_here, padded - width - expert_count), BF),
        ],
        axis=1,
    )
    cot_rows = gather_seq(cot_packed)

    part = attn_gain.shape[0]
    q_part, kv_part = query_bias_vector.shape[0], key_bias_vector.shape[0]
    tiny = jnp.concatenate(
        [sink_logit_values, router_bias, query_bias_vector, key_bias_vector, value_bias_vector]
    )
    tiny = jnp.concatenate([tiny, jnp.zeros((part - tiny.shape[0],), BF)])
    small = jnp.concatenate(
        [
            attn_gain[None],
            ffn_gain[None],
            output_bias_vector[None],
            tiny[None],
            expert_down_bias,
            router_weight.T,
        ],
        axis=0,
    )
    small_all = lax.all_gather(small, "fsdp", axis=0)
    wide = jnp.swapaxes(small_all, 0, 1).reshape(small.shape[0], width).astype(F32)
    attn_gain_f, ffn_gain_f, out_bias_f = wide[0], wide[1], wide[2]
    down_bias_f = wide[4 : 4 + expert_count]
    router_t = wide[4 + expert_count :].astype(BF)
    tiny_all = small_all[:, 3]
    places = [0]
    for piece in (sink_logit_values, router_bias, query_bias_vector, key_bias_vector, value_bias_vector):
        places.append(places[-1] + piece.shape[0])
    sinks_f, router_bias_f, q_bias, k_bias, v_bias = (
        tiny_all[:, a:b].reshape(-1).astype(F32) for a, b in zip(places[:-1], places[1:])
    )
    wq = lax.all_gather(query_matrix, "fsdp", axis=1, tiled=True)
    wo = lax.all_gather(output_matrix, "fsdp", axis=0, tiled=True)
    if shared_kv:
        share = seq_count // KEY_VALUE_HEADS
        kv_head = seq_index // share

        def own_head(piece, axis):
            whole = lax.all_gather(piece, ("seq", "fsdp"), axis=axis, tiled=True)
            return lax.dynamic_slice_in_dim(whole, kv_head * HEAD_DIM, HEAD_DIM, axis)

        wk, wv = own_head(key_matrix, 1), own_head(value_matrix, 1)
        k_bias = own_head(key_bias_vector, 0).astype(F32)
        v_bias = own_head(value_bias_vector, 0).astype(F32)
    else:
        wkv = lax.all_gather(jnp.stack([key_matrix, value_matrix]), "fsdp", axis=2, tiled=True)
        wk, wv = wkv[0], wkv[1]
    sinks_here = lax.dynamic_slice_in_dim(sinks_f, seq_index * heads_here, heads_here, 0)
    sink_grid = sinks_here.reshape(kv_here, group)

    rows_f = rows_x.astype(F32)
    unit_rows = rows_f * rms_scale(rows_f)
    normed_rows = (unit_rows * attn_gain_f).astype(BF)
    cosine_values, sine_values = rope_tables(jnp.arange(length, dtype=jnp.int32))
    query = apply_rotary(
        dot(normed_rows, wq, 1, 0) + q_bias, cosine_values, sine_values, 1.0
    ).astype(BF)
    keys = apply_rotary(
        dot(normed_rows, wk, 1, 0) + k_bias, cosine_values, sine_values, 1.0
    ).astype(BF)
    values = (dot(normed_rows, wv, 1, 0) + v_bias).astype(BF)
    doc_row = lax.dynamic_slice_in_dim(doc_lengths, fsdp_index, 1, 0)[0]
    allowed = window_mask(doc_row, block_count, block_rows)
    query_grid = query.reshape(block_count, block_rows, kv_here, group, HEAD_DIM)
    key_all = with_previous(keys.reshape(block_count, block_rows, kv_here, HEAD_DIM))
    value_all = with_previous(values.reshape(block_count, block_rows, kv_here, HEAD_DIM))
    scores = masked_scores(query_grid, key_all, allowed)
    sink_col = sink_grid[None, :, :, None]
    top_score = jnp.maximum(jnp.max(scores, axis=-1), sink_col)
    exp_scores = jnp.exp(scores - top_score[..., None])
    denominator = jnp.sum(exp_scores, axis=-1) + jnp.exp(sink_col - top_score)
    log_total = top_score + jnp.log(denominator)
    probabilities = exp_scores / denominator[..., None]
    heads = jnp.einsum(
        "nhgqk,nkhd->nqhgd", probabilities.astype(BF), value_all, preferred_element_type=F32
    )
    heads = heads.reshape(length, q_width).astype(BF)
    attn_sum = scatter_seq(dot(heads, wo, 1, 0).astype(BF))

    resid_in = layer_input[0].astype(F32)
    resid_mid = resid_in + attn_sum.astype(F32) + out_bias_f
    norm_two = rms_scale(resid_mid)
    unit_mid = resid_mid * norm_two
    normed_mid = (unit_mid * ffn_gain_f).astype(BF)
    logits = dot(normed_mid, router_t, 1, 1) + router_bias_f
    gates = jax.nn.softmax(jnp.where(member_here, logits, -1e30), axis=-1)
    gates = jnp.where(member_here, gates, 0.0)
    gate_high, gate_low = split_low(gates)
    mid_packed = jnp.concatenate(
        [
            normed_mid,
            gate_high,
            gate_low,
            jnp.zeros((tokens_here, padded - width - 2 * expert_count), BF),
        ],
        axis=1,
    )
    mid_rows = gather_seq(mid_packed)

    expert_lane = (jnp.arange(expert_count, dtype=jnp.int32) == seq_index).astype(F32)
    member_row = dot(cot_rows[:, width : width + expert_count].astype(F32), expert_lane[:, None], 1, 0)[:, 0] > 0.5
    slot = jnp.cumsum(member_row.astype(jnp.int32)) - 1
    select = (
        (jnp.arange(capacity, dtype=jnp.int32)[:, None] == slot[None, :]) & member_row[None, :]
    ).astype(BF)
    cot_arrived = gather_fsdp(dot(select, cot_rows, 1, 0).astype(BF))[:, :width]
    arrived = gather_fsdp(dot(select, mid_rows, 1, 0).astype(BF))
    tail = arrived[:, width:].astype(F32)
    gate_col = jnp.sum(
        (tail[:, :expert_count] + tail[:, expert_count : 2 * expert_count]) * expert_lane,
        axis=1,
        keepdims=True,
    )
    expert_rows = arrived[:, :width]
    gate_w, up_w, down_w = expert_gate_up[0, 0], expert_gate_up[0, 1], expert_down[0]
    gate_pre = dot(expert_rows, gate_w, 1, 0) + expert_gate_up_bias[0, 0].astype(F32)
    up_pre = dot(expert_rows, up_w, 1, 0) + expert_gate_up_bias[0, 1].astype(F32)
    hidden_f, glu_back = jax.vjp(swiglu, gate_pre, up_pre)
    hidden = hidden_f.astype(BF).astype(F32)
    hidden_gated = (hidden * gate_col).astype(BF)
    mix_part = dot(hidden_gated, down_w, 1, 0).astype(BF)
    grad_hidden = dot(cot_arrived, down_w, 1, 1)
    gate_grad_part = jnp.sum(hidden * grad_hidden, axis=1)
    grad_gate_pre, grad_up_pre = glu_back(grad_hidden * gate_col)
    grad_gate_low = grad_gate_pre.astype(BF)
    grad_up_low = grad_up_pre.astype(BF)
    row_part = (dot(grad_gate_low, gate_w, 1, 1) + dot(grad_up_low, up_w, 1, 1)).astype(BF)
    down_grad = dot(hidden_gated, cot_arrived, 0, 0)
    gate_up_grad = jnp.stack(
        [dot(expert_rows, grad_gate_low, 0, 0), dot(expert_rows, grad_up_low, 0, 0)]
    )
    gate_up_bias_grad = jnp.stack(
        [jnp.sum(grad_gate_low.astype(F32), axis=0), jnp.sum(grad_up_low.astype(F32), axis=0)]
    )

    row_sum = scatter_fsdp(row_part)
    gate_grad = scatter_fsdp(gate_grad_part)
    grad_high, grad_low = split_low(gate_grad[:, None] * expert_lane)
    back_packed = jnp.concatenate(
        [
            row_sum,
            grad_high,
            grad_low,
            jnp.zeros((capacity, padded - width - 2 * expert_count), BF),
        ],
        axis=1,
    )
    back = scatter_seq(dot(select, back_packed, 0, 0).astype(BF))
    mix_sum = scatter_fsdp(mix_part)
    mixture = scatter_seq(dot(select, mix_sum, 0, 0).astype(BF)).astype(F32)
    mixture = mixture + dot(gates, down_bias_f, 1, 0, EXACT)
    layer_output = (resid_mid + mixture).astype(BF)[None]

    back_tail = back[:, width:].astype(F32)
    cot_f = cot_here.astype(F32)
    grad_gates = (
        back_tail[:, :expert_count]
        + back_tail[:, expert_count : 2 * expert_count]
        + dot(cot_f, down_bias_f, 1, 1, EXACT)
    )
    mean_gate = jnp.sum(gates * grad_gates, axis=-1, keepdims=True)
    grad_logits = gates * (grad_gates - mean_gate)
    router_grad_t = dot(grad_logits, normed_mid.astype(F32), 0, 0, EXACT)
    router_bias_grad = jnp.sum(grad_logits, axis=0)
    down_bias_grad = dot(gates, cot_f, 0, 0, EXACT)
    grad_normed_mid = back[:, :width].astype(F32) + dot(grad_logits, router_t.astype(F32), 1, 0, EXACT)
    ffn_gain_grad = jnp.sum(grad_normed_mid * unit_mid, axis=0)
    grad_unit_mid = grad_normed_mid * ffn_gain_f
    grad_mid = (
        norm_two
        * (grad_unit_mid - unit_mid * jnp.mean(grad_unit_mid * unit_mid, axis=-1, keepdims=True))
        + cot_f
    )
    grad_attn = grad_mid.astype(BF)
    out_bias_grad = jnp.sum(grad_attn.astype(F32), axis=0)

    attn_rows = gather_seq(grad_attn)
    out_w_part = dot(heads, attn_rows, 0, 0)
    grad_heads = dot(attn_rows, wo, 1, 1).astype(BF)
    grad_heads_grid = grad_heads.reshape(query_grid.shape)
    probs_again = jnp.exp(masked_scores(query_grid, key_all, allowed) - log_total[..., None])
    sink_prob = jnp.exp(sink_col - log_total)
    grad_probs = jnp.einsum(
        "nqhgd,nkhd->nhgqk", grad_heads_grid, value_all, preferred_element_type=F32
    )
    row_delta = jnp.sum(probs_again * grad_probs, axis=-1)
    grad_scores = (probs_again * (grad_probs - row_delta[..., None])).astype(BF)
    sink_here_grad = -jnp.sum(sink_prob * row_delta, axis=(0, 3)).reshape(heads_here)
    grad_query = (
        jnp.einsum("nhgqk,nkhd->nqhgd", grad_scores, key_all, preferred_element_type=F32) * 0.125
    ).reshape(length, q_width)

    def to_owner(grad_all):
        own = grad_all[:, block_rows:]
        later = grad_all[1:, :block_rows]
        later = jnp.concatenate([later, jnp.zeros_like(own[:1])], axis=0)
        return (own + later).reshape(length, kv_width)

    grad_key = to_owner(
        jnp.einsum("nhgqk,nqhgd->nkhd", grad_scores, query_grid, preferred_element_type=F32) * 0.125
    )
    grad_value = to_owner(
        jnp.einsum(
            "nhgqk,nqhgd->nkhd",
            probs_again.astype(BF),
            grad_heads_grid,
            preferred_element_type=F32,
        )
    )
    grad_query_lin = apply_rotary(grad_query, cosine_values, sine_values, -1.0).astype(BF)
    grad_key_lin = apply_rotary(grad_key, cosine_values, sine_values, -1.0).astype(BF)
    grad_value_lin = grad_value.astype(BF)
    normed_part = (
        dot(grad_query_lin, wq, 1, 1) + dot(grad_key_lin, wk, 1, 1) + dot(grad_value_lin, wv, 1, 1)
    )
    grad_normed_in = scatter_seq(normed_part.astype(BF)).astype(F32)
    query_w_part = dot(grad_query_lin, normed_rows, 0, 0)
    key_w_part = dot(grad_key_lin, normed_rows, 0, 0)
    value_w_part = dot(grad_value_lin, normed_rows, 0, 0)
    query_b_part = jnp.sum(grad_query_lin.astype(F32), axis=0)
    key_b_part = jnp.sum(grad_key_lin.astype(F32), axis=0)
    value_b_part = jnp.sum(grad_value_lin.astype(F32), axis=0)
    attn_gain_grad = jnp.sum(normed_part * unit_rows, axis=0)

    resid_scale = rms_scale(resid_in)
    unit_in = resid_in * resid_scale
    grad_unit_in = grad_normed_in * attn_gain_f
    input_grad = (
        resid_scale
        * (grad_unit_in - unit_in * jnp.mean(grad_unit_in * unit_in, axis=-1, keepdims=True))
        + grad_mid
    )

    query_w_own = scatter_fsdp(query_w_part).T
    out_w_own = scatter_fsdp(out_w_part)
    query_b_own = scatter_fsdp(query_b_part)
    if shared_kv:

        def whole_sum(part_grad, head_axis_rows):
            whole = jnp.zeros((KEY_VALUE_HEADS * HEAD_DIM,) + part_grad.shape[1:], F32)
            whole = lax.dynamic_update_slice_in_dim(whole, part_grad, kv_head * HEAD_DIM, 0)
            return lax.psum_scatter(whole, ("seq", "fsdp"), scatter_dimension=0, tiled=True)

        key_w_own = whole_sum(key_w_part, True).T
        value_w_own = whole_sum(value_w_part, True).T
        key_b_own, value_b_own = whole_sum(key_b_part, False), whole_sum(value_b_part, False)
    else:
        key_w_own = scatter_fsdp(key_w_part).T
        value_w_own = scatter_fsdp(value_w_part).T
        key_b_own, value_b_own = scatter_fsdp(key_b_part), scatter_fsdp(value_b_part)

    sink_all_grad = lax.dynamic_update_slice_in_dim(
        jnp.zeros((QUERY_HEADS,), F32), sink_here_grad, seq_index * heads_here, 0
    )
    tiny_grad = jnp.concatenate([sink_all_grad, router_bias_grad])
    tiny_grad = jnp.concatenate([tiny_grad, jnp.zeros((width - tiny_grad.shape[0],), F32)])
    small_grad = jnp.concatenate(
        [
            attn_gain_grad[None],
            out_bias_grad[None],
            ffn_gain_grad[None],
            tiny_grad[None],
            down_bias_grad,
            router_grad_t,
        ],
        axis=0,
    )
    small_sum = lax.psum(small_grad, ("seq", "fsdp"))

    def own_part(whole_array, axis_number):
        piece_size = whole_array.shape[axis_number] // fsdp_count
        return lax.dynamic_slice_in_dim(
            whole_array, fsdp_index * piece_size, piece_size, axis_number
        )

    small_own = own_part(small_sum, 1)
    return (
        layer_output,
        input_grad[None],
        small_own[0],
        query_w_own,
        query_b_own,
        key_w_own,
        key_b_own,
        value_w_own,
        value_b_own,
        own_part(small_sum[3, :QUERY_HEADS], 0),
        out_w_own,
        small_own[1],
        small_own[2],
        small_own[4 + expert_count :].T,
        own_part(small_sum[3, QUERY_HEADS : QUERY_HEADS + expert_count], 0),
        gate_up_grad[None],
        gate_up_bias_grad[None],
        down_grad[None],
        small_own[4 : 4 + expert_count],
    )


def solution(mesh):
    return jax.shard_map(
        per_device,
        mesh=mesh,
        in_specs=(
            P("fsdp", "seq", None),
            P("fsdp"),
            P(None, ("seq", "fsdp")),
            P(("seq", "fsdp")),
            P(None, ("seq", "fsdp")),
            P(("seq", "fsdp")),
            P(None, ("seq", "fsdp")),
            P(("seq", "fsdp")),
            P("fsdp"),
            P(("seq", "fsdp"), None),
            P("fsdp"),
            P("fsdp"),
            P("fsdp", None),
            P("fsdp"),
            P("seq", None, None, "fsdp"),
            P("seq", None, "fsdp"),
            P("seq", "fsdp", None),
            P(None, "fsdp"),
            P("fsdp", "seq", None),
            P(),
            P("fsdp", "seq", None),
        ),
        out_specs=(
            P("fsdp", "seq", None),
            P("fsdp", "seq", None),
            P("fsdp"),
            P(None, ("seq", "fsdp")),
            P(("seq", "fsdp")),
            P(None, ("seq", "fsdp")),
            P(("seq", "fsdp")),
            P(None, ("seq", "fsdp")),
            P(("seq", "fsdp")),
            P("fsdp"),
            P(("seq", "fsdp"), None),
            P("fsdp"),
            P("fsdp"),
            P("fsdp", None),
            P("fsdp"),
            P("seq", None, None, "fsdp"),
            P("seq", None, "fsdp"),
            P("seq", "fsdp", None),
            P(None, "fsdp"),
        ),
        check_vma=False,
    )
```

time: 4070 us -> 1820 us (0.45)
  waiting for transfers between devices: 2790 us -> 1250 us
  blocking collectives: 675 us -> 32 us
    all_to_all x3 -> x0, waiting for transfers between devices: 1430 us -> none  [the longest x2 1100 us: from_experts(): lax.all_to_all(partials, ('seq', 'fsdp'), split_axis=0, concat_axis=0, ti...]
    reduce_scatter x4, waiting for transfers between devices: 979 us -> 164 us  [scatter_fsdp(): lax.psum_scatter(partial_rows, 'fsdp', scatter_dimension=0, tiled=True)]
    unnamed x9 -> x25, waiting for transfers between devices: 2.66 us -> 514 us
    all_to_all x1 -> x0, blocking collectives: 357 us -> none  [to_experts(): lax.all_to_all(buffer, ('seq', 'fsdp'), split_axis=0, concat_axis=0, tile...]
    all_gather x4 -> x8, waiting for transfers between devices: 286 us -> 512 us  [the longest x4 328 us: gather_seq(): return lax.all_gather(block, 'seq', axis=0, tiled=True)]
    all_gather x3 -> x2, blocking collectives: 221 us -> 15.4 us  [the longest x1 8.77 us: per_device(): lax.all_gather(jnp.stack([key_matrix, value_matrix]), 'fsdp', axis=2, til...]
    unnamed x181 -> x196, local copies, waits for them, and re-layouts: 15.6 us -> 90.4 us
    psum x1 -> x0, blocking collectives: 43.8 us -> none  [per_device(): lax.psum((attn_gain_grad, ffn_gain_grad, out_bias_grad, sink_mine_grad, r...]
  transfers between devices with their start and end apart: 14 -> 19, of which waited for: 12 -> 18; matrix products, arithmetic and copies ran while one was open for 5% -> 19% of each run, Pallas kernels for 0% -> 0%
where the time goes in v1:
time: 1820 us; the launch traced here: 1800 us
  waiting for transfers between devices  1250 us (69%)
  matrix products  333 us (18%)
  local copies, waits for them, and re-layouts  123 us (7%)
  other arithmetic  45 us (2%)
  blocking collectives  32 us (2%)
    unnamed x25, waiting for transfers between devices  514 us
    all_gather x4, waiting for transfers between devices, gather_seq(): return lax.all_gather(block, 'seq', axis=0, tiled=True)  328 us
    dot_general x32, matrix products, dot(): lax.dot_general(left, right, (((left_dim,), (right_dim,)), ((), ())), pre...  313 us
    reduce_scatter x4, waiting for transfers between devices, scatter_fsdp(): lax.psum_scatter(partial_rows, 'fsdp', scatter_dimension=0, tiled=True)  164 us
    all_gather x2, waiting for transfers between devices, gather_fsdp(): return lax.all_gather(block, 'fsdp', axis=0, tiled=True)  157 us
    unnamed x196, local copies, waits for them, and re-layouts  90.4 us
    psum x1, waiting for transfers between devices, per_device(): small_sum = lax.psum(small_grad, ('seq', 'fsdp'))  63.4 us
  transfers between devices with their start and end apart: 19, of which 18 were waited for; matrix products, arithmetic and copies ran while one was open for 19% of the time, Pallas kernels for 0%

profile of v1, /device:TPU:0, one launch (start us, length us, event | category | flops | bytes accessed | tf_op | source)
XLA Modules:
  0.0 1804.9 jit_solution(17349680863579196518)
XLA Ops:
  36.7 71.3 %all-gather.26.cloned.1.call-done = bf16[1,1024,2880]{1,2,0:T(8,128)(2,1)} async-done(((bf16[1,128,2880]{1,2,0:T(8,128)(2,1)}), bf16[1,1024,2880]{1,2,0:T(8,128)(2,1)}) %all-gather.26.cloned.1.call-update) | async-done | bytes 5898256 | tf_op jit(solution)/shard_map/all_gather | solution.py:62
  122.6 13.0 all-gather.12.cloned.1.call-done
  150.7 14.2 all-gather.14.cloned.1.call-done
  184.2 110.1 %reduce-scatter.31.cloned.1.call-done = bf16[128,2880]{1,0:T(8,128)(2,1)} async-done(((bf16[1024,2880]{1,0:T(8,128)(2,1)}), bf16[128,2880]{1,0:T(8,128)(2,1)}) %reduce-scatter.31.cloned.1.call-update) | async-done | bytes 737296
  300.7 92.9 %all-gather.16.cloned.1.call-done = bf16[1024,2944]{0,1:T(8,128)(2,1)} async-done(((bf16[128,2944]{0,1:T(8,128)(2,1)}), bf16[1024,2944]{0,1:T(8,128)(2,1)}) %all-gather.16.cloned.1.call-update) | async-done | bytes 6029328 | tf_op jit(solution)/shard_map/all_gather | solution.py:62
  403.6 87.6 %all-gather.18.cloned.1.call-done = bf16[1024,2944]{0,1:T(8,128)(2,1)} async-done(((bf16[128,2944]{0,1:T(8,128)(2,1)}), bf16[1024,2944]{0,1:T(8,128)(2,1)}) %all-gather.18.cloned.1.call-update) | async-done | bytes 6029328 | tf_op jit(solution)/shard_map/all_gather | solution.py:62
  491.2 19.2 %convolution_convert_fusion.5 = bf16[640,2944]{1,0:T(8,128)(2,1)} fusion(bf16[1024,2944]{0,1:T(8,128)(2,1)} %all-gather.18.cloned.1.call-done, s32[1024]{0:T(1024)S(1)} %add_bitcast_fusion, pred[1024]{0:T(1024)(128)(4,1)S(1)} %get-tuple-element.50), kind=kOutput, calls=%fused_computation.69 | convolution fusion | flops 3861954560 | bytes 9802752 | tf_op jit(solution)/shard_map/dot_general | solution.py:52
  510.5 76.8 %all-gather.22.cloned.1.call-done = bf16[2560,2944]{1,0:T(8,128)(2,1)} async-done(((bf16[640,2944]{1,0:T(8,128)(2,1)}), bf16[2560,2944]{1,0:T(8,128)(2,1)}) %all-gather.22.cloned.1.call-update) | async-done | bytes 15073296 | tf_op jit(solution)/shard_map/all_gather | solution.py:70
  587.3 18.1 %fusion.4 = f32[2560,720]{0,1:T(8,128)} fusion(bf16[2560,2944]{1,0:T(8,128)(2,1)} %all-gather.22.cloned.1.call-done, bf16[1,720,2880]{2,1,0:T(8,128)(2,1)} %param.37), kind=kOutput, calls=%fused_computation.12 | convolution fusion | flops 10616832000 | bytes 26593280 | tf_op jit(solution)/shard_map/dot_general | solution.py:52
  605.4 80.4 %all-gather.20.cloned.1.call-done = bf16[2560,2944]{1,0:T(8,128)(2,1)} async-done(((bf16[640,2944]{1,0:T(8,128)(2,1)}), bf16[2560,2944]{1,0:T(8,128)(2,1)}) %all-gather.20.cloned.1.call-update) | async-done | bytes 15073296 | tf_op jit(solution)/shard_map/all_gather | solution.py:70
  688.1 18.1 %fusion.13 = f32[2560,720]{0,1:T(8,128)} fusion(bf16[2560,2944]{1,0:T(8,128)(2,1)} %all-gather.20.cloned.1.call-done, bf16[1,2,2880,720]{2,3,1,0:T(8,128)(2,1)} %param.35), kind=kOutput, calls=%fused_computation.23 | convolution fusion | flops 10616832000 | bytes 26685440 | tf_op jit(solution)/shard_map/dot_general | solution.py:52
  706.3 31.3 %convert_reduce_fusion = (f32[720]{0:T(1024)}, bf16[2560,720]{0,1:T(8,128)(2,1)}, f32[720]{0:T(1024)}, bf16[2560,720]{0,1:T(8,128)(2,1)}, f32[2560]{0:T(1024)S(1)}, /*index=5*/bf16[2560,720]{0,1:T(8,128)(2,1)}) fusion(f32[2560,720]{0,1:T(8,128)} %fusion.13, f32[720]{0:T(1024)S(1)} %get-tuple-element.28, f32[2560,720]{0,1:T(8,128)} %fusion.4, ...), kind=kOutput, calls=%fused_computation.50 | convolution fusion | flops 10714517504 | bytes 45153920 | tf_op jit(solution)/shard_map/dot_general | solution.py:52
  737.6 20.5 %fusion.48 = f32[2560,2880]{0,1:T(8,128)} fusion(bf16[2560,720]{0,1:T(8,128)(2,1)} %get-tuple-element.55, bf16[1,2,2880,720]{2,3,1,0:T(8,128)(2,1)} %param.35), kind=kOutput, calls=%fused_computation.72 | convolution fusion | flops 10616832000 | bytes 37416960 | tf_op jit(solution)/shard_map/dot_general | solution.py:52
  758.1 23.0 %add_convert_fusion = bf16[2560,2880]{0,1:T(8,128)(2,1)} fusion(f32[2560,2880]{0,1:T(8,128)} %fusion.48, bf16[2560,720]{0,1:T(8,128)(2,1)} %get-tuple-element.36, bf16[1,2,2880,720]{2,3,1,0:T(8,128)(2,1)} %param.35), kind=kOutput, calls=%fused_computation | convolution fusion | flops 10631577600 | bytes 52162560 | tf_op jit(solution)/shard_map/dot_general | solution.py:52
  781.1 20.2 %copy.150 = bf16[2560,2880]{1,0:T(8,128)(2,1)} copy(bf16[2560,2880]{0,1:T(8,128)(2,1)} %add_convert_fusion) | data formatting | bytes 29491200
  803.2 10.5 all-reduce.4
  813.9 103.2 %reduce-scatter.37.cloned.1.call-done = bf16[640,2880]{1,0:T(8,128)(2,1)} async-done(((bf16[2560,2880]{1,0:T(8,128)(2,1)}), bf16[640,2880]{1,0:T(8,128)(2,1)}) %reduce-scatter.37.cloned.1.call-update) | async-done | bytes 3686416
  932.9 17.8 convolution_convert_fusion
  950.7 20.4 %copy.146 = bf16[2560,2880]{1,0:T(8,128)(2,1)} copy(bf16[2560,2880]{0,1:T(8,128)(2,1)} %convolution_convert_fusion) | data formatting | bytes 29491200
  972.1 74.4 %reduce-scatter.39.cloned.1.call-done = bf16[128,2944]{1,0:T(8,128)(2,1)} async-done(((bf16[1024,2944]{1,0:T(8,128)(2,1)}), bf16[128,2944]{1,0:T(8,128)(2,1)}) %reduce-scatter.39.cloned.1.call-update) | async-done | bytes 753680
  1053.7 111.3 %reduce-scatter.33.cloned.1.call-done = bf16[640,2880]{1,0:T(8,128)(2,1)} async-done(((bf16[2560,2880]{1,0:T(8,128)(2,1)}), bf16[640,2880]{1,0:T(8,128)(2,1)}) %reduce-scatter.33.cloned.1.call-update) | async-done | bytes 3686416
  1186.8 75.9 %all-gather.24.cloned.1.call-done = bf16[1024,2880]{0,1:T(8,128)(2,1)} async-done(((bf16[128,2880]{0,1:T(8,128)(2,1)}), bf16[1024,2880]{0,1:T(8,128)(2,1)}) %all-gather.24.cloned.1.call-update) | async-done | bytes 5898256 | tf_op jit(solution)/shard_map/all_gather | solution.py:62
  1320.1 14.1 fusion.7
  1377.7 15.8 fusion.37
  1394.2 15.8 fusion.40
  1416.3 18.3 %fusion.43 = f32[1,720,2880]{2,1,0:T(8,128)} fusion(bf16[2560,2944]{1,0:T(8,128)(2,1)} %all-gather.22.cloned.1.call-done, bf16[2560,720]{0,1:T(8,128)(2,1)} %get-tuple-element.57, f32[2560]{0:T(1024)S(1)} %copy-done.62), kind=kOutput, calls=%fused_computation.67 | convolution fusion | flops 10622361600 | bytes 27064320 | tf_op jit(solution)/shard_map/dot_general | solution.py:52
  1446.5 63.4 %all-reduce.11.cloned.1.call-done = f32[20,2880]{1,0:T(8,128)} async-done(((f32[20,2880]{1,0:T(8,128)}), f32[20,2880]{1,0:T(8,128)}) %all-reduce.11.cloned.1.call-update) | async-done | bytes 230416 | tf_op jit(solution)/shard_map/psum | solution.py:428
  1515.6 112.4 %reduce-scatter.41.cloned.1.call-done = bf16[128,2880]{1,0:T(8,128)(2,1)} async-done(((bf16[1024,2880]{1,0:T(8,128)(2,1)}), bf16[128,2880]{1,0:T(8,128)(2,1)}) %reduce-scatter.41.cloned.1.call-update) | async-done | bytes 737296
  1634.3 19.7 %reduce-scatter.27.cloned.1.call-done = f32[16,2880]{1,0:T(8,128)} async-done(((f32[64,2880]{1,0:T(8,128)}), f32[16,2880]{1,0:T(8,128)}) %reduce-scatter.27.cloned.1.call-update) | async-done | bytes 184336 | tf_op jit(solution)/shard_map/reduce_scatter | solution.py:74
  1654.0 26.1 %reduce-scatter.25.cloned.1.call-done = f32[16,2880]{1,0:T(8,128)} async-done(((f32[64,2880]{1,0:T(8,128)}), f32[16,2880]{1,0:T(8,128)}) %reduce-scatter.25.cloned.1.call-update) | async-done | bytes 184336 | tf_op jit(solution)/shard_map/reduce_scatter | solution.py:74
  1680.1 58.9 %reduce-scatter.29.cloned.1.call-done = f32[128,2880]{0,1:T(8,128)} async-done(((f32[512,2880]{0,1:T(8,128)}), f32[128,2880]{0,1:T(8,128)}) %reduce-scatter.29.cloned.1.call-update) | async-done | bytes 1474576 | tf_op jit(solution)/shard_map/reduce_scatter | solution.py:74
  1739.0 58.9 %reduce-scatter.23.cloned.1.call-done = f32[128,2880]{0,1:T(8,128)} async-done(((f32[512,2880]{0,1:T(8,128)}), f32[128,2880]{0,1:T(8,128)}) %reduce-scatter.23.cloned.1.call-update) | async-done | bytes 1474576 | tf_op jit(solution)/shard_map/reduce_scatter | solution.py:74
  (389 shorter events, 273.5 us)
Async XLA Ops:
  7.2 100.8 %all-gather.26.cloned.1.call-start = ((), (), s32[]{:S(2)}) async-start(), calls=%async_computation.22 | async-start | bytes 6635520 | tf_op jit(solution)/shard_map/all_gather | solution.py:62
  7.9 127.6 %all-gather.12.cloned.1.call-start = ((), (), s32[]{:S(2)}) async-start(), calls=%async_computation.10 | async-start | bytes 3686400 | tf_op jit(solution)/shard_map/all_gather | solution.py:192
  8.7 156.2 %all-gather.14.cloned.1.call-start = ((), (), s32[]{:S(2)}) async-start(), calls=%async_computation.11 | async-start | bytes 3686400 | tf_op jit(solution)/shard_map/all_gather | solution.py:193
  9.4 284.8 %reduce-scatter.31.cloned.1.call-start = ((), (), s32[]{:S(2)}) async-start(), calls=%async_computation.23 | async-start | bytes 6782976
  180.5 213.1 %all-gather.16.cloned.1.call-start = ((), (), s32[]{:S(2)}) async-start(), calls=%async_computation.12 | async-start | bytes 6782976 | tf_op jit(solution)/shard_map/all_gather | solution.py:62
  182.9 308.3 %all-gather.18.cloned.1.call-start = ((), (), s32[]{:S(2)}) async-start(), calls=%async_computation.13 | async-start | bytes 6782976 | tf_op jit(solution)/shard_map/all_gather | solution.py:62
  183.0 220.4 %copy-start.59 = (bf16[2944]{0:T(1024)(128)(2,1)}, bf16[2944]{0:T(1024)(128)(2,1)S(1)}, u32[]{:S(2)}) copy-start(bf16[2944]{0:T(1024)(128)(2,1)S(1)} %pad.21.clone) | copy-start | bytes 17668
  184.0 219.5 %copy-start.52 = (bf16[8,2880]{1,0:T(8,128)(2,1)}, bf16[8,2880]{1,0:T(8,128)(2,1)S(1)}, u32[]{:S(2)}) copy-start(bf16[8,2880]{1,0:T(8,128)(2,1)S(1)} %convert_element_type.355) | copy-start | bytes 138244
  184.1 219.4 %copy-start.41 = (f32[2880]{0:T(1024)}, f32[2880]{0:T(1024)S(1)}, u32[]{:S(2)}) copy-start(f32[2880]{0:T(1024)S(1)} %add.321) | copy-start | bytes 34564
  184.2 219.3 %copy-start.49 = (f32[2880]{0:T(1024)}, f32[2880]{0:T(1024)S(1)}, u32[]{:S(2)}) copy-start(f32[2880]{0:T(1024)S(1)} %mul.534) | copy-start | bytes 34564
  300.7 286.7 %all-gather.22.cloned.1.call-start = ((), (), s32[]{:S(2)}) async-start(), calls=%async_computation.15 | async-start | bytes 18841600 | tf_op jit(solution)/shard_map/all_gather | solution.py:70
  403.5 282.3 %all-gather.20.cloned.1.call-start = ((), (), s32[]{:S(2)}) async-start(), calls=%async_computation.14 | async-start | bytes 18841600 | tf_op jit(solution)/shard_map/all_gather | solution.py:70
  510.4 406.6 %reduce-scatter.37.cloned.1.call-start = ((), (), s32[]{:S(2)}) async-start(), calls=%async_computation.26 | async-start | bytes 18841600
  688.1 244.8 %copy-start.61 = (f32[2560]{0:T(1024)}, f32[2560]{0:T(1024)S(1)}, u32[]{:S(2)}) copy-start(f32[2560]{0:T(1024)S(1)} %fusion.98) | copy-start | bytes 30724
  801.4 121.8 %copy-start.60 = (bf16[2944]{0:T(1024)(128)(2,1)S(1)}, bf16[2944]{0:T(1024)(128)(2,1)}, u32[]{:S(2)}) copy-start(bf16[2944]{0:T(1024)(128)(2,1)} %copy-done.59) | copy-start | bytes 17668
  801.4 121.8 %copy-start.74 = (s32[1024]{0:T(1024)S(1)}, s32[1024]{0:T(1024)}, u32[]{:S(2)}) copy-start(s32[1024]{0:T(1024)} %copy-done.73) | copy-start | bytes 12292
  801.4 245.0 %reduce-scatter.39.cloned.1.call-start = ((), (), s32[]{:S(2)}) async-start(), calls=%async_computation.27 | async-start | bytes 6782976
  932.8 232.2 %reduce-scatter.33.cloned.1.call-start = ((), (), s32[]{:S(2)}) async-start(), calls=%async_computation.24 | async-start | bytes 18841600
  971.2 291.5 %all-gather.24.cloned.1.call-start = ((), (), s32[]{:S(2)}) async-start(), calls=%async_computation.16 | async-start | bytes 6635520 | tf_op jit(solution)/shard_map/all_gather | solution.py:62
  1051.9 122.3 %copy-start.75 = (f32[128]{0:T(128)}, f32[128]{0:T(128)S(1)}, u32[]{:S(2)}) copy-start(f32[128]{0:T(128)S(1)} %broadcast_multiply_fusion.2) | copy-start | bytes 1540
  1053.6 381.1 %reduce-scatter.35.cloned.1.call-start = ((), (), s32[]{:S(2)}) async-start(), calls=%async_computation.25 | async-start | bytes 6782976
  1182.9 327.0 %all-reduce.11.cloned.1.call-start = ((), (), s32[]{:S(2)}) async-start(), calls=%async_computation.17 | async-start | bytes 565248 | tf_op jit(solution)/shard_map/psum | solution.py:428
  1339.1 288.9 %reduce-scatter.41.cloned.1.call-start = ((), (), s32[]{:S(2)}) async-start(), calls=%async_computation.28 | async-start | bytes 6782976
  1347.6 306.4 %reduce-scatter.27.cloned.1.call-start = ((), (), s32[]{:S(2)}) async-start(), calls=%async_computation.20 | async-start | bytes 942080 | tf_op jit(solution)/shard_map/reduce_scatter | solution.py:74
  1354.5 325.6 %reduce-scatter.25.cloned.1.call-start = ((), (), s32[]{:S(2)}) async-start(), calls=%async_computation.19 | async-start | bytes 942080 | tf_op jit(solution)/shard_map/reduce_scatter | solution.py:74
  1360.1 378.9 %reduce-scatter.29.cloned.1.call-start = ((), (), s32[]{:S(2)}) async-start(), calls=%async_computation.21 | async-start | bytes 7372800 | tf_op jit(solution)/shard_map/reduce_scatter | solution.py:74
  1368.1 429.8 %reduce-scatter.23.cloned.1.call-start = ((), (), s32[]{:S(2)}) async-start(), calls=%async_computation.18 | async-start | bytes 7372800 | tf_op jit(solution)/shard_map/reduce_scatter | solution.py:74
  1434.7 194.8 %copy-start.47 = (f32[2880]{0:T(1024)S(1)}, f32[2880]{0:T(1024)}, u32[]{:S(2)}) copy-start(f32[2880]{0:T(1024)} %copy-done.46) | copy-start | bytes 34564
  1434.7 195.3 %copy-start.51 = (f32[2880]{0:T(1024)S(1)}, f32[2880]{0:T(1024)}, u32[]{:S(2)}) copy-start(f32[2880]{0:T(1024)} %copy-done.49) | copy-start | bytes 34564
  1434.7 195.3 %copy-start.66 = (f32[128]{0:T(128)S(1)}, f32[128]{0:T(128)}, u32[]{:S(2)}) copy-start(f32[128]{0:T(128)} %copy-done.64) | copy-start | bytes 1540
  1434.7 195.3 %copy-start.76 = (f32[128]{0:T(128)S(1)}, f32[128]{0:T(128)}, u32[]{:S(2)}) copy-start(f32[128]{0:T(128)} %copy-done.75) | copy-start | bytes 1540
  1434.7 363.2 %copy-start.1 = (s32[4,3]{1,0:T(4,128)S(1)}, s32[4,3]{1,0:T(4,128)}, u32[]{:S(2)}) copy-start(s32[4,3]{1,0:T(4,128)} %param.40) | copy-start | bytes 148
  (76 other events, 2489.0 us)
Sparse Core Ops, SparseCore 0:
  10.1 97.8 all-gather.25
  109.5 25.9 all-gather.11
  137.1 27.7 all-gather.13
  180.6 113.6 reduce-scatter.30
  296.9 96.6 all-gather.15
  396.2 94.9 all-gather.17
  492.8 94.4 all-gather.21
  589.5 96.2 all-gather.19
  801.5 115.5 reduce-scatter.36
  932.9 113.4 reduce-scatter.38
  1049.6 115.3 reduce-scatter.32
  1167.5 95.1 all-gather.23
  1266.4 111.7 reduce-scatter.34
  1384.3 125.4 all-reduce.10
  1513.4 114.5 reduce-scatter.40
  1631.1 22.8 reduce-scatter.26
  1657.0 23.0 reduce-scatter.24
  1683.3 55.7 reduce-scatter.28
  1742.1 55.7 reduce-scatter.22

commit v2 on v1

--- a/solution.py
+++ b/solution.py
@@ -58,6 +58,111 @@
     )
 
 
+def tie(*arrays):
+    return lax.optimization_barrier(arrays)
+
+
+class Line:
+    def __init__(self):
+        index = lax.axis_index("seq")
+        self.place, self.side = index // 2, index % 2
+        at_low, at_high = self.place == 0, self.place == 3
+        self.at_end = at_low | at_high
+        self.at_low = at_low
+        place = self.place
+        self.order = [
+            place,
+            jnp.where(at_low, 1, place - 1),
+            jnp.where(at_low, 2, jnp.where(at_high, 1, place + 1)),
+            jnp.where(place < 2, 3, 0),
+        ]
+
+    @staticmethod
+    def along(block, moves):
+        route = [(2 * i + k, 2 * j + k) for i, j in moves for k in range(2)]
+        return lax.ppermute(block, "seq", route)
+
+    @staticmethod
+    def across(block):
+        return lax.ppermute(block, "seq", [(i, i ^ 1) for i in range(8)])
+
+    def as_pair(self, own, other):
+        first = jnp.where(self.side == 0, own, other)
+        second = jnp.where(self.side == 0, other, own)
+        return jnp.concatenate([first, second], axis=0)
+
+    def gather(self, block):
+        up, down, side_0 = (
+            self.along(block, [(0, 1), (1, 2), (2, 3)]),
+            self.along(block, [(1, 0), (2, 1), (3, 2)]),
+            self.across(block),
+        )
+        up, down, side_0 = tie(up, down, side_0)
+        near = jnp.where(self.at_low, down, up)
+        up_2, down_2, side_1 = (
+            self.along(up, [(1, 2), (2, 3)]),
+            self.along(down, [(2, 1), (1, 0)]),
+            self.across(near),
+        )
+        up_2, down_2, side_1, down = tie(up_2, down_2, side_1, down)
+        second = up_2 + down_2
+        far = jnp.where(self.at_end, second, down)
+        third, side_2 = self.along(second, [(2, 3), (1, 0)]), self.across(far)
+        third, side_2, second = tie(third, side_2, second)
+        last = jnp.where(self.at_end, third, second)
+        side_3 = self.across(last)
+        return [
+            self.as_pair(block, side_0),
+            self.as_pair(near, side_1),
+            self.as_pair(far, side_2),
+            self.as_pair(last, side_3),
+        ]
+
+    def halves(self, pair):
+        rows = pair.shape[0] // 2
+        own = lax.dynamic_slice_in_dim(pair, self.side * rows, rows, 0)
+        other = lax.dynamic_slice_in_dim(pair, (1 - self.side) * rows, rows, 0)
+        return own, other
+
+    def scatter(self, pairs):
+        own, other = zip(*(self.halves(pair) for pair in pairs))
+        side_3 = self.across(other[3])
+        sum_3 = own[3].astype(F32) + side_3.astype(F32)
+        sent, later = tie(sum_3.astype(BF), other[2])
+        step_1, side_2 = self.along(sent, [(0, 1), (3, 2)]), self.across(later)
+        step_1, side_2, later = tie(step_1, side_2, other[1])
+        sum_2 = own[2].astype(F32) + side_2.astype(F32)
+        sent = jnp.where(self.at_end, sum_2, sum_3 + step_1.astype(F32)).astype(BF)
+        up, down, side_1 = (
+            self.along(sent, [(0, 1), (1, 2)]),
+            self.along(sent, [(3, 2), (2, 1)]),
+            self.across(later),
+        )
+        up, down, side_1, later = tie(up, down, side_1, other[0])
+        sum_1 = own[1].astype(F32) + side_1.astype(F32)
+        sent_up = jnp.where(self.at_low, sum_1, sum_2 + up.astype(F32)).astype(BF)
+        sent_down = (sum_1 + down.astype(F32)).astype(BF)
+        up, down, side_0 = (
+            self.along(sent_up, [(0, 1), (1, 2), (2, 3)]),
+            self.along(sent_down, [(1, 0), (2, 1), (3, 2)]),
+            self.across(later),
+        )
+        return (
+            own[0].astype(F32) + side_0.astype(F32) + up.astype(F32) + down.astype(F32)
+        )
+
+
+class Whole:
+    def __init__(self):
+        self.order = [jnp.int32(0)]
+
+    def gather(self, block):
+        return [gather_seq(block)]
+
+    def scatter(self, pairs):
+        return scatter_seq(pairs[0]).astype(F32)
+
+
 def gather_seq(block):
     return lax.all_gather(block, "seq", axis=0, tiled=True)
 
@@ -66,12 +171,16 @@
     return lax.psum_scatter(partial_rows, "seq", scatter_dimension=0, tiled=True)
 
 
-def gather_fsdp(block):
-    return lax.all_gather(block, "fsdp", axis=0, tiled=True)
-
-
 def scatter_fsdp(partial_rows):
     return lax.psum_scatter(partial_rows, "fsdp", scatter_dimension=0, tiled=True)
+
+
+def to_core(block):
+    return lax.ppermute(block, "fsdp", [(i, i ^ 1) for i in range(4)])
+
+
+def to_chip(block):
+    return lax.ppermute(block, "fsdp", [(i, i ^ 2) for i in range(4)])
 
 
 def split_low(values):
@@ -137,7 +246,8 @@
     block_rows = WINDOW_LENGTH
     length = seq_count * tokens_here
     block_count = length // block_rows
-    capacity = max(2, tokens_here * choose_count * 5 // (4 * expert_count)) * seq_count
+    block_capacity = max(2, tokens_here * choose_count * 5 // (4 * expert_count))
+    capacity = block_capacity * seq_count
     padded = -(-(width + 2 * expert_count) // 128) * 128
     heads_here = QUERY_HEADS // seq_count
     kv_here = max(1, KEY_VALUE_HEADS // seq_count)
@@ -145,7 +255,13 @@
     shared_kv = seq_count > KEY_VALUE_HEADS
     q_width, kv_width = heads_here * HEAD_DIM, kv_here * HEAD_DIM
 
-    rows_x = gather_seq(layer_input[0])
+    line = Line() if seq_count == 8 else Whole()
+    chunk = length // len(line.order)
+    starts = [place * chunk for place in line.order]
+
+    rows_x = jnp.zeros((length, width), BF)
+    for start, pair in zip(starts, line.gather(layer_input[0])):
+        rows_x = lax.dynamic_update_slice_in_dim(rows_x, pair, start, 0)
     member_here = jnp.any(
         route_ids[0][:, :, None] == jnp.arange(expert_count, dtype=jnp.int32), axis=1
     )
@@ -235,10 +351,14 @@
         "nhgqk,nkhd->nqhgd", probabilities.astype(BF), value_all, preferred_element_type=F32
     )
     heads = heads.reshape(length, q_width).astype(BF)
-    attn_sum = scatter_seq(dot(heads, wo, 1, 0).astype(BF))
+
+    def taken(rows, start):
+        return lax.dynamic_slice_in_dim(rows, start, chunk, 0)
+
+    attn_sum = line.scatter([dot(taken(heads, start), wo, 1, 0).astype(BF) for start in starts])
 
     resid_in = layer_input[0].astype(F32)
-    resid_mid = resid_in + attn_sum.astype(F32) + out_bias_f
+    resid_mid = resid_in + attn_sum + out_bias_f
     norm_two = rms_scale(resid_mid)
     unit_mid = resid_mid * norm_two
     normed_mid = (unit_mid * ffn_gain_f).astype(BF)
@@ -255,63 +375,118 @@
         ],
         axis=1,
     )
-    mid_rows = gather_seq(mid_packed)
-
     expert_lane = (jnp.arange(expert_count, dtype=jnp.int32) == seq_index).astype(F32)
-    member_row = dot(cot_rows[:, width : width + expert_count].astype(F32), expert_lane[:, None], 1, 0)[:, 0] > 0.5
-    slot = jnp.cumsum(member_row.astype(jnp.int32)) - 1
-    select = (
-        (jnp.arange(capacity, dtype=jnp.int32)[:, None] == slot[None, :]) & member_row[None, :]
-    ).astype(BF)
-    cot_arrived = gather_fsdp(dot(select, cot_rows, 1, 0).astype(BF))[:, :width]
-    arrived = gather_fsdp(dot(select, mid_rows, 1, 0).astype(BF))
-    tail = arrived[:, width:].astype(F32)
-    gate_col = jnp.sum(
-        (tail[:, :expert_count] + tail[:, expert_count : 2 * expert_count]) * expert_lane,
-        axis=1,
-        keepdims=True,
-    )
-    expert_rows = arrived[:, :width]
+    member_rows = cot_rows[:, width : width + expert_count].astype(F32)
+    member_row = jnp.sum(member_rows * expert_lane, axis=1) > 0.5
+    selects = []
+    for start in starts:
+        member = taken(member_row, start).reshape(-1, tokens_here)
+        slot = jnp.cumsum(member.astype(jnp.int32), axis=1) - 1
+        slot = slot + (jnp.arange(member.shape[0], dtype=jnp.int32) * block_capacity)[:, None]
+        slot = jnp.where(member, slot, -1).reshape(-1)
+        slots = block_capacity * (chunk // tokens_here)
+        selects.append((jnp.arange(slots, dtype=jnp.int32)[:, None] == slot[None, :]).astype(BF))
+    cot_own = jnp.concatenate(
+        [
+            dot(select, taken(cot_rows, start)[:, :width], 1, 0).astype(BF)
+            for select, start in zip(selects, starts)
+        ]
+    )
+    cot_core, cot_chip = to_core(cot_own), to_chip(cot_own)
+    cot_near = jnp.concatenate([cot_own, cot_core])
+    cot_far = jnp.concatenate([cot_chip, to_core(cot_chip)])
+    own_parts, core_parts, chip_parts, both_parts = [], [], [], []
+    for select, pair in zip(selects, line.gather(mid_packed)):
+        rows = dot(select, pair, 1, 0).astype(BF)
+        rows_chip = to_chip(rows)
+        own_parts.append(rows)
+        core_parts.append(to_core(rows))
+        chip_parts.append(rows_chip)
+        both_parts.append(to_core(rows_chip))
+    near = jnp.concatenate(own_parts + core_parts)
+    far = jnp.concatenate(chip_parts + both_parts)
     gate_w, up_w, down_w = expert_gate_up[0, 0], expert_gate_up[0, 1], expert_down[0]
-    gate_pre = dot(expert_rows, gate_w, 1, 0) + expert_gate_up_bias[0, 0].astype(F32)
-    up_pre = dot(expert_rows, up_w, 1, 0) + expert_gate_up_bias[0, 1].astype(F32)
-    hidden_f, glu_back = jax.vjp(swiglu, gate_pre, up_pre)
-    hidden = hidden_f.astype(BF).astype(F32)
-    hidden_gated = (hidden * gate_col).astype(BF)
-    mix_part = dot(hidden_gated, down_w, 1, 0).astype(BF)
-    grad_hidden = dot(cot_arrived, down_w, 1, 1)
-    gate_grad_part = jnp.sum(hidden * grad_hidden, axis=1)
-    grad_gate_pre, grad_up_pre = glu_back(grad_hidden * gate_col)
-    grad_gate_low = grad_gate_pre.astype(BF)
-    grad_up_low = grad_up_pre.astype(BF)
-    row_part = (dot(grad_gate_low, gate_w, 1, 1) + dot(grad_up_low, up_w, 1, 1)).astype(BF)
-    down_grad = dot(hidden_gated, cot_arrived, 0, 0)
-    gate_up_grad = jnp.stack(
-        [dot(expert_rows, grad_gate_low, 0, 0), dot(expert_rows, grad_up_low, 0, 0)]
-    )
-    gate_up_bias_grad = jnp.stack(
-        [jnp.sum(grad_gate_low.astype(F32), axis=0), jnp.sum(grad_up_low.astype(F32), axis=0)]
-    )
-
-    row_sum = scatter_fsdp(row_part)
-    gate_grad = scatter_fsdp(gate_grad_part)
-    grad_high, grad_low = split_low(gate_grad[:, None] * expert_lane)
-    back_packed = jnp.concatenate(
-        [
-            row_sum,
-            grad_high,
-            grad_low,
-            jnp.zeros((capacity, padded - width - 2 * expert_count), BF),
-        ],
-        axis=1,
-    )
-    back = scatter_seq(dot(select, back_packed, 0, 0).astype(BF))
-    mix_sum = scatter_fsdp(mix_part)
-    mixture = scatter_seq(dot(select, mix_sum, 0, 0).astype(BF)).astype(F32)
+
+    def expert(arrived, cot_arrived):
+        tail = arrived[:, width:].astype(F32)
+        gate_col = jnp.sum(
+            (tail[:, :expert_count] + tail[:, expert_count : 2 * expert_count]) * expert_lane,
+            axis=1,
+            keepdims=True,
+        )
+        expert_rows = arrived[:, :width]
+        gate_pre = dot(expert_rows, gate_w, 1, 0) + expert_gate_up_bias[0, 0].astype(F32)
+        up_pre = dot(expert_rows, up_w, 1, 0) + expert_gate_up_bias[0, 1].astype(F32)
+        hidden_f, glu_back = jax.vjp(swiglu, gate_pre, up_pre)
+        hidden = hidden_f.astype(BF).astype(F32)
+        hidden_gated = (hidden * gate_col).astype(BF)
+        grad_hidden = dot(cot_arrived, down_w, 1, 1)
+        gate_grad_part = jnp.sum(hidden * grad_hidden, axis=1)
+        grad_gate_pre, grad_up_pre = glu_back(grad_hidden * gate_col)
+        grad_gate_low = grad_gate_pre.astype(BF)
+        grad_up_low = grad_up_pre.astype(BF)
+        row_part = (dot(grad_gate_low, gate_w, 1, 1) + dot(grad_up_low, up_w, 1, 1)).astype(BF)
+        return expert_rows, hidden_gated, grad_gate_low, grad_up_low, gate_grad_part, row_part
+
+    rows_n, hidden_n, gate_n, up_n, gate_part_n, row_part_n = expert(near, cot_near)
+    rows_o, hidden_o, gate_o, up_o, gate_part_o, row_part_o = expert(far, cot_far)
+
+    half = capacity
+
+    def return_rows(near_part, far_part):
+        from_core_near, from_core_far = to_core(near_part[half:]), to_core(far_part[half:])
+        near_sum = near_part[:half].astype(F32) + from_core_near.astype(F32)
+        far_sum = far_part[:half].astype(F32) + from_core_far.astype(F32)
+        far_sum = far_sum.astype(far_part.dtype)
+        sums = []
+        for at in reversed(range(len(starts))):
+            first = at * slots
+            arrived = to_chip(far_sum[first : first + slots])
+            sums.append(near_sum[first : first + slots] + arrived.astype(F32))
+        return sums[::-1]
+
+    row_sums = return_rows(row_part_n, row_part_o)
+    gate_sums = return_rows(gate_part_n[:, None], gate_part_o[:, None])
+    back_pairs = []
+    for select, row_sum, gate_sum in zip(selects, row_sums, gate_sums):
+        grad_high, grad_low = split_low(gate_sum * expert_lane)
+        back_packed = jnp.concatenate(
+            [
+                row_sum.astype(BF),
+                grad_high,
+                grad_low,
+                jnp.zeros((slots, padded - width - 2 * expert_count), BF),
+            ],
+            axis=1,
+        )
+        back_pairs.append(dot(select, back_packed, 0, 0).astype(BF))
+    back = line.scatter(back_pairs)
+
+    mix_sums = return_rows(
+        dot(hidden_n, down_w, 1, 0).astype(BF), dot(hidden_o, down_w, 1, 0).astype(BF)
+    )
+    mix_dense = jnp.zeros((length, width), BF)
+    for select, start, mix_sum in zip(selects, starts, mix_sums):
+        mix_dense = lax.dynamic_update_slice_in_dim(
+            mix_dense, dot(select, mix_sum.astype(BF), 0, 0).astype(BF), start, 0
+        )
+    mixture = scatter_seq(mix_dense).astype(F32)
     mixture = mixture + dot(gates, down_bias_f, 1, 0, EXACT)
     layer_output = (resid_mid + mixture).astype(BF)[None]
-
-    back_tail = back[:, width:].astype(F32)
+    down_grad = dot(hidden_n, cot_near, 0, 0) + dot(hidden_o, cot_far, 0, 0)
+    gate_up_grad = jnp.stack(
+        [
+            dot(rows_n, gate_n, 0, 0) + dot(rows_o, gate_o, 0, 0),
+            dot(rows_n, up_n, 0, 0) + dot(rows_o, up_o, 0, 0),
+        ]
+    )
+
+    def column_sum(near_part, far_part):
+        return jnp.sum(near_part.astype(F32), axis=0) + jnp.sum(far_part.astype(F32), axis=0)
+
+    gate_up_bias_grad = jnp.stack([column_sum(gate_n, gate_o), column_sum(up_n, up_o)])
+
+    back_tail = back[:, width:]
     cot_f = cot_here.astype(F32)
     grad_gates = (
         back_tail[:, :expert_count]
@@ -323,7 +498,7 @@
     router_grad_t = dot(grad_logits, normed_mid.astype(F32), 0, 0, EXACT)
     router_bias_grad = jnp.sum(grad_logits, axis=0)
     down_bias_grad = dot(gates, cot_f, 0, 0, EXACT)
-    grad_normed_mid = back[:, :width].astype(F32) + dot(grad_logits, router_t.astype(F32), 1, 0, EXACT)
+    grad_normed_mid = back[:, :width] + dot(grad_logits, router_t.astype(F32), 1, 0, EXACT)
     ffn_gain_grad = jnp.sum(grad_normed_mid * unit_mid, axis=0)
     grad_unit_mid = grad_normed_mid * ffn_gain_f
     grad_mid = (
@@ -334,7 +509,9 @@
     grad_attn = grad_mid.astype(BF)
     out_bias_grad = jnp.sum(grad_attn.astype(F32), axis=0)
 
-    attn_rows = gather_seq(grad_attn)
+    attn_rows = jnp.zeros((length, width), BF)
+    for start, pair in zip(starts, line.gather(grad_attn)):
+        attn_rows = lax.dynamic_update_slice_in_dim(attn_rows, pair, start, 0)
     out_w_part = dot(heads, attn_rows, 0, 0)
     grad_heads = dot(attn_rows, wo, 1, 1).astype(BF)
     grad_heads_grid = grad_heads.reshape(query_grid.shape)
@@ -370,17 +547,23 @@
     grad_query_lin = apply_rotary(grad_query, cosine_values, sine_values, -1.0).astype(BF)
     grad_key_lin = apply_rotary(grad_key, cosine_values, sine_values, -1.0).astype(BF)
     grad_value_lin = grad_value.astype(BF)
-    normed_part = (
-        dot(grad_query_lin, wq, 1, 1) + dot(grad_key_lin, wk, 1, 1) + dot(grad_value_lin, wv, 1, 1)
-    )
-    grad_normed_in = scatter_seq(normed_part.astype(BF)).astype(F32)
+    attn_gain_grad = jnp.zeros((width,), F32)
+    normed_parts = []
+    for start in starts:
+        normed_part = (
+            dot(taken(grad_query_lin, start), wq, 1, 1)
+            + dot(taken(grad_key_lin, start), wk, 1, 1)
+            + dot(taken(grad_value_lin, start), wv, 1, 1)
+        )
+        attn_gain_grad = attn_gain_grad + jnp.sum(normed_part * taken(unit_rows, start), axis=0)
+        normed_parts.append(normed_part.astype(BF))
+    grad_normed_in = line.scatter(normed_parts)
     query_w_part = dot(grad_query_lin, normed_rows, 0, 0)
     key_w_part = dot(grad_key_lin, normed_rows, 0, 0)
     value_w_part = dot(grad_value_lin, normed_rows, 0, 0)
     query_b_part = jnp.sum(grad_query_lin.astype(F32), axis=0)
     key_b_part = jnp.sum(grad_key_lin.astype(F32), axis=0)
     value_b_part = jnp.sum(grad_value_lin.astype(F32), axis=0)
-    attn_gain_grad = jnp.sum(normed_part * unit_rows, axis=0)
 
     resid_scale = rms_scale(resid_in)
     unit_in = resid_in * resid_scale
@@ -416,7 +599,6 @@
     tiny_grad = jnp.concatenate([tiny_grad, jnp.zeros((width - tiny_grad.shape[0],), F32)])
     small_grad = jnp.concatenate(
         [
-            attn_gain_grad[None],
             out_bias_grad[None],
             ffn_gain_grad[None],
             tiny_grad[None],
@@ -434,26 +616,27 @@
         )
 
     small_own = own_part(small_sum, 1)
+    attn_gain_sum = lax.psum(attn_gain_grad, ("seq", "fsdp"))
     return (
         layer_output,
         input_grad[None],
-        small_own[0],
+        own_part(attn_gain_sum, 0),
         query_w_own,
         query_b_own,
         key_w_own,
         key_b_own,
         value_w_own,
         value_b_own,
-        own_part(small_sum[3, :QUERY_HEADS], 0),
+        own_part(small_sum[2, :QUERY_HEADS], 0),
         out_w_own,
+        small_own[0],
         small_own[1],
-        small_own[2],
-        small_own[4 + expert_count :].T,
-        own_part(small_sum[3, QUERY_HEADS : QUERY_HEADS + expert_count], 0),
+        small_own[3 + expert_count :].T,
+        own_part(small_sum[2, QUERY_HEADS : QUERY_HEADS + expert_count], 0),
         gate_up_grad[None],
         gate_up_bias_grad[None],
         down_grad[None],
-        small_own[4 : 4 + expert_count],
+        small_own[3 : 3 + expert_count],
     )
 
 

time: 1820 us -> 1300 us (0.71)
  waiting for transfers between devices: 1250 us -> 433 us
  starting transfers between devices: 0.99 us -> 120 us
  other arithmetic: 45 us -> 117 us
  local copies, waits for them, and re-layouts: 123 us -> 169 us
  blocking collectives: 32 us -> 66 us
  matrix products: 333 us -> 365 us
    unnamed x25 -> x10, waiting for transfers between devices: 514 us -> 0.82 us
    ppermute x0 -> x87, waiting for transfers between devices: none -> 400 us  [the longest x30 149 us: along(): return lax.ppermute(block, 'seq', route)]
    all_gather x4 -> x1, waiting for transfers between devices: 328 us -> 0.01 us  [gather_seq(): return lax.all_gather(block, 'seq', axis=0, tiled=True)]
    all_gather x2 -> x0, waiting for transfers between devices: 157 us -> none  [gather_fsdp(): return lax.all_gather(block, 'fsdp', axis=0, tiled=True)]
    reduce_scatter x4, waiting for transfers between devices: 164 us -> 31.4 us  [scatter_fsdp(): lax.psum_scatter(partial_rows, 'fsdp', scatter_dimension=0, tiled=True)]
    ppermute x0 -> x87, starting transfers between devices: none -> 119 us  [the longest x30 64.6 us: along(): return lax.ppermute(block, 'seq', route)]
    psum x1, waiting for transfers between devices: 63.4 us -> 0.01 us  [per_device(): small_sum = lax.psum(small_grad, ('seq', 'fsdp'))]
    unnamed x196 -> x335, local copies, waits for them, and re-layouts: 90.4 us -> 46 us
  transfers between devices with their start and end apart: 19 -> 96, of which waited for: 18 -> 35; matrix products, arithmetic and copies ran while one was open for 19% -> 47% of each run, Pallas kernels for 0% -> 0%
where the time goes in v2:
time: 1300 us; the launch traced here: 1290 us
  waiting for transfers between devices  433 us (33%)
  matrix products  365 us (28%)
  local copies, waits for them, and re-layouts  169 us (13%)
  starting transfers between devices  120 us (9%)
  other arithmetic  117 us (9%)
  blocking collectives  66 us (5%)
  between operations  19.8 us (2%)
    dot_general x64, matrix products, dot(): lax.dot_general(left, right, (((left_dim,), (right_dim,)), ((), ())), pre...  348 us
    ppermute x30, waiting for transfers between devices, along(): return lax.ppermute(block, 'seq', route)  149 us
    ppermute x17, waiting for transfers between devices, to_chip(): return lax.ppermute(block, 'fsdp', [(i, i ^ 2) for i in range(4)])  145 us
    ppermute x24, waiting for transfers between devices, across(): return lax.ppermute(block, 'seq', [(i, i ^ 1) for i in range(8)])  104 us
    ppermute x30, starting transfers between devices, along(): return lax.ppermute(block, 'seq', route)  64.6 us
    unnamed x335, local copies, waits for them, and re-layouts  46 us
    psum x1, blocking collectives, per_device(): attn_gain_sum = lax.psum(attn_gain_grad, ('seq', 'fsdp'))  43.5 us
    reduce_scatter x4, waiting for transfers between devices, scatter_fsdp(): lax.psum_scatter(partial_rows, 'fsdp', scatter_dimension=0, tiled=True)  31.4 us
  transfers between devices with their start and end apart: 96, of which 35 were waited for; matrix products, arithmetic and copies ran while one was open for 47% of the time, Pallas kernels for 0%

profile of v2, /device:TPU:0, one launch (start us, length us, event | category | flops | bytes accessed | tf_op | source)
XLA Modules:
  0.0 1289.2 jit_solution(13105436366958936959)
XLA Ops:
  50.8 14.9 %collective-permute-done.5 = bf16[128,2880]{0,1:T(8,128)(2,1)S(1)} collective-permute-done((bf16[128,2880]{0,1:T(8,128)(2,1)S(1)}, bf16[128,2880]{0,1:T(8,128)(2,1)S(1)}, u32[]{:S(2)}, u32[]{:S(2)}) %collective-permute-start.5) | collective-permute-done | bytes 737312 | tf_op jit(solution)/shard_map/ppermute | solution.py:87
  69.4 18.2 %collective-permute-done.6 = bf16[128,2880]{0,1:T(8,128)(2,1)S(1)} collective-permute-done((bf16[128,2880]{0,1:T(8,128)(2,1)S(1)}, bf16[128,2880]{0,1:T(8,128)(2,1)S(1)}, u32[]{:S(2)}, u32[]{:S(2)}) %collective-permute-start.6) | collective-permute-done | bytes 737312 | tf_op jit(solution)/shard_map/ppermute | solution.py:83
  89.8 14.7 %collective-permute-done.8 = bf16[128,2880]{0,1:T(8,128)(2,1)S(1)} collective-permute-done((bf16[128,2880]{0,1:T(8,128)(2,1)S(1)}, bf16[128,2880]{0,1:T(8,128)(2,1)S(1)}, u32[]{:S(2)}, u32[]{:S(2)}) %collective-permute-start.8) | collective-permute-done | bytes 737312 | tf_op jit(solution)/shard_map/ppermute | solution.py:87
  141.6 11.6 collective-permute-done.9
  208.9 21.0 %collective-permute-done.16 = bf16[128,2880]{0,1:T(8,128)(2,1)S(1)} collective-permute-done((bf16[128,2880]{0,1:T(8,128)(2,1)}, bf16[128,2880]{0,1:T(8,128)(2,1)S(1)}, u32[]{:S(2)}, u32[]{:S(2)}) %collective-permute-start.16) | collective-permute-done | bytes 737312 | tf_op jit(solution)/shard_map/ppermute | solution.py:83
  244.2 23.9 %collective-permute-done.18 = bf16[128,2944]{0,1:T(8,128)(2,1)} collective-permute-done((bf16[128,2944]{0,1:T(8,128)(2,1)S(1)}, bf16[128,2944]{0,1:T(8,128)(2,1)}, u32[]{:S(2)}, u32[]{:S(2)}) %collective-permute-start.18) | collective-permute-done | bytes 753696 | tf_op jit(solution)/shard_map/ppermute | solution.py:83
  268.0 20.1 %collective-permute-done.19 = bf16[128,2944]{0,1:T(8,128)(2,1)S(1)} collective-permute-done((bf16[128,2944]{0,1:T(8,128)(2,1)S(1)}, bf16[128,2944]{0,1:T(8,128)(2,1)S(1)}, u32[]{:S(2)}, u32[]{:S(2)}) %collective-permute-start.19) | collective-permute-done | bytes 753696 | tf_op jit(solution)/shard_map/ppermute | solution.py:83
  302.4 22.3 %collective-permute-done.22 = bf16[128,2944]{0,1:T(8,128)(2,1)} collective-permute-done((bf16[128,2944]{0,1:T(8,128)(2,1)S(1)}, bf16[128,2944]{0,1:T(8,128)(2,1)}, u32[]{:S(2)}, u32[]{:S(2)}) %collective-permute-start.22) | collective-permute-done | bytes 753696 | tf_op jit(solution)/shard_map/ppermute | solution.py:83
  427.4 18.8 %collective-permute-done.35 = bf16[160,2944]{1,0:T(8,128)(2,1)S(1)} collective-permute-done((bf16[160,2944]{1,0:T(8,128)(2,1)S(1)}, bf16[160,2944]{1,0:T(8,128)(2,1)S(1)}, u32[]{:S(2)}, u32[]{:S(2)}) %collective-permute-start.35) | collective-permute-done | bytes 942112 | tf_op jit(solution)/shard_map/ppermute | solution.py:183
  458.9 13.3 %concatenate.135 = bf16[1280,2880]{0,1:T(8,128)(2,1)} concatenate(bf16[160,2880]{0,1:T(8,128)(2,1)} %copy.144, bf16[160,2880]{0,1:T(8,128)(2,1)S(1)} %copy-done.27, bf16[160,2880]{0,1:T(8,128)(2,1)S(1)} %copy-done.26, bf16[160,2880]{0,1:T(8,128)(2,1)} %copy.147, bf16[640,2880]{0,1:T(8,128)(2,1)} %collective-permute-done.45), dimensions={0} | concatenate | bytes 14745600 | tf_op jit(solution)/shard_map/concatenate | solution.py:396
  483.4 41.2 %collective-permute-done.47 = bf16[640,2880]{0,1:T(8,128)(2,1)} collective-permute-done((bf16[640,2880]{0,1:T(8,128)(2,1)}, bf16[640,2880]{0,1:T(8,128)(2,1)}, u32[]{:S(2)}, u32[]{:S(2)}) %collective-permute-start.47) | collective-permute-done | bytes 3686432 | tf_op jit(solution)/shard_map/ppermute | solution.py:183
  524.6 19.6 %convert_reduce_fusion.1 = (f32[720]{0:T(1024)}, bf16[1280,720]{0,1:T(8,128)(2,1)}, f32[720]{0:T(1024)}, bf16[1280,720]{0,1:T(8,128)(2,1)S(1)}, f32[1280]{0:T(1024)S(1)}, /*index=5*/bf16[1280,720]{0,1:T(8,128)(2,1)}) fusion(f32[1280,720]{0,1:T(8,128)} %fusion.63, f32[1280,720]{0,1:T(8,128)} %fusion.20, f32[1280]{0:T(1024)S(1)} %get-tuple-element.155, ...), kind=kOutput, calls=%fused_computation.135 | convolution fusion | flops 5355415552 | bytes 24697280 | tf_op jit(solution)/shard_map/dot_general | solution.py:52
  556.9 11.7 fusion.22
  568.7 17.8 %convert_reduce_fusion = (f32[720]{0:T(1024)}, bf16[1280,720]{0,1:T(8,128)(2,1)S(1)}, f32[720]{0:T(1024)}, bf16[1280,720]{0,1:T(8,128)(2,1)S(1)}, f32[1280]{0:T(1024)S(1)}, /*index=5*/bf16[1280,720]{0,1:T(8,128)(2,1)}) fusion(f32[1280,720]{0,1:T(8,128)} %fusion.83, f32[1280,720]{0,1:T(8,128)} %fusion.22, f32[1280]{0:T(1024)S(1)} %get-tuple-element.154, ...), kind=kOutput, calls=%fused_computation.134 | convolution fusion | flops 5355415552 | bytes 24697280 | tf_op jit(solution)/shard_map/dot_general | solution.py:52
  586.4 14.1 %fusion.26 = f32[1280,2880]{0,1:T(8,128)} fusion(bf16[1280,720]{0,1:T(8,128)(2,1)S(1)} %get-tuple-element.193, bf16[1,2,2880,720]{2,3,1,0:T(8,128)(2,1)} %param.36), kind=kOutput, calls=%fused_computation.59 | convolution fusion | flops 5308416000 | bytes 20828160 | tf_op jit(solution)/shard_map/dot_general | solution.py:52
  600.5 13.8 %add_convert_fusion = bf16[1280,2880]{0,1:T(8,128)(2,1)} fusion(f32[1280,2880]{0,1:T(8,128)} %fusion.26, bf16[1280,720]{0,1:T(8,128)(2,1)S(1)} %get-tuple-element.164, bf16[1,2,2880,720]{2,3,1,0:T(8,128)(2,1)} %param.36), kind=kOutput, calls=%fused_computation.1 | convolution fusion | flops 5315788800 | bytes 28200960 | tf_op jit(solution)/shard_map/dot_general | solution.py:52
  617.2 16.0 %add_convert_fusion.1 = bf16[1280,2880]{0,1:T(8,128)(2,1)} fusion(f32[1280,2880]{0,1:T(8,128)} %fusion.28, bf16[1280,720]{0,1:T(8,128)(2,1)} %get-tuple-element.166, bf16[1,2,2880,720]{2,3,1,0:T(8,128)(2,1)} %param.36), kind=kOutput, calls=%fused_computation.2 | convolution fusion | flops 5315788800 | bytes 28200960 | tf_op jit(solution)/shard_map/dot_general | solution.py:52
  638.2 11.9 convolution_convert_fusion
  695.7 18.3 %collective-permute-done.54 = bf16[160,2880]{1,0:T(8,128)(2,1)} collective-permute-done((bf16[160,2880]{1,0:T(8,128)(2,1)}, bf16[160,2880]{1,0:T(8,128)(2,1)}, u32[]{:S(2)}, u32[]{:S(2)}) %collective-permute-start.54) | collective-permute-done | bytes 921632 | tf_op jit(solution)/shard_map/ppermute | solution.py:183
  715.9 18.3 %collective-permute-done.56 = bf16[160,2880]{1,0:T(8,128)(2,1)} collective-permute-done((bf16[160,2880]{1,0:T(8,128)(2,1)}, bf16[160,2880]{1,0:T(8,128)(2,1)}, u32[]{:S(2)}, u32[]{:S(2)}) %collective-permute-start.56) | collective-permute-done | bytes 921632 | tf_op jit(solution)/shard_map/ppermute | solution.py:183
  736.6 15.7 %collective-permute-done.61 = bf16[160,2880]{1,0:T(8,128)(2,1)} collective-permute-done((bf16[160,2880]{1,0:T(8,128)(2,1)}, bf16[160,2880]{1,0:T(8,128)(2,1)}, u32[]{:S(2)}, u32[]{:S(2)}) %collective-permute-start.61) | collective-permute-done | bytes 921632 | tf_op jit(solution)/shard_map/ppermute | solution.py:183
  915.3 13.1 %collective-permute-done.74 = bf16[128,2880]{0,1:T(8,128)(2,1)S(1)} collective-permute-done((bf16[128,2880]{0,1:T(8,128)(2,1)S(1)}, bf16[128,2880]{0,1:T(8,128)(2,1)S(1)}, u32[]{:S(2)}, u32[]{:S(2)}) %collective-permute-start.74) | collective-permute-done | bytes 737312 | tf_op jit(solution)/shard_map/ppermute | solution.py:87
  933.9 14.6 %collective-permute-done.75 = bf16[128,2880]{0,1:T(8,128)(2,1)S(1)} collective-permute-done((bf16[128,2880]{0,1:T(8,128)(2,1)S(1)}, bf16[128,2880]{0,1:T(8,128)(2,1)S(1)}, u32[]{:S(2)}, u32[]{:S(2)}) %collective-permute-start.75) | collective-permute-done | bytes 737312 | tf_op jit(solution)/shard_map/ppermute | solution.py:83
  950.3 13.5 %collective-permute-done.77 = bf16[128,2880]{0,1:T(8,128)(2,1)S(1)} collective-permute-done((bf16[128,2880]{0,1:T(8,128)(2,1)S(1)}, bf16[128,2880]{0,1:T(8,128)(2,1)S(1)}, u32[]{:S(2)}, u32[]{:S(2)}) %collective-permute-start.77) | collective-permute-done | bytes 737312 | tf_op jit(solution)/shard_map/ppermute | solution.py:87
  1031.8 11.8 fusion.146
  1043.6 11.5 fusion.12
  1055.1 11.5 fusion.14
  1090.1 13.2 %multiply_reduce_fusion.2 = (f32[2880]{0:T(1024)}, f32[2880]{0:T(1024)}, f32[2880]{0:T(1024)}, f32[2880]{0:T(1024)}, bf16[256,2880]{0,1:T(8,128)(2,1)}, /*index=...) fusion(f32[1024,2880]{0,1:T(8,128)S(1)} %bitcast.353, s32[]{:T(128)S(6)} %select_n.347, ...), kind=kOutput, calls=%fused_computation.180 | convolution fusion | flops 103944960 | bytes 29949440 | tf_op jit(solution)/shard_map/dot_general | solution.py:52
  1130.3 12.5 add_bitcast_fusion.1
  1150.2 12.8 add_bitcast_fusion
  1190.4 43.5 %psum.14 = f32[2880]{0:T(1024)S(1)} all-reduce(f32[2880]{0:T(1024)S(1)} %add_add_fusion), channel_id=1, replica_groups=mesh['seq'=8,'fsdp'=4] {'seq','fsdp'}, use_global_device_ids=true, to_apply=%region_29.31 | all-reduce | flops 2880 | bytes 23040 | tf_op jit(solution)/shard_map/psum | solution.py:619
  1250.2 31.4 %reduce-scatter.8.cloned.1.call-done = f32[128,2880]{0,1:T(8,128)} async-done(((f32[512,2880]{0,1:T(8,128)}), f32[128,2880]{0,1:T(8,128)}) %reduce-scatter.8.cloned.1.call-update) | async-done | bytes 1474576 | tf_op jit(solution)/shard_map/reduce_scatter | solution.py:175
  (816 shorter events, 702.9 us)
Async XLA Ops:
  8.1 108.2 %all-gather.6.cloned.1.call-start = ((), (), s32[]{:S(2)}) async-start(), calls=%async_computation.5 | async-start | bytes 3686400 | tf_op jit(solution)/shard_map/all_gather | solution.py:308
  8.8 123.2 %all-gather.8.cloned.1.call-start = ((), (), s32[]{:S(2)}) async-start(), calls=%async_computation.6 | async-start | bytes 3686400 | tf_op jit(solution)/shard_map/all_gather | solution.py:309
  8.9 35.9 %collective-permute-start = (bf16[128,2880]{0,1:T(8,128)(2,1)}, bf16[128,2880]{0,1:T(8,128)(2,1)S(1)}, u32[]{:S(2)}, u32[]{:S(2)}) collective-permute-start(bf16[128,2880]{0,1:T(8,128)(2,1)} %bitcast.354), channel_id=1, source_target_pairs={{0,8},{4,12},{8,16},{12,20},{16,24},{20,28},{1,9},{5,13},{9,17},{1... | collective-permute-start | bytes 2211848 | tf_op jit(solution)/shard_map/ppermute | solution.py:83
  16.8 341.2 %all-gather.10.cloned.1.call-start = ((), (), s32[]{:S(2)}) async-start(), calls=%async_computation.7 | async-start | bytes 6782976 | tf_op jit(solution)/shard_map/all_gather | solution.py:167
  181.4 1053.3 %all-reduce.10.cloned.1.call-start = ((), (), s32[]{:S(2)}) async-start(), calls=%async_computation.11 | async-start | bytes 565248 | tf_op jit(solution)/shard_map/psum | solution.py:610
  241.3 46.8 %collective-permute-start.19 = (bf16[128,2944]{0,1:T(8,128)(2,1)S(1)}, bf16[128,2944]{0,1:T(8,128)(2,1)S(1)}, u32[]{:S(2)}, u32[]{:S(2)}) collective-permute-start(bf16[128,2944]{0,1:T(8,128)(2,1)S(1)} %maximum_maximum_fusion.1), channel_id=1, source_target_pairs={{8,0},{12,4},{16,8},{20,12},{24,16},{28,20},{9,1},{13,5},{17,9},{2... | collective-permute-start | bytes 2261000 | tf_op jit(solution)/shard_map/ppermute | solution.py:83
  242.6 45.5 %collective-permute-start.20 = (bf16[128,2944]{0,1:T(8,128)(2,1)S(1)}, bf16[128,2944]{0,1:T(8,128)(2,1)}, u32[]{:S(2)}, u32[]{:S(2)}) collective-permute-start(bf16[128,2944]{0,1:T(8,128)(2,1)S(1)} %maximum_maximum_fusion.1), channel_id=1, source_target_pairs={{0,4},{4,0},{8,12},{12,8},{16,20},{20,16},{24,28},{28,24},{1,5},{5... | collective-permute-start | bytes 2261000 | tf_op jit(solution)/shard_map/ppermute | solution.py:87
  363.1 59.1 %collective-permute-start.32 = (bf16[160,2944]{1,0:T(8,128)(2,1)}, bf16[160,2944]{1,0:T(8,128)(2,1)}, u32[]{:S(2)}, u32[]{:S(2)}) collective-permute-start(bf16[160,2944]{1,0:T(8,128)(2,1)} %get-tuple-element.306), channel_id=1, source_target_pairs={{0,2},{1,3},{2,0},{3,1},{4,6},{5,7},{6,4},{7,5},{8,10},{9,11},{10,... | collective-permute-start | bytes 2826248 | tf_op jit(solution)/shard_map/ppermute | solution.py:183
  366.7 58.6 %collective-permute-start.33 = (bf16[160,2944]{1,0:T(8,128)(2,1)}, bf16[160,2944]{1,0:T(8,128)(2,1)}, u32[]{:S(2)}, u32[]{:S(2)}) collective-permute-start(bf16[160,2944]{1,0:T(8,128)(2,1)} %get-tuple-element.308), channel_id=1, source_target_pairs={{0,2},{1,3},{2,0},{3,1},{4,6},{5,7},{6,4},{7,5},{8,10},{9,11},{10,... | collective-permute-start | bytes 2826248 | tf_op jit(solution)/shard_map/ppermute | solution.py:183
  406.1 40.0 %collective-permute-start.35 = (bf16[160,2944]{1,0:T(8,128)(2,1)S(1)}, bf16[160,2944]{1,0:T(8,128)(2,1)S(1)}, u32[]{:S(2)}, u32[]{:S(2)}) collective-permute-start(bf16[160,2944]{1,0:T(8,128)(2,1)S(1)} %get-tuple-element.312), channel_id=1, source_target_pairs={{0,2},{1,3},{2,0},{3,1},{4,6},{5,7},{6,4},{7,5},{8,10},{9,11},{10,... | collective-permute-start | bytes 2826248 | tf_op jit(solution)/shard_map/ppermute | solution.py:183
  408.6 50.2 %collective-permute-start.45 = (bf16[640,2880]{0,1:T(8,128)(2,1)}, bf16[640,2880]{0,1:T(8,128)(2,1)}, u32[]{:S(2)}, u32[]{:S(2)}) collective-permute-start(bf16[640,2880]{0,1:T(8,128)(2,1)} %copy.143), channel_id=1, source_target_pairs={{0,1},{1,0},{2,3},{3,2},{4,5},{5,4},{6,7},{7,6},{8,9},{9,8},{10,11... | collective-permute-start | bytes 11059208 | tf_op jit(solution)/shard_map/ppermute | solution.py:179
  422.2 102.4 %collective-permute-start.47 = (bf16[640,2880]{0,1:T(8,128)(2,1)}, bf16[640,2880]{0,1:T(8,128)(2,1)}, u32[]{:S(2)}, u32[]{:S(2)}) collective-permute-start(bf16[640,2880]{0,1:T(8,128)(2,1)} %copy.143), channel_id=1, source_target_pairs={{0,2},{1,3},{2,0},{3,1},{4,6},{5,7},{6,4},{7,5},{8,10},{9,11},{10,... | collective-permute-start | bytes 11059208 | tf_op jit(solution)/shard_map/ppermute | solution.py:183
  544.2 93.4 %collective-permute-start.51 = (f32[640,1]{0,1:T(1,128)S(1)}, f32[640,1]{0,1:T(1,128)S(1)}, u32[]{:S(2)}, u32[]{:S(2)}) collective-permute-start(f32[640,1]{0,1:T(1,128)S(1)} %slice.359), channel_id=1, source_target_pairs={{0,1},{1,0},{2,3},{3,2},{4,5},{5,4},{6,7},{7,6},{8,9},{9,8},{10,11... | collective-permute-start | bytes 7688 | tf_op jit(solution)/shard_map/ppermute | solution.py:179
  616.6 37.3 %collective-permute-start.49 = (bf16[640,2880]{0,1:T(8,128)(2,1)S(1)}, bf16[640,2880]{0,1:T(8,128)(2,1)}, u32[]{:S(2)}, u32[]{:S(2)}) collective-permute-start(bf16[640,2880]{0,1:T(8,128)(2,1)S(1)} %slice.439), channel_id=1, source_target_pairs={{0,1},{1,0},{2,3},{3,2},{4,5},{5,4},{6,7},{7,6},{8,9},{9,8},{10,11... | collective-permute-start | bytes 11059208 | tf_op jit(solution)/shard_map/ppermute | solution.py:179
  671.4 42.6 %collective-permute-start.54 = (bf16[160,2880]{1,0:T(8,128)(2,1)}, bf16[160,2880]{1,0:T(8,128)(2,1)}, u32[]{:S(2)}, u32[]{:S(2)}) collective-permute-start(bf16[160,2880]{1,0:T(8,128)(2,1)} %copy.152), channel_id=1, source_target_pairs={{0,2},{1,3},{2,0},{3,1},{4,6},{5,7},{6,4},{7,5},{8,10},{9,11},{10,... | collective-permute-start | bytes 2764808 | tf_op jit(solution)/shard_map/ppermute | solution.py:183
  671.7 62.5 %collective-permute-start.56 = (bf16[160,2880]{1,0:T(8,128)(2,1)}, bf16[160,2880]{1,0:T(8,128)(2,1)}, u32[]{:S(2)}, u32[]{:S(2)}) collective-permute-start(bf16[160,2880]{1,0:T(8,128)(2,1)} %copy.155), channel_id=1, source_target_pairs={{0,2},{1,3},{2,0},{3,1},{4,6},{5,7},{6,4},{7,5},{8,10},{9,11},{10,... | collective-permute-start | bytes 2764808 | tf_op jit(solution)/shard_map/ppermute | solution.py:183
  673.4 78.9 %collective-permute-start.61 = (bf16[160,2880]{1,0:T(8,128)(2,1)}, bf16[160,2880]{1,0:T(8,128)(2,1)}, u32[]{:S(2)}, u32[]{:S(2)}) collective-permute-start(bf16[160,2880]{1,0:T(8,128)(2,1)} %copy.158), channel_id=1, source_target_pairs={{0,2},{1,3},{2,0},{3,1},{4,6},{5,7},{6,4},{7,5},{8,10},{9,11},{10,... | collective-permute-start | bytes 2764808 | tf_op jit(solution)/shard_map/ppermute | solution.py:183
  682.8 105.0 %collective-permute-start.40 = (bf16[640,2880]{0,1:T(8,128)(2,1)}, bf16[640,2880]{0,1:T(8,128)(2,1)}, u32[]{:S(2)}, u32[]{:S(2)}) collective-permute-start(bf16[640,2880]{0,1:T(8,128)(2,1)} %slice.426), channel_id=1, source_target_pairs={{0,1},{1,0},{2,3},{3,2},{4,5},{5,4},{6,7},{7,6},{8,9},{9,8},{10,11... | collective-permute-start | bytes 11059208 | tf_op jit(solution)/shard_map/ppermute | solution.py:179
  782.3 55.6 %collective-permute-start.31 = (bf16[640,2880]{0,1:T(8,128)(2,1)}, bf16[640,2880]{0,1:T(8,128)(2,1)}, u32[]{:S(2)}, u32[]{:S(2)}) collective-permute-start(bf16[640,2880]{0,1:T(8,128)(2,1)} %slice.419), channel_id=1, source_target_pairs={{0,1},{1,0},{2,3},{3,2},{4,5},{5,4},{6,7},{7,6},{8,9},{9,8},{10,11... | collective-permute-start | bytes 11059208 | tf_op jit(solution)/shard_map/ppermute | solution.py:179
  834.2 39.8 %collective-permute-start.67 = (bf16[128,2944]{0,1:T(8,128)(2,1)}, bf16[128,2944]{0,1:T(8,128)(2,1)}, u32[]{:S(2)}, u32[]{:S(2)}) collective-permute-start(bf16[128,2944]{0,1:T(8,128)(2,1)} %get-tuple-element.222), channel_id=1, source_target_pairs={{0,8},{4,12},{8,16},{12,20},{16,24},{20,28},{1,9},{5,13},{9,17},{1... | collective-permute-start | bytes 2261000 | tf_op jit(solution)/shard_map/ppermute | solution.py:83
  836.6 37.4 %collective-permute-start.68 = (bf16[128,2944]{0,1:T(8,128)(2,1)}, bf16[128,2944]{0,1:T(8,128)(2,1)}, u32[]{:S(2)}, u32[]{:S(2)}) collective-permute-start(bf16[128,2944]{0,1:T(8,128)(2,1)} %get-tuple-element.223), channel_id=1, source_target_pairs={{8,0},{12,4},{16,8},{20,12},{24,16},{28,20},{9,1},{13,5},{17,9},{2... | collective-permute-start | bytes 2261000 | tf_op jit(solution)/shard_map/ppermute | solution.py:83
  837.9 36.1 %collective-permute-start.66 = (bf16[128,2944]{0,1:T(8,128)(2,1)}, bf16[128,2944]{0,1:T(8,128)(2,1)}, u32[]{:S(2)}, u32[]{:S(2)}) collective-permute-start(bf16[128,2944]{0,1:T(8,128)(2,1)} %constant_dynamic-slice_fusion.7), channel_id=1, source_target_pairs={{0,4},{4,0},{8,12},{12,8},{16,20},{20,16},{24,28},{28,24},{1,5},{5... | collective-permute-start | bytes 2261000 | tf_op jit(solution)/shard_map/ppermute | solution.py:87
  848.7 40.3 %collective-permute-start.43 = (bf16[160,2880]{1,0:T(8,128)(2,1)}, bf16[160,2880]{1,0:T(8,128)(2,1)}, u32[]{:S(2)}, u32[]{:S(2)}) collective-permute-start(bf16[160,2880]{1,0:T(8,128)(2,1)} %copy.138), channel_id=1, source_target_pairs={{0,2},{1,3},{2,0},{3,1},{4,6},{5,7},{6,4},{7,5},{8,10},{9,11},{10,... | collective-permute-start | bytes 2764808 | tf_op jit(solution)/shard_map/ppermute | solution.py:183
  863.3 38.5 %collective-permute-start.44 = (bf16[160,2880]{1,0:T(8,128)(2,1)}, bf16[160,2880]{1,0:T(8,128)(2,1)}, u32[]{:S(2)}, u32[]{:S(2)}) collective-permute-start(bf16[160,2880]{1,0:T(8,128)(2,1)} %copy.140), channel_id=1, source_target_pairs={{0,2},{1,3},{2,0},{3,1},{4,6},{5,7},{6,4},{7,5},{8,10},{9,11},{10,... | collective-permute-start | bytes 2764808 | tf_op jit(solution)/shard_map/ppermute | solution.py:183
  983.6 263.0 %reduce-scatter.16.cloned.1.call-start = ((), (), s32[]{:S(2)}) async-start(), calls=%async_computation.13 | async-start | bytes 6782976
  996.7 253.5 %reduce-scatter.12.cloned.1.call-start = ((), (), s32[]{:S(2)}) async-start(), calls=%async_computation.10 | async-start | bytes 942080 | tf_op jit(solution)/shard_map/reduce_scatter | solution.py:175
  1008.1 242.1 %reduce-scatter.10.cloned.1.call-start = ((), (), s32[]{:S(2)}) async-start(), calls=%async_computation.9 | async-start | bytes 942080 | tf_op jit(solution)/shard_map/reduce_scatter | solution.py:175
  1021.1 229.1 %reduce-scatter.14.cloned.1.call-start = ((), (), s32[]{:S(2)}) async-start(), calls=%async_computation.12 | async-start | bytes 7372800 | tf_op jit(solution)/shard_map/reduce_scatter | solution.py:175
  1031.1 250.5 %reduce-scatter.8.cloned.1.call-start = ((), (), s32[]{:S(2)}) async-start(), calls=%async_computation.8 | async-start | bytes 7372800 | tf_op jit(solution)/shard_map/reduce_scatter | solution.py:175
  1167.3 73.9 %collective-permute-start.85 = (bf16[128,2880]{0,1:T(8,128)(2,1)}, bf16[128,2880]{0,1:T(8,128)(2,1)S(1)}, u32[]{:S(2)}, u32[]{:S(2)}) collective-permute-start(bf16[128,2880]{0,1:T(8,128)(2,1)} %get-tuple-element.224), channel_id=1, source_target_pairs={{0,8},{4,12},{8,16},{12,20},{16,24},{20,28},{1,9},{5,13},{9,17},{1... | collective-permute-start | bytes 2211848 | tf_op jit(solution)/shard_map/ppermute | solution.py:83
  1169.4 71.7 %collective-permute-start.86 = (bf16[128,2880]{0,1:T(8,128)(2,1)}, bf16[128,2880]{0,1:T(8,128)(2,1)}, u32[]{:S(2)}, u32[]{:S(2)}) collective-permute-start(bf16[128,2880]{0,1:T(8,128)(2,1)} %get-tuple-element.225), channel_id=1, source_target_pairs={{8,0},{12,4},{16,8},{20,12},{24,16},{28,20},{9,1},{13,5},{17,9},{2... | collective-permute-start | bytes 2211848 | tf_op jit(solution)/shard_map/ppermute | solution.py:83
  1170.9 70.3 %collective-permute-start.84 = (bf16[128,2880]{0,1:T(8,128)(2,1)}, bf16[128,2880]{0,1:T(8,128)(2,1)}, u32[]{:S(2)}, u32[]{:S(2)}) collective-permute-start(bf16[128,2880]{0,1:T(8,128)(2,1)} %constant_dynamic-slice_fusion.3), channel_id=1, source_target_pairs={{0,4},{4,0},{8,12},{12,8},{16,20},{20,16},{24,28},{28,24},{1,5},{5... | collective-permute-start | bytes 2211848 | tf_op jit(solution)/shard_map/ppermute | solution.py:87
  (221 other events, 4599.6 us)
Sparse Core Ops, SparseCore 0:
  10.4 33.2 all-gather.5
  45.3 27.4 all-gather.7
  983.8 167.0 all-reduce.9
Sparse Core Ops, SparseCore 1:
  181.4 133.1 all-gather.9
  996.8 114.2 reduce-scatter.15
  1114.2 22.5 reduce-scatter.11
  1139.8 23.0 reduce-scatter.9
  1166.2 56.3 reduce-scatter.13
  1225.7 55.8 reduce-scatter.7

commit v3 on v2

v3 whole, which is shorter than its diff:
```python
import jax
import jax.numpy as jnp
from jax import lax
from jax.experimental import pallas as pl
from jax.experimental.pallas import tpu as pltpu
from jax.sharding import PartitionSpec as P

QUERY_HEADS = 64
KEY_VALUE_HEADS = 8
HEAD_DIM = 64
WINDOW_LENGTH = 128


ROPE_BASE = 150000.0
NORM_EPS = 1e-05
GLU_ALPHA = 1.702
GLU_LIMIT = 7.0
EXACT = lax.Precision.HIGHEST
BF = jnp.bfloat16
F32 = jnp.float32
VMEM_BYTES = 60 * 2**20


def dot(left, right, left_dim, right_dim, precision=None):
    return lax.dot_general(
        left,
        right,
        (((left_dim,), (right_dim,)), ((), ())),
        precision=precision,
        preferred_element_type=jnp.float32,
    )


def turn_halves(values, cosines, sines):
    rows, width = values.shape
    half = HEAD_DIM // 2
    lane = lax.broadcasted_iota(jnp.int32, (rows, width), 1) % HEAD_DIM
    ahead = pltpu.roll(values, width - half, 1)
    behind = pltpu.roll(values, half, 1)
    other = jnp.where(lane < half, ahead, behind)
    copies = width // cosines.shape[1]
    wide_cos = jnp.concatenate([cosines] * copies, axis=1)
    wide_sin = jnp.concatenate([sines] * copies, axis=1)
    return values * wide_cos + other * wide_sin


def turn_keys(pair, cosines, sines, direction):
    lane = lax.broadcasted_iota(jnp.int32, pair.shape, 1)
    keys = lane < HEAD_DIM
    return turn_halves(pair, jnp.where(keys, cosines, 1.0), jnp.where(keys, direction * sines, 0.0))


def stack_heads(rows):
    return jnp.concatenate(
        [rows[:, at : at + HEAD_DIM] for at in range(0, rows.shape[1], HEAD_DIM)], axis=0
    )


def unstack_heads(stacked, rows):
    return jnp.concatenate(
        [stacked[at : at + rows] for at in range(0, stacked.shape[0], rows)], axis=1
    )


def block_probs(block, ends_ref, sinks_ref, queries, keys, rows):
    heads = queries.shape[0] // rows
    spread = lax.broadcasted_iota(jnp.int32, (rows, 2 * rows), 0)
    key_at = lax.broadcasted_iota(jnp.int32, (rows, 2 * rows), 1)
    position = block * rows + spread
    key_pos = (block - 1) * rows + key_at
    offset = position - key_pos
    allowed = (key_pos >= 0) & (offset >= 0) & (offset <= WINDOW_LENGTH)
    for document in range(ends_ref.shape[0]):
        end = ends_ref[document]
        allowed = allowed & ((position >= end) == (key_pos >= end))
    scores = dot(queries, keys, 1, 1) * 0.125
    scores = scores.reshape(heads, rows, 2 * rows)
    scores = jnp.where(allowed[None], scores, -1e30)
    head = lax.broadcasted_iota(jnp.int32, (heads, rows, 1), 0)
    sink = jnp.zeros((heads, rows, 1), F32)
    for at in range(heads):
        sink = jnp.where(head == at, sinks_ref[at], sink)
    top = jnp.maximum(jnp.max(scores, axis=-1, keepdims=True), sink)
    weights = jnp.exp(scores - top)
    sink_weight = jnp.exp(sink - top)
    inverse = 1.0 / (jnp.sum(weights, axis=-1, keepdims=True) + sink_weight)
    probs = (weights * inverse).reshape(heads * rows, 2 * rows)
    return probs, sink_weight * inverse


def attend_kernel(
    ends_ref, sinks_ref, lin_ref, before_ref, cos_ref, sin_ref, cos_before_ref, sin_before_ref,
    turned_ref, heads_ref,
):
    block = pl.program_id(0)
    rows = lin_ref.shape[0]
    wide = lin_ref.shape[1] - 2 * HEAD_DIM
    cosines, sines = cos_ref[...], sin_ref[...]
    queries = turn_halves(lin_ref[:, :wide], cosines, sines).astype(BF)
    own = turn_keys(lin_ref[:, wide:], cosines, sines, 1.0).astype(BF)
    before = turn_keys(before_ref[...], cos_before_ref[...], sin_before_ref[...], 1.0).astype(BF)
    turned_ref[:, :wide] = queries
    turned_ref[:, wide:] = own
    pair = jnp.concatenate([before, own], axis=0)
    probs, _ = block_probs(
        block, ends_ref, sinks_ref, stack_heads(queries), pair[:, :HEAD_DIM], rows
    )
    mixed = dot(probs.astype(BF), pair[:, HEAD_DIM:], 1, 0)
    heads_ref[...] = unstack_heads(mixed.astype(BF), rows)


def attend(lin, cosines, sines, doc_ends, sinks):
    length, full = lin.shape
    rows = WINDOW_LENGTH
    wide = full - 2 * HEAD_DIM
    pair_at = wide // (2 * HEAD_DIM)
    smem = pl.BlockSpec(memory_space=pltpu.SMEM)
    here = lambda block: (block, 0)
    previous = lambda block: (jnp.maximum(block - 1, 0), 0)
    table = pl.BlockSpec((rows, 2 * HEAD_DIM), here)
    table_before = pl.BlockSpec((rows, 2 * HEAD_DIM), previous)
    return pl.pallas_call(
        attend_kernel,
        grid=(length // rows,),
        in_specs=[
            smem,
            smem,
            pl.BlockSpec((rows, full), here),
            pl.BlockSpec((rows, 2 * HEAD_DIM), lambda block: (jnp.maximum(block - 1, 0), pair_at)),
            table,
            table,
            table_before,
            table_before,
        ],
        out_specs=[pl.BlockSpec((rows, full), here), pl.BlockSpec((rows, wide), here)],
        out_shape=[
            jax.ShapeDtypeStruct((length, full), BF),
            jax.ShapeDtypeStruct((length, wide), BF),
        ],
        compiler_params=pltpu.CompilerParams(vmem_limit_bytes=VMEM_BYTES),
        cost_estimate=pl.CostEstimate(
            flops=8 * length * rows * full, bytes_accessed=10 * length * full,
            transcendentals=2 * length * rows * wide // HEAD_DIM,
        ),
    )(doc_ends, sinks, lin, lin, cosines, sines, cosines, sines)


def attend_back_kernel(
    ends_ref, sinks_ref, turned_ref, before_ref, cos_ref, sin_ref, grad_ref,
    out_ref, sums_ref, sink_ref, carry_ref,
):
    step = pl.program_id(0)
    block = pl.num_programs(0) - 1 - step
    rows = turned_ref.shape[0]
    wide = turned_ref.shape[1] - 2 * HEAD_DIM

    @pl.when(step == 0)
    def _():
        carry_ref[...] = jnp.zeros_like(carry_ref)
        sums_ref[...] = jnp.zeros_like(sums_ref)
        sink_ref[...] = jnp.zeros_like(sink_ref)

    queries = stack_heads(turned_ref[:, :wide])
    grads = stack_heads(grad_ref[...])
    pair = jnp.concatenate([before_ref[...], turned_ref[:, wide:]], axis=0)
    keys, values = pair[:, :HEAD_DIM], pair[:, HEAD_DIM:]
    probs, sink_share = block_probs(block, ends_ref, sinks_ref, queries, keys, rows)
    grad_probs = dot(grads, values, 1, 1)
    row_delta = jnp.sum(probs * grad_probs, axis=-1, keepdims=True)
    grad_scores = (probs * (grad_probs - row_delta)).astype(BF)
    heads = wide // HEAD_DIM
    sink_part = sink_share * row_delta.reshape(heads, rows, 1)
    sink_ref[...] -= jnp.broadcast_to(jnp.sum(sink_part, axis=1), sink_ref.shape)
    grad_query = unstack_heads(dot(grad_scores, keys, 1, 0) * 0.125, rows)
    grad_pair = jnp.concatenate(
        [dot(grad_scores, queries, 0, 0) * 0.125, dot(probs.astype(BF), grads, 0, 0)], axis=1
    )
    own_pair = grad_pair[rows:] + carry_ref[...]
    carry_ref[...] = grad_pair[:rows]
    cosines, sines = cos_ref[...], sin_ref[...]
    query_out = turn_halves(grad_query, cosines, -sines).astype(BF)
    pair_out = turn_keys(own_pair, cosines, sines, -1.0).astype(BF)
    out_ref[:, :wide] = query_out
    out_ref[:, wide:] = pair_out
    sums_ref[:, :wide] += jnp.broadcast_to(
        jnp.sum(query_out.astype(F32), axis=0, keepdims=True), (sums_ref.shape[0], wide)
    )
    sums_ref[:, wide:] += jnp.broadcast_to(
        jnp.sum(pair_out.astype(F32), axis=0, keepdims=True), (sums_ref.shape[0], 2 * HEAD_DIM)
    )


def attend_back(turned, cosines, sines, doc_ends, sinks, grads):
    length, full = turned.shape
    rows = WINDOW_LENGTH
    wide = full - 2 * HEAD_DIM
    heads = wide // HEAD_DIM
    pair_at = wide // (2 * HEAD_DIM)
    last = length // rows - 1
    smem = pl.BlockSpec(memory_space=pltpu.SMEM)
    here = lambda step: (last - step, 0)
    still = lambda step: (0, 0)
    table = pl.BlockSpec((rows, 2 * HEAD_DIM), here)
    grad_all, sums, sink_grad = pl.pallas_call(
        attend_back_kernel,
        grid=(length // rows,),
        in_specs=[
            smem,
            smem,
            pl.BlockSpec((rows, full), here),
            pl.BlockSpec(
                (rows, 2 * HEAD_DIM), lambda step: (jnp.maximum(last - step - 1, 0), pair_at)
            ),
            table,
            table,
            pl.BlockSpec((rows, wide), here),
        ],
        out_specs=[
            pl.BlockSpec((rows, full), here),
            pl.BlockSpec((8, full), still),
            pl.BlockSpec((heads, 128), still),
        ],
        out_shape=[
            jax.ShapeDtypeStruct((length, full), BF),
            jax.ShapeDtypeStruct((8, full), F32),
            jax.ShapeDtypeStruct((heads, 128), F32),
        ],
        scratch_shapes=[pltpu.VMEM((rows, 2 * HEAD_DIM), F32)],
        compiler_params=pltpu.CompilerParams(vmem_limit_bytes=VMEM_BYTES),
        cost_estimate=pl.CostEstimate(
            flops=20 * length * rows * full, bytes_accessed=10 * length * full,
            transcendentals=2 * length * rows * heads,
        ),
    )(doc_ends, sinks, turned, turned, cosines, sines, grads)
    return grad_all, sums[0], sink_grad[:, 0]


def rms_scale(values):
    return lax.rsqrt(jnp.mean(values * values, axis=-1, keepdims=True) + NORM_EPS)


def rope_tables(length):
    lane = jnp.arange(2 * HEAD_DIM, dtype=jnp.int32)
    frequency = ROPE_BASE ** (-(lane % (HEAD_DIM // 2)).astype(F32) * 2.0 / HEAD_DIM)
    angles = jnp.arange(length, dtype=F32)[:, None] * frequency[None, :]
    sign = jnp.where(lane % HEAD_DIM < HEAD_DIM // 2, -1.0, 1.0)
    return jnp.cos(angles), jnp.sin(angles) * sign


def swiglu(gate_pre, up_pre):
    gate_soft = GLU_LIMIT - jax.nn.softplus(GLU_LIMIT - gate_pre)
    up_soft = GLU_LIMIT * jnp.tanh(up_pre / GLU_LIMIT)
    return (up_soft + 1.0) * gate_soft * jax.nn.sigmoid(GLU_ALPHA * gate_soft)


class Work:
    def __init__(self):
        self.waiting = []
        self.done = {}
        self.pool = {}

    def add(self, name, make, *inputs):
        self.waiting.append([name, make, list(inputs)])

    def run(self, entry):
        _, make, inputs = entry
        return make(*(self.done[item] if isinstance(item, str) else item for item in inputs))

    def take(self, name):
        while name not in self.done:
            entry = self.waiting.pop(0)
            self.done[entry[0]] = self.run(entry)
        return self.done[name]

    def tie(self, *arrays, count=0, pool=()):
        taken = []
        for entry in self.waiting[:count]:
            result = self.run(entry)
            self.done[entry[0]] = result
            taken.append((entry[0], result))
        self.waiting = self.waiting[count:]
        coming = self.waiting[:2]
        held = [[item for item in entry[2] if not isinstance(item, str)] for entry in coming]
        arrays, made, held, pooled = lax.optimization_barrier(
            (arrays, [r for _, r in taken], held, [self.pool[name] for name in pool])
        )
        self.pool.update(zip(pool, pooled))
        for (name, _), result in zip(taken, made):
            self.done[name] = result
        for entry, kept in zip(coming, held):
            kept = list(kept)
            entry[2] = [item if isinstance(item, str) else kept.pop(0) for item in entry[2]]
        return arrays


class Line:
    def __init__(self, work):
        self.work = work
        index = lax.axis_index("seq")
        self.place, self.side = index // 2, index % 2
        at_low, at_high = self.place == 0, self.place == 3
        self.at_end = at_low | at_high
        self.at_low = at_low
        place = self.place
        self.order = [
            place,
            jnp.where(at_low, 1, place - 1),
            jnp.where(at_low, 2, jnp.where(at_high, 1, place + 1)),
            jnp.where(place < 2, 3, 0),
        ]

    @staticmethod
    def along(block, moves):
        route = [(2 * i + k, 2 * j + k) for i, j in moves for k in range(2)]
        return lax.ppermute(block, "seq", route)

    @staticmethod
    def across(block):
        return lax.ppermute(block, "seq", [(i, i ^ 1) for i in range(8)])

    def as_pair(self, own, other):
        first = jnp.where(self.side == 0, own, other)
        second = jnp.where(self.side == 0, other, own)
        return jnp.concatenate([first, second], axis=0)

    def gather(self, block, use, later=None, counts=(0, 0, 0, 0), pools=((), (), (), ())):
        tie = self.work.tie
        later = later or (lambda at, used: ())
        up, down, side_0 = (
            self.along(block, [(0, 1), (1, 2), (2, 3)]),
            self.along(block, [(1, 0), (2, 1), (3, 2)]),
            self.across(block),
        )
        up, down, side_0 = tie(up, down, side_0, count=counts[0], pool=pools[0])
        near = jnp.where(self.at_low, down, up)
        up_2, down_2, side_1 = (
            self.along(up, [(1, 2), (2, 3)]),
            self.along(down, [(2, 1), (1, 0)]),
            self.across(near),
        )
        used_0 = use(0, self.as_pair(block, side_0))
        up_2, down_2, side_1, down, near, used_0 = tie(
            up_2, down_2, side_1, down, near, used_0, count=counts[1], pool=pools[1]
        )
        sent_0 = later(0, used_0)
        second = up_2 + down_2
        far = jnp.where(self.at_end, second, down)
        third, side_2 = self.along(second, [(2, 3), (1, 0)]), self.across(far)
        used_1 = use(1, self.as_pair(near, side_1))
        third, side_2, second, far, used_1, sent_0 = tie(
            third, side_2, second, far, used_1, sent_0, count=counts[2], pool=pools[2]
        )
        sent_1 = later(1, used_1)
        last = jnp.where(self.at_end, third, second)
        side_3 = self.across(last)
        used_2 = use(2, self.as_pair(far, side_2))
        side_3, last, used_2, sent_1 = tie(
            side_3, last, used_2, sent_1, count=counts[3], pool=pools[3]
        )
        sent_2 = later(2, used_2)
        used_3 = use(3, self.as_pair(last, side_3))
        return [used_0, used_1, used_2, used_3], [sent_0, sent_1, sent_2, later(3, used_3)]

    def halves(self, pair):
        rows = pair.shape[0] // 2
        own = lax.dynamic_slice_in_dim(pair, self.side * rows, rows, 0)
        other = lax.dynamic_slice_in_dim(pair, (1 - self.side) * rows, rows, 0)
        return own, other

    def scatter(self, term, counts=(0, 0, 0, 0)):
        tie = self.work.tie
        own_3, other_3 = self.halves(term(3))
        side_3 = self.across(other_3)
        own_2, other_2 = self.halves(term(2))
        side_3, other_2, own_2 = tie(side_3, other_2, own_2, count=counts[0])
        sum_3 = own_3.astype(F32) + side_3.astype(F32)
        step_1, side_2 = self.along(sum_3.astype(BF), [(0, 1), (3, 2)]), self.across(other_2)
        own_1, other_1 = self.halves(term(1))
        step_1, side_2, other_1, own_1 = tie(step_1, side_2, other_1, own_1, count=counts[1])
        sum_2 = own_2.astype(F32) + side_2.astype(F32)
        sent = jnp.where(self.at_end, sum_2, sum_3 + step_1.astype(F32)).astype(BF)
        up, down, side_1 = (
            self.along(sent, [(0, 1), (1, 2)]),
            self.along(sent, [(3, 2), (2, 1)]),
            self.across(other_1),
        )
        own_0, other_0 = self.halves(term(0))
        up, down, side_1, own_0, other_0 = tie(up, down, side_1, own_0, other_0, count=counts[2])
        sum_1 = own_1.astype(F32) + side_1.astype(F32)
        sent_up = jnp.where(self.at_low, sum_1, sum_2 + up.astype(F32)).astype(BF)
        sent_down = (sum_1 + down.astype(F32)).astype(BF)
        up, down, side_0 = (
            self.along(sent_up, [(0, 1), (1, 2), (2, 3)]),
            self.along(sent_down, [(1, 0), (2, 1), (3, 2)]),
            self.across(other_0),
        )
        if counts[3]:
            up, down, side_0 = tie(up, down, side_0, count=counts[3])
        return own_0.astype(F32) + side_0.astype(F32) + up.astype(F32) + down.astype(F32)


class Whole:
    def __init__(self, work):
        self.order = [jnp.int32(0)]

    def gather(self, block, use, later=None, counts=(), pools=()):
        used = use(0, gather_seq(block))
        return [used], [later(0, used) if later else ()]

    def scatter(self, term, counts=()):
        return scatter_seq(term(0)).astype(F32)


def gather_seq(block):
    return lax.all_gather(block, "seq", axis=0, tiled=True)


def scatter_seq(partial_rows):
    return lax.psum_scatter(partial_rows, "seq", scatter_dimension=0, tiled=True)


def to_core(block):
    return lax.ppermute(block, "fsdp", [(i, i ^ 1) for i in range(4)])


def to_chip(block):
    return lax.ppermute(block, "fsdp", [(i, i ^ 2) for i in range(4)])


def split_low(values):
    high = values.astype(BF)
    low = (values - high.astype(F32)).astype(BF)
    return high, low


def place_rows(whole, piece, start):
    return lax.dynamic_update_slice_in_dim(whole, piece, start, 0)


def per_device(
    layer_input,
    attn_gain,
    query_matrix,
    query_bias_vector,
    key_matrix,
    key_bias_vector,
    value_matrix,
    value_bias_vector,
    sink_logit_values,
    output_matrix,
    output_bias_vector,
    ffn_gain,
    router_weight,
    router_bias,
    expert_gate_up,
    expert_gate_up_bias,
    expert_down,
    expert_down_bias,
    route_ids,
    doc_lengths,
    out_cotangent,
):
    seq_count = lax.axis_size("seq")
    fsdp_count = lax.axis_size("fsdp")
    seq_index = lax.axis_index("seq")
    fsdp_index = lax.axis_index("fsdp")
    tokens_here, width = layer_input.shape[1:]
    choose_count = route_ids.shape[2]
    expert_count = seq_count
    length = seq_count * tokens_here
    block_capacity = max(2, tokens_here * choose_count * 5 // (4 * expert_count))
    capacity = block_capacity * seq_count
    padded = -(-(width + 3 * expert_count) // 128) * 128
    heads_here = QUERY_HEADS // seq_count
    shared_kv = seq_count > KEY_VALUE_HEADS
    q_width = heads_here * HEAD_DIM
    q_part, kv_part = query_matrix.shape[1], key_matrix.shape[1]
    work = Work()
    line = Line(work) if seq_count == 8 else Whole(work)
    chunk = length // len(line.order)
    starts = [place * chunk for place in line.order]
    last = len(starts) - 1

    def taken(rows, start):
        return lax.dynamic_slice_in_dim(rows, start, chunk, 0)

    member_here = jnp.any(
        route_ids[0][:, :, None] == jnp.arange(expert_count, dtype=jnp.int32), axis=1
    )
    cot_here = out_cotangent[0]
    ranks = jnp.cumsum(member_here.astype(jnp.int32), axis=0)
    slot_here = jnp.where(member_here, ranks, 0).astype(BF)

    part = attn_gain.shape[0]
    near_first = [fsdp_index ^ turn for turn in range(fsdp_count)]

    def from_all(piece):
        core, chip = to_core(piece), to_chip(piece)
        return [piece, core, chip, to_core(chip)]

    def in_order(pieces):
        core_bit, chip_bit = fsdp_index % 2 == 0, fsdp_index < 2
        pairs = []
        for own, other in ((pieces[0], pieces[1]), (pieces[2], pieces[3])):
            pairs.append((jnp.where(core_bit, own, other), jnp.where(core_bit, other, own)))
        first = [jnp.where(chip_bit, a, b) for a, b in zip(*pairs)]
        second = [jnp.where(chip_bit, b, a) for a, b in zip(*pairs)]
        return first + second

    kv_head = seq_index // max(1, seq_count // KEY_VALUE_HEADS)

    def parameters(
        attn_gain,
        ffn_gain,
        output_bias_vector,
        sink_logit_values,
        router_bias,
        query_bias_vector,
        key_bias_vector,
        value_bias_vector,
        expert_down_bias,
        router_weight,
        query_matrix,
        output_matrix,
        key_matrix,
        value_matrix,
    ):
        tiny = jnp.concatenate(
            [sink_logit_values, router_bias, query_bias_vector, key_bias_vector, value_bias_vector]
        )
        tiny = jnp.concatenate([tiny, jnp.zeros((part - tiny.shape[0],), BF)])
        small = jnp.concatenate(
            [
                attn_gain[None],
                ffn_gain[None],
                output_bias_vector[None],
                tiny[None],
                expert_down_bias,
                router_weight.T,
            ],
            axis=0,
        )
        small_all = jnp.stack(in_order(from_all(small)))
        wide = jnp.swapaxes(small_all, 0, 1).reshape(small.shape[0], width).astype(F32)
        attn_gain_f, ffn_gain_f, out_bias_f = wide[0], wide[1], wide[2]
        down_bias_f = wide[4 : 4 + expert_count]
        router_t = wide[4 + expert_count :].astype(BF)
        tiny_all = small_all[:, 3]
        places = [0]
        for piece in (sink_logit_values, router_bias, query_bias_vector, key_bias_vector, value_bias_vector):
            places.append(places[-1] + piece.shape[0])
        sinks_f, router_bias_f, q_bias, k_bias, v_bias = (
            tiny_all[:, a:b].astype(F32) for a, b in zip(places[:-1], places[1:])
        )
        sinks_f, router_bias_f = sinks_f.reshape(-1), router_bias_f.reshape(-1)
        k_bias, v_bias = k_bias.reshape(-1), v_bias.reshape(-1)
        q_bias = jnp.concatenate(
            [lax.dynamic_slice_in_dim(q_bias, at, 1, 0)[0] for at in near_first]
        )
        pieces = from_all(jnp.concatenate([query_matrix, output_matrix.T], axis=0))
        w_query = jnp.concatenate([piece[:width] for piece in pieces], axis=1)
        wo_t = jnp.concatenate([piece[width:] for piece in pieces], axis=1)
        if shared_kv:

            def own_head(piece):
                whole = lax.all_gather(piece, ("seq", "fsdp"), axis=0, tiled=True)
                return lax.dynamic_slice_in_dim(whole, kv_head * HEAD_DIM, HEAD_DIM, 0)

            w_pair = jnp.concatenate([own_head(key_matrix.T), own_head(value_matrix.T)], axis=0)
            k_bias = own_head(key_bias_vector).astype(F32)
            v_bias = own_head(value_bias_vector).astype(F32)
        else:
            kv_pieces = in_order(from_all(jnp.concatenate([key_matrix.T, value_matrix.T], axis=0)))
            w_pair = jnp.concatenate(
                [piece[:kv_part] for piece in kv_pieces] + [piece[kv_part:] for piece in kv_pieces],
                axis=0,
            )
        lin_bias = jnp.concatenate([q_bias, k_bias, v_bias])
        return (
            attn_gain_f,
            ffn_gain_f,
            out_bias_f,
            down_bias_f,
            router_t,
            sinks_f,
            router_bias_f,
            w_query,
            wo_t,
            w_pair,
            lin_bias,
        )

    work.add(
        "parameters",
        parameters,
        attn_gain,
        ffn_gain,
        output_bias_vector,
        sink_logit_values,
        router_bias,
        query_bias_vector,
        key_bias_vector,
        value_bias_vector,
        expert_down_bias,
        router_weight,
        query_matrix,
        output_matrix,
        key_matrix,
        value_matrix,
    )

    columns = jnp.concatenate(
        [
            (seq_index * fsdp_count + at) * q_part + jnp.arange(q_part, dtype=jnp.int32)
            for at in near_first
        ]
    )
    whole_heads = q_part % HEAD_DIM == 0

    cosine_table, sine_table = rope_tables(length)
    doc_row = lax.dynamic_slice_in_dim(doc_lengths, fsdp_index, 1, 0)[0]
    doc_ends = jnp.cumsum(doc_row)

    def project(pair):
        pair_f = pair.astype(F32)
        normed = (pair_f * rms_scale(pair_f) * attn_gain_f).astype(BF)
        query_part = dot(normed, w_query, 1, 0) + lin_bias[:q_width]
        return normed, query_part, dot(normed, w_pair, 1, 1) + lin_bias[q_width:]

    pairs = []

    def arrive(at, pair):
        pairs.append(pair)
        return pair

    line.gather(layer_input[0], lambda at, pair: (work.take("parameters"), arrive(at, pair))[1])
    (
        attn_gain_f,
        ffn_gain_f,
        out_bias_f,
        down_bias_f,
        router_t,
        sinks_f,
        router_bias_f,
        w_query,
        wo_t,
        w_pair,
        lin_bias,
    ) = work.take("parameters")
    projected = [project(pair) for pair in pairs]
    normed_rows = jnp.zeros((length, width), BF)
    lin = jnp.zeros((length, q_width + 2 * HEAD_DIM), F32)
    for start, (normed, query_part, pair_part) in zip(starts, projected):
        normed_rows = place_rows(normed_rows, normed, start)
        lin = lax.dynamic_update_slice(lin, query_part, (start, 0))
        lin = lax.dynamic_update_slice(lin, pair_part, (start, q_width))
    if not whole_heads:
        order = jnp.argsort(columns)
        w_query = w_query[:, order]
        wo_t = wo_t[:, order]
        lin = jnp.concatenate([lin[:, :q_width][:, order], lin[:, q_width:]], axis=1)
        head_numbers = seq_index * heads_here + jnp.arange(heads_here, dtype=jnp.int32)
    else:
        head_numbers = columns[::HEAD_DIM] // HEAD_DIM
    head_lane = (head_numbers[:, None] == jnp.arange(QUERY_HEADS)[None, :]).astype(F32)
    sinks_here = jnp.sum(head_lane * sinks_f[None, :], axis=1)
    turned, heads = attend(lin, cosine_table, sine_table, doc_ends, sinks_here)
    attn_sum = line.scatter(
        lambda at: dot(taken(heads, starts[at]), wo_t, 1, 1).astype(BF), counts=(0, 0, 0, 0)
    )

    resid_in = layer_input[0].astype(F32)
    resid_mid = resid_in + attn_sum + out_bias_f
    norm_two = rms_scale(resid_mid)
    unit_mid = resid_mid * norm_two
    normed_mid = (unit_mid * ffn_gain_f).astype(BF)
    logits = dot(normed_mid, router_t, 1, 1) + router_bias_f
    gates = jax.nn.softmax(jnp.where(member_here, logits, -1e30), axis=-1)
    gates = jnp.where(member_here, gates, 0.0)
    gate_high, gate_low = split_low(gates)
    mid_packed = jnp.concatenate(
        [
            normed_mid,
            slot_here,
            gate_high,
            gate_low,
            jnp.zeros((tokens_here, padded - width - 3 * expert_count), BF),
        ],
        axis=1,
    )

    expert_lane = (jnp.arange(expert_count, dtype=jnp.int32) == seq_index).astype(F32)
    slots = block_capacity * (chunk // tokens_here)
    slot_number = jnp.arange(block_capacity, dtype=F32) + 1.0
    selects = {}

    def pick_rows(at, pair):
        rank = jnp.sum(pair[:, width : width + expert_count].astype(F32) * expert_lane, axis=1)
        blocks = chunk // tokens_here
        hit = slot_number[None, :, None] == rank.reshape(blocks, 1, tokens_here)
        same = jnp.eye(blocks, dtype=jnp.bool_)[:, None, :, None]
        select = (hit[:, :, None, :] & same).reshape(slots, chunk).astype(BF)
        return select, dot(select, pair, 1, 0).astype(BF)

    def send_rows(at, used):
        return to_core(used[1]), to_chip(used[1])

    picked, sent = line.gather(mid_packed, pick_rows, send_rows)
    selects = [select for select, _ in picked]
    own_rows = [rows for _, rows in picked]
    core_rows = [core for core, _ in sent]
    chip_rows = [chip for _, chip in sent]
    spare = padded - width
    units_w = jnp.pad(jnp.swapaxes(expert_gate_up[0], 1, 2), ((0, 0), (0, 0), (0, spare)))
    down_w = jnp.pad(expert_down[0], ((0, 0), (0, spare)))
    units_b = expert_gate_up_bias[0].astype(F32)[:, None, :]

    def joined(pieces):
        whole = jnp.zeros((2 * capacity, pieces[0].shape[1]), BF)
        first = 0
        for piece in pieces:
            whole = place_rows(whole, piece, first)
            first += piece.shape[0]
        return whole

    def einsum(form, left, right):
        return jnp.einsum(form, left, right, preferred_element_type=F32)

    def hidden_step(rows):
        tail = rows[:, width + expert_count :].astype(F32)
        share = jnp.sum(
            (tail[:, :expert_count] + tail[:, expert_count : 2 * expert_count]) * expert_lane,
            axis=1,
            keepdims=True,
        )
        before = einsum("rd,khd->krh", rows, units_w) + units_b
        hidden = swiglu(before[0], before[1]).astype(BF)
        return share, before, hidden, (hidden.astype(F32) * share).astype(BF)

    def mix_step(made):
        return dot(made[3], down_w, 1, 0).astype(BF)

    def back_step(made, cot):
        share, before, hidden, _ = made
        grad_hidden = dot(cot, down_w, 1, 1)
        score = jnp.sum(hidden.astype(F32) * grad_hidden, axis=1, keepdims=True)
        _, glu_back = jax.vjp(swiglu, before[0], before[1])
        grad_gate_pre, grad_up_pre = glu_back(grad_hidden * share)
        return score, jnp.stack([grad_gate_pre.astype(BF), grad_up_pre.astype(BF)])

    def row_step(made):
        return einsum("krh,khd->rd", made[1], units_w).astype(BF)

    cot_block = jnp.concatenate([cot_here, jnp.zeros((tokens_here, spare), BF)], axis=1)
    cot_block, own_rows = work.tie(cot_block, own_rows)
    cot_rows = gather_seq(cot_block)
    near = joined(own_rows + core_rows)
    made_n = hidden_step(near)
    made_n, chip_rows = work.tie(made_n, chip_rows)
    far = joined(chip_rows + [to_core(chip) for chip in chip_rows])
    mix_n = mix_step(made_n)
    made_o = hidden_step(far)
    mix_o = mix_step(made_o)
    mix_core_n = to_core(mix_n[capacity:])
    mix_core_o = to_core(mix_o[capacity:])
    cot_rows, made_o, mix_n, mix_o, mix_core_n = work.tie(
        cot_rows, made_o, mix_n, mix_o, mix_core_n
    )
    cot_own = [dot(select, taken(cot_rows, at), 1, 0).astype(BF) for select, at in zip(selects, starts)]
    half = (len(cot_own) + 1) // 2
    cot_own = [jnp.concatenate(cot_own[:half])] + (
        [jnp.concatenate(cot_own[half:])] if cot_own[half:] else []
    )
    cot_chip = [to_chip(rows) for rows in cot_own]
    cot_near = joined(cot_own + [to_core(rows) for rows in cot_own])

    def core_sum(part, from_core):
        return (part[:capacity].astype(F32) + from_core.astype(F32)).astype(part.dtype)

    def total(near_part, from_core, arrived, at):
        return (
            slot_rows(near_part, at).astype(F32)
            + slot_rows(from_core, at).astype(F32)
            + arrived.astype(F32)
        )

    def slot_rows(rows, at):
        return rows[at * slots : (at + 1) * slots]

    def from_chip(far_sum):
        return [to_chip(slot_rows(far_sum, at)) for at in reversed(range(len(starts)))][::-1]

    def score_step(back_n, back_o):
        scores = jnp.concatenate([back_n[0], back_o[0]], axis=1)
        return scores[:capacity] + to_core(scores[capacity:])

    back_n = back_step(made_n, cot_near)
    row_n = row_step(back_n)
    back_n, row_n, cot_chip = work.tie(back_n, row_n, cot_chip)
    row_near_core = to_core(row_n[capacity:])
    cot_far = joined(cot_chip + [to_core(rows) for rows in cot_chip])
    back_o = back_step(made_o, cot_far)
    back_n, back_o, row_near_core = work.tie(back_n, back_o, row_near_core)
    score = score_step(back_n, back_o)
    score = score[:, :1] + to_chip(score[:, 1:])
    row_o = row_step(back_o)
    row_o, score = work.tie(row_o, score)
    (score_n, low_n), (score_o, low_o) = back_n, back_o
    row_far_core = to_core(row_o[capacity:])

    def units_step(low_n, rows_n, low_o, rows_o):
        return einsum("krh,rd->khd", low_n, rows_n[:, :width]) + einsum(
            "krh,rd->khd", low_o, rows_o[:, :width]
        )

    def down_step(hidden_n, cot_n, hidden_o, cot_o):
        return dot(hidden_n, cot_n[:, :width], 0, 0) + dot(hidden_o, cot_o[:, :width], 0, 0)

    work.add("units", units_step, low_n, near, low_o, far)
    work.add("down", down_step, made_n[3], cot_near, made_o[3], cot_far)
    (row_far_core,) = work.tie(row_far_core)
    arrivals = from_chip(core_sum(row_o, row_far_core))

    def back_term(at):
        row_sum = total(row_n, row_near_core, arrivals[at], at)
        grad_high, grad_low = split_low(slot_rows(score, at) * expert_lane)
        back_packed = jnp.concatenate(
            [
                row_sum[:, :width].astype(BF),
                grad_high,
                grad_low,
                jnp.zeros((slots, padded - width - 2 * expert_count), BF),
            ],
            axis=1,
        )
        return dot(selects[at], back_packed, 0, 0).astype(BF)

    back = line.scatter(back_term, counts=(1, 0, 0, 0))

    mix_far = core_sum(mix_o, mix_core_o)
    mix_far, arrivals_end = lax.optimization_barrier((mix_far, arrivals[0][:8]))
    mix_chip = to_chip(mix_far)

    def mix_place(mix_chip):
        whole = jnp.zeros((length, width), BF)
        for at, start in enumerate(starts):
            mix_sum = total(mix_n, mix_core_n, slot_rows(mix_chip, at), at)
            term = dot(selects[at], mix_sum[:, :width].astype(BF), 0, 0).astype(BF)
            whole = place_rows(whole, term, start)
        return whole

    cot_f = cot_here.astype(F32)
    grad_gates = (
        back[:, width : width + expert_count]
        + back[:, width + expert_count : width + 2 * expert_count]
        + dot(cot_f, down_bias_f, 1, 1, EXACT)
    )
    mean_gate = jnp.sum(gates * grad_gates, axis=-1, keepdims=True)
    grad_logits = gates * (grad_gates - mean_gate)
    router_grad_t = dot(grad_logits, normed_mid.astype(F32), 0, 0, EXACT)
    router_bias_grad = jnp.sum(grad_logits, axis=0)
    down_bias_grad = dot(gates, cot_f, 0, 0, EXACT)
    grad_normed_mid = back[:, :width] + dot(grad_logits, router_t.astype(F32), 1, 0, EXACT)
    ffn_gain_grad = jnp.sum(grad_normed_mid * unit_mid, axis=0)
    grad_unit_mid = grad_normed_mid * ffn_gain_f
    grad_mid = (
        norm_two
        * (grad_unit_mid - unit_mid * jnp.mean(grad_unit_mid * unit_mid, axis=-1, keepdims=True))
        + cot_f
    )
    grad_attn = grad_mid.astype(BF)
    out_bias_grad = jnp.sum(grad_attn.astype(F32), axis=0)

    def to_core_owners(blocks, kind=BF):
        both = to_core(jnp.stack([blocks[1], blocks[3]]).astype(kind))
        return blocks[0] + both[0].astype(F32), (blocks[2] + both[1].astype(F32)).astype(kind)

    def to_owners(sums):
        own, chip = sums
        return own + to_chip(chip).astype(F32)

    def seq_sum(values):
        step = 1
        while step < seq_count:
            values = values + lax.ppermute(values, "seq", [(i, i ^ step) for i in range(seq_count)])
            step *= 2
        return values

    def small_step(rows):
        blocks = [lax.dynamic_slice_in_dim(rows, at * part, part, 1) for at in near_first]
        return to_core_owners(blocks, F32)

    tiny_grad = jnp.zeros((fsdp_count, part), F32)
    tiny_grad = lax.dynamic_update_slice(
        tiny_grad, router_bias_grad.reshape(fsdp_count, -1), (0, 0)
    ).reshape(1, width)
    small_grad = jnp.concatenate(
        [out_bias_grad[None], ffn_gain_grad[None], tiny_grad, down_bias_grad, router_grad_t],
        axis=0,
    )

    attn_rows = jnp.zeros((length, width), BF)
    grad_heads = jnp.zeros((length, q_width), BF)

    def head_grads(at, pair):
        return pair, dot(pair, wo_t, 1, 0).astype(BF)

    work.take("units")
    grads, _ = line.gather(grad_attn, head_grads, counts=(1, 0, 0, 0))
    mixture = scatter_seq(mix_place(mix_chip)).astype(F32)
    mixture = mixture + dot(gates, down_bias_f, 1, 0, EXACT)
    layer_output = (resid_mid + mixture).astype(BF)[None]
    for start, (pair, grad_part) in zip(starts, grads):
        attn_rows = place_rows(attn_rows, pair, start)
        grad_heads = place_rows(grad_heads, grad_part, start)

    lin_grad, lin_sums, sink_here_grad = attend_back(
        turned, cosine_table, sine_table, doc_ends, sinks_here, grad_heads
    )

    order = None if whole_heads else jnp.argsort(columns)
    back_order = None if whole_heads else jnp.argsort(order)

    def column_blocks(whole):
        if back_order is not None:
            whole = whole[:, back_order]
        return [whole[:, at * q_part : (at + 1) * q_part] for at in range(fsdp_count)]

    def query_step(rows, grads):
        return dot(rows, grads[:, :q_width], 0, 0)

    def pair_step(rows, grads):
        return dot(grads[:, q_width:], rows, 0, 0)

    sink_all_grad = jnp.sum(head_lane * sink_here_grad[:, None], axis=0)

    def row_blocks(query_w_part, pair_w_part):
        attn_gain_grad = (
            jnp.sum(query_w_part * w_query.astype(F32), axis=1)
            + jnp.sum(pair_w_part * w_pair.astype(F32), axis=0)
        ) / attn_gain_f
        query_sums = lin_sums[:q_width]
        if back_order is not None:
            query_sums = query_sums[back_order]
        pair_sums = lin_sums[q_width:]
        blocks = []
        for turn, at in enumerate(near_first):
            gain = lax.dynamic_slice_in_dim(attn_gain_grad, at * part, part, 0)
            row = [gain, sink_all_grad, query_sums[turn * q_part : (turn + 1) * q_part]]
            block = []
            if not shared_kv:
                for first in (0, HEAD_DIM):
                    row.append(lax.dynamic_slice_in_dim(pair_sums, first + at * kv_part, kv_part, 0))
                    block.append(
                        lax.dynamic_slice_in_dim(pair_w_part, first + at * kv_part, kv_part, 0)
                    )
            row = jnp.concatenate(row)
            row = jnp.concatenate([row, jnp.zeros((width - row.shape[0],), F32)])
            block.append(jnp.broadcast_to(row[None], (16, width)))
            blocks.append(jnp.concatenate(block, axis=0))
        return to_core_owners(blocks)

    work.add("query_w", query_step, normed_rows, lin_grad)
    work.add("out_w", lambda a, b: dot(a, b, 0, 0), attn_rows, heads)
    work.add("pair_w", pair_step, normed_rows, lin_grad)
    work.add("query_core", lambda whole: to_core_owners(column_blocks(whole)), "query_w")
    work.add("out_core", lambda whole: to_core_owners(column_blocks(whole)), "out_w")
    work.add("small_core", small_step, small_grad)
    work.add("row_core", row_blocks, "query_w", "pair_w")
    work.add("small_chip", to_owners, "small_core")
    work.add("row_chip", to_owners, "row_core")
    work.add("query_chip", to_owners, "query_core")

    def input_term(at):
        grad_part = taken(lin_grad, starts[at])
        return (
            dot(grad_part[:, :q_width], w_query, 1, 1) + dot(grad_part[:, q_width:], w_pair, 1, 0)
        ).astype(BF)

    grad_normed_in = line.scatter(input_term, counts=(1, 2, 4, 3))
    query_w_own = work.take("query_chip")
    out_w_own = to_owners(work.take("out_core")).T
    owned, small_own = work.take("row_chip"), seq_sum(work.take("small_chip"))
    down_grad = work.take("down")
    gate_up_grad = jnp.swapaxes(work.take("units"), 1, 2)
    gate_up_bias_grad = jnp.sum(low_n.astype(F32), axis=1) + jnp.sum(low_o.astype(F32), axis=1)

    resid_scale = rms_scale(resid_in)
    unit_in = resid_in * resid_scale
    grad_unit_in = grad_normed_in * attn_gain_f
    input_grad = (
        resid_scale
        * (grad_unit_in - unit_in * jnp.mean(grad_unit_in * unit_in, axis=-1, keepdims=True))
        + grad_mid
    )

    owned_row = owned[-1]
    gain_own = seq_sum(owned_row[None, : part + QUERY_HEADS])[0]
    sink_own = lax.dynamic_slice_in_dim(
        gain_own[part:], fsdp_index * sink_logit_values.shape[0], sink_logit_values.shape[0], 0
    )
    at = part + QUERY_HEADS
    query_b_own = owned_row[at : at + q_part]
    if shared_kv:

        def whole_sum(part_grad):
            whole = jnp.zeros((KEY_VALUE_HEADS * HEAD_DIM,) + part_grad.shape[1:], F32)
            whole = lax.dynamic_update_slice_in_dim(whole, part_grad, kv_head * HEAD_DIM, 0)
            return lax.psum_scatter(whole, ("seq", "fsdp"), scatter_dimension=0, tiled=True)

        pair_w_part = work.take("pair_w")
        key_w_own = whole_sum(pair_w_part[:HEAD_DIM]).T
        value_w_own = whole_sum(pair_w_part[HEAD_DIM:]).T
        key_b_own = whole_sum(lin_sums[q_width : q_width + HEAD_DIM])
        value_b_own = whole_sum(lin_sums[q_width + HEAD_DIM :])
    else:
        key_w_own, value_w_own = owned[:kv_part].T, owned[kv_part : 2 * kv_part].T
        at = at + q_part
        key_b_own, value_b_own = owned_row[at : at + kv_part], owned_row[at + kv_part : at + 2 * kv_part]

    return (
        layer_output,
        input_grad[None],
        gain_own[:part],
        query_w_own,
        query_b_own,
        key_w_own,
        key_b_own,
        value_w_own,
        value_b_own,
        sink_own,
        out_w_own,
        small_own[0],
        small_own[1],
        small_own[3 + expert_count :].T,
        lax.dynamic_slice_in_dim(small_own[2], 0, router_bias.shape[0], 0),
        gate_up_grad[None],
        gate_up_bias_grad[None],
        down_grad[None],
        small_own[3 : 3 + expert_count],
    )


def solution(mesh):
    return jax.shard_map(
        per_device,
        mesh=mesh,
        in_specs=(
            P("fsdp", "seq", None),
            P("fsdp"),
            P(None, ("seq", "fsdp")),
            P(("seq", "fsdp")),
            P(None, ("seq", "fsdp")),
            P(("seq", "fsdp")),
            P(None, ("seq", "fsdp")),
            P(("seq", "fsdp")),
            P("fsdp"),
            P(("seq", "fsdp"), None),
            P("fsdp"),
            P("fsdp"),
            P("fsdp", None),
            P("fsdp"),
            P("seq", None, None, "fsdp"),
            P("seq", None, "fsdp"),
            P("seq", "fsdp", None),
            P(None, "fsdp"),
            P("fsdp", "seq", None),
            P(),
            P("fsdp", "seq", None),
        ),
        out_specs=(
            P("fsdp", "seq", None),
            P("fsdp", "seq", None),
            P("fsdp"),
            P(None, ("seq", "fsdp")),
            P(("seq", "fsdp")),
            P(None, ("seq", "fsdp")),
            P(("seq", "fsdp")),
            P(None, ("seq", "fsdp")),
            P(("seq", "fsdp")),
            P("fsdp"),
            P(("seq", "fsdp"), None),
            P("fsdp"),
            P("fsdp"),
            P("fsdp", None),
            P("fsdp"),
            P("seq", None, None, "fsdp"),
            P("seq", None, "fsdp"),
            P("seq", "fsdp", None),
            P(None, "fsdp"),
        ),
        check_vma=False,
    )
```

time: 1300 us -> 1100 us (0.85)
  matrix products: 365 us -> 256 us
  waiting for transfers between devices: 433 us -> 362 us
  blocking collectives: 66 us -> 0 us
  Pallas kernels: 0 us -> 30.2 us
  starting transfers between devices: 120 us -> 136 us
    dot_general x64 -> x55, matrix products: 348 us -> 158 us  [dot(): lax.dot_general(left, right, (((left_dim,), (right_dim,)), ((), ())), pre...]
    dot_general x6, matrix products: 17.1 us -> 97.9 us  [einsum(): return jnp.einsum(form, left, right, preferred_element_type=F32)]
    psum x1 -> x0, blocking collectives: 43.5 us -> none  [per_device(): attn_gain_sum = lax.psum(attn_gain_grad, ('seq', 'fsdp'))]
    reduce_scatter x4 -> x0, waiting for transfers between devices: 31.4 us -> none  [scatter_fsdp(): lax.psum_scatter(partial_rows, 'fsdp', scatter_dimension=0, tiled=True)]
    dynamic_update_slice x0 -> x30, local copies, waits for them, and re-layouts: none -> 31.1 us  [the longest x29 31.1 us: place_rows(): return lax.dynamic_update_slice_in_dim(whole, piece, start, 0)]
    pallas_call x0 -> x2, Pallas kernels: none -> 30.2 us  [the longest x1 15.5 us: attend_back(): pl.pallas_call(attend_back_kernel, grid=(length // rows,), in_specs=[smem...]
    ppermute x17 -> x19, waiting for transfers between devices: 145 us -> 121 us  [to_chip(): return lax.ppermute(block, 'fsdp', [(i, i ^ 2) for i in range(4)])]
    ppermute x24, waiting for transfers between devices: 104 us -> 82.8 us  [across(): return lax.ppermute(block, 'seq', [(i, i ^ 1) for i in range(8)])]
  transfers between devices with their start and end apart: 96 -> 108, of which waited for: 35 -> 43; matrix products, arithmetic and copies ran while one was open for 47% -> 45% of each run, Pallas kernels for 0% -> 0%
where the time goes in v3:
time: 1100 us
  waiting for transfers between devices  362 us (33%)
  matrix products  256 us (23%)
  local copies, waits for them, and re-layouts  170 us (15%)
  starting transfers between devices  136 us (12%)
  other arithmetic  122 us (11%)
  Pallas kernels  30.2 us (3%)
  between operations  17.8 us (2%)
    dot_general x55, matrix products, dot(): lax.dot_general(left, right, (((left_dim,), (right_dim,)), ((), ())), pre...  158 us
    ppermute x30, waiting for transfers between devices, along(): return lax.ppermute(block, 'seq', route)  146 us
    ppermute x19, waiting for transfers between devices, to_chip(): return lax.ppermute(block, 'fsdp', [(i, i ^ 2) for i in range(4)])  121 us
    dot_general x6, matrix products, einsum(): return jnp.einsum(form, left, right, preferred_element_type=F32)  97.9 us
    ppermute x24, waiting for transfers between devices, across(): return lax.ppermute(block, 'seq', [(i, i ^ 1) for i in range(8)])  82.8 us
    ppermute x30, starting transfers between devices, along(): return lax.ppermute(block, 'seq', route)  72.3 us
    dynamic_update_slice x29, local copies, waits for them, and re-layouts, place_rows(): return lax.dynamic_update_slice_in_dim(whole, piece, start, 0)  31.1 us
    ppermute x24, starting transfers between devices, across(): return lax.ppermute(block, 'seq', [(i, i ^ 1) for i in range(8)])  30.5 us
  transfers between devices with their start and end apart: 108, of which 43 were waited for; matrix products, arithmetic and copies ran while one was open for 45% of the time, Pallas kernels for 0%

profile of v3, /device:TPU:0, one launch (start us, length us, event | category | flops | bytes accessed | tf_op | source)
XLA Modules:
  0.0 1095.4 jit_solution(11240872762030332783)
XLA Ops:
  19.8 8.5 collective-permute-done
  54.8 28.6 %collective-permute-done.10 = bf16[32,2880]{1,0:T(8,128)(2,1)S(1)} collective-permute-done((bf16[32,2880]{1,0:T(8,128)(2,1)S(1)}, bf16[32,2880]{1,0:T(8,128)(2,1)S(1)}, u32[]{:S(2)}, u32[]{:S(2)}) %collective-permute-start.10) | collective-permute-done | bytes 184352 | tf_op jit(solution)/shard_map/ppermute | solution.py:427
  112.5 15.1 %collective-permute-done.15 = bf16[128,2880]{0,1:T(8,128)(2,1)S(1)} collective-permute-done((bf16[128,2880]{0,1:T(8,128)(2,1)S(1)}, bf16[128,2880]{0,1:T(8,128)(2,1)S(1)}, u32[]{:S(2)}, u32[]{:S(2)}) %collective-permute-start.15) | collective-permute-done | bytes 737312 | tf_op jit(solution)/shard_map/ppermute | solution.py:315
  135.1 9.9 collective-permute-done.17
  161.5 14.7 %shard_map.348 = (bf16[1024,640]{1,0:T(8,128)(2,1)}, bf16[1024,512]{1,0:T(8,128)(2,1)}) custom-call(s32[3]{0:T(128)} %bitcast.451, f32[8]{0:T(128)} %select_reduce_fusion.1.sinks_ref, f32[1024,640]{1,0:T(8,128)} %copy-done.6, f32[1024,640]{1,0:T(8,128)} %copy-done.6, f32[1024,128]{1,0:T(8,128)} %get-tuple-element.654.cos_ref.cos_before_ref, ...), custom_call_target="tpu_custom_call" | custom-call | flops 671088640 | bytes 6553600 | tf_op jit(solution)/shard_map/pallas_call | solution.py:122
  184.1 12.3 %collective-permute-done.18 = bf16[128,2880]{0,1:T(8,128)(2,1)S(1)} collective-permute-done((bf16[128,2880]{0,1:T(8,128)(2,1)}, bf16[128,2880]{0,1:T(8,128)(2,1)S(1)}, u32[]{:S(2)}, u32[]{:S(2)}) %collective-permute-start.18) | collective-permute-done | bytes 737312 | tf_op jit(solution)/shard_map/ppermute | solution.py:319
  288.4 9.5 collective-permute-done.31
  302.5 17.8 %collective-permute-done.33 = bf16[128,2944]{0,1:T(8,128)(2,1)S(1)} collective-permute-done((bf16[128,2944]{0,1:T(8,128)(2,1)S(1)}, bf16[128,2944]{0,1:T(8,128)(2,1)S(1)}, u32[]{:S(2)}, u32[]{:S(2)}) %collective-permute-start.33) | collective-permute-done | bytes 753696 | tf_op jit(solution)/shard_map/ppermute | solution.py:315
  327.1 14.9 %collective-permute-done.37 = bf16[128,2944]{0,1:T(8,128)(2,1)S(1)} collective-permute-done((bf16[128,2944]{0,1:T(8,128)(2,1)S(1)}, bf16[128,2944]{0,1:T(8,128)(2,1)S(1)}, u32[]{:S(2)}, u32[]{:S(2)}) %collective-permute-start.37) | collective-permute-done | bytes 753696 | tf_op jit(solution)/shard_map/ppermute | solution.py:319
  356.7 16.4 %add_bitcast_fusion.1 = f32[2,1280,720]{1,2,0:T(8,128)S(1)} fusion(bf16[1280,2944]{1,0:T(8,128)(2,1)S(1)} %constant_dynamic-update-slice_fusion.23, bf16[2,720,2880]{2,1,0:T(8,128)(2,1)} %bitcast.453, f32[2,720]{1,0:T(2,128)S(1)} %copy-done.160), kind=kOutput, calls=%fused_computation.31 | convolution fusion | flops 10854604800 | bytes 23209600 | tf_op jit(solution)/shard_map/rd,khd->krh/dot_general | solution.py:727
  377.9 10.5 collective-permute-done.43
  390.1 8.8 convolution_convert_fusion.1
  407.5 16.1 %add_bitcast_fusion = f32[2,1280,720]{1,2,0:T(8,128)S(1)} fusion(bf16[1280,2944]{1,0:T(8,128)(2,1)S(1)} %constant_dynamic-update-slice_fusion.16, bf16[2,720,2880]{2,1,0:T(8,128)(2,1)} %bitcast.454, f32[2,720]{1,0:T(2,128)S(1)} %copy-done.160), kind=kOutput, calls=%fused_computation.30 | convolution fusion | flops 10854604800 | bytes 23209600 | tf_op jit(solution)/shard_map/rd,khd->krh/dot_general | solution.py:727
  428.4 9.5 convolution_convert_fusion
  480.3 18.2 %fusion.108 = (bf16[1,1280,720]{1,2,0:T(8,128)(2,1)S(1)}, bf16[1,1280,720]{1,2,0:T(8,128)(2,1)S(1)}, f32[1280]{0:T(1024)S(1)}) fusion(f32[1280]{0:T(1024)S(1)} %reduce.3, f32[2,1280,720]{1,2,0:T(8,128)} %copy-done.22, bf16[1280,720]{0,1:T(8,128)(2,1)S(1)} %copy-done.81, bf16[1280,2944]{1,0:T(8,128)(2,1)} %constant_dynamic-update-slice_fusion.13, ...), kind=kOutput, calls=%fused_computation.200 | convolution fusion | flops 5467851776 | bytes 24596480 | tf_op jit(solution)/shard_map/dot_general | solution.py:25
  500.7 14.6 %bitcast_convert_fusion.1 = bf16[1280,2944]{1,0:T(8,128)(2,1)} fusion(bf16[2,720,2880]{2,1,0:T(8,128)(2,1)S(1)} %bitcast.458, bf16[1,1280,720]{1,2,0:T(8,128)(2,1)S(1)} %get-tuple-element.476, bf16[1,1280,720]{1,2,0:T(8,128)(2,1)S(1)} %get-tuple-element.475), kind=kOutput, calls=%fused_computation.1 | convolution fusion | flops 10858373120 | bytes 19517440 | tf_op jit(solution)/shard_map/krh,khd->rd/dot_general | solution.py:727
  515.3 33.8 %collective-permute-done.54 = bf16[320,2944]{1,0:T(8,128)(2,1)} collective-permute-done((bf16[320,2944]{1,0:T(8,128)(2,1)}, bf16[320,2944]{1,0:T(8,128)(2,1)}, u32[]{:S(2)}, u32[]{:S(2)}) %collective-permute-start.54) | collective-permute-done | bytes 1884192 | tf_op jit(solution)/shard_map/ppermute | solution.py:427
  567.9 18.8 %fusion.107 = (bf16[1,1280,720]{1,2,0:T(8,128)(2,1)}, bf16[1,1280,720]{1,2,0:T(8,128)(2,1)}, f32[1280]{0:T(1024)S(1)}) fusion(f32[1280]{0:T(1024)S(1)} %reduce.4, f32[2,1280,720]{1,2,0:T(8,128)} %copy-done.23, bf16[1280,720]{0,1:T(8,128)(2,1)S(1)} %copy-done.82, bf16[1280,2944]{1,0:T(8,128)(2,1)S(1)} %constant_dynamic-update-slice_fusion.10, ...), kind=kOutput, calls=%fused_computation.199 | convolution fusion | flops 5467851776 | bytes 24596480 | tf_op jit(solution)/shard_map/dot_general | solution.py:25
  594.0 14.7 %bitcast_convert_fusion = bf16[1280,2944]{1,0:T(8,128)(2,1)S(1)} fusion(bf16[2,1280,720]{1,2,0:T(8,128)(2,1)S(1)} %pad_maximum_fusion.1, bf16[2,720,2880]{2,1,0:T(8,128)(2,1)} %bitcast.455), kind=kOutput, calls=%fused_computation | convolution fusion | flops 10856529920 | bytes 19517440 | tf_op jit(solution)/shard_map/krh,khd->rd/dot_general | solution.py:727
  608.8 20.2 %collective-permute-done.59 = f32[640,1]{0,1:T(1,128)S(1)} collective-permute-done((f32[640,1]{0,1:T(1,128)S(1)}, f32[640,1]{0,1:T(1,128)S(1)}, u32[]{:S(2)}, u32[]{:S(2)}) %collective-permute-start.59) | collective-permute-done | bytes 2592 | tf_op jit(solution)/shard_map/ppermute | solution.py:427
  644.4 8.9 copy.163
  678.0 14.5 %fusion = f32[2,720,2880]{2,1,0:T(8,128)} fusion(bf16[2,1280,720]{1,2,0:T(8,128)(2,1)S(1)} %copy-done.9, bf16[1280,2944]{1,0:T(8,128)(2,1)S(1)} %bitcast.411), kind=kOutput, calls=%fused_computation.13 | convolution fusion | flops 10616832000 | bytes 27811840 | tf_op jit(solution)/shard_map/krh,rd->khd/dot_general | solution.py:727
  692.6 21.5 %convolution_add_fusion = f32[2,720,2880]{2,1,0:T(8,128)} fusion(f32[2,720,2880]{2,1,0:T(8,128)} %fusion, bf16[2,1280,720]{1,2,0:T(8,128)(2,1)} %pad_maximum_fusion, bf16[1280,2944]{1,0:T(8,128)(2,1)} %copy-done.17), kind=kOutput, calls=%fused_computation.12 | convolution fusion | flops 10620979200 | bytes 44400640 | tf_op jit(solution)/shard_map/krh,rd->khd/dot_general | solution.py:727
  729.8 16.4 %collective-permute-done.62 = bf16[128,2944]{0,1:T(8,128)(2,1)} collective-permute-done((bf16[128,2944]{0,1:T(8,128)(2,1)}, bf16[128,2944]{0,1:T(8,128)(2,1)}, u32[]{:S(2)}, u32[]{:S(2)}) %collective-permute-start.62) | collective-permute-done | bytes 753696 | tf_op jit(solution)/shard_map/ppermute | solution.py:319
  759.5 24.8 %collective-permute-done.64 = bf16[128,2944]{0,1:T(8,128)(2,1)} collective-permute-done((bf16[128,2944]{0,1:T(8,128)(2,1)}, bf16[128,2944]{0,1:T(8,128)(2,1)}, u32[]{:S(2)}, u32[]{:S(2)}) %collective-permute-start.64) | collective-permute-done | bytes 753696 | tf_op jit(solution)/shard_map/ppermute | solution.py:315
  821.7 8.2 fusion.7
  848.7 12.8 %fusion.21 = f32[720,2880]{1,0:T(8,128)} fusion(f32[720,2880]{1,0:T(8,128)} %fusion.7, bf16[1280,720]{0,1:T(8,128)(2,1)} %copy-done.78, bf16[1280,2944]{1,0:T(8,128)(2,1)} %constant_dynamic-update-slice_fusion.13), kind=kOutput, calls=%fused_computation.39 | convolution fusion | flops 5310489600 | bytes 25968640 | tf_op jit(solution)/shard_map/dot_general | solution.py:25
  869.3 17.7 %collective-permute-done.78 = bf16[128,2880]{0,1:T(8,128)(2,1)S(1)} collective-permute-done((bf16[128,2880]{0,1:T(8,128)(2,1)}, bf16[128,2880]{0,1:T(8,128)(2,1)S(1)}, u32[]{:S(2)}, u32[]{:S(2)}) %collective-permute-start.78) | collective-permute-done | bytes 737312 | tf_op jit(solution)/shard_map/ppermute | solution.py:315
  917.1 11.1 %collective-permute-done.82 = bf16[128,2880]{0,1:T(8,128)(2,1)S(1)} collective-permute-done((bf16[128,2880]{0,1:T(8,128)(2,1)S(1)}, bf16[128,2880]{0,1:T(8,128)(2,1)S(1)}, u32[]{:S(2)}, u32[]{:S(2)}) %collective-permute-start.82) | collective-permute-done | bytes 737312 | tf_op jit(solution)/shard_map/ppermute | solution.py:319
  930.8 15.5 %shard_map.349 = (bf16[1024,640]{1,0:T(8,128)(2,1)}, f32[8,640]{1,0:T(8,128)}, f32[8,128]{1,0:T(8,128)}) custom-call(s32[3]{0:T(128)} %bitcast.452, f32[8]{0:T(128)} %select_reduce_fusion.1.sinks_ref, bf16[1024,640]{1,0:T(8,128)(2,1)} %get-tuple-element.291.turned_ref.before_ref, bf16[1024,640]{1,0:T(8,128)(2,1)} %get-tuple-element.291.turned_ref.before_ref, ...), custom_call_target="tpu_custom_call" | custom-call | flops 1677721600 | bytes 6553600 | tf_op jit(solution)/shard_map/pallas_call | solution.py:204
  1036.9 14.2 %collective-permute-done.98 = bf16[2880,128]{1,0:T(8,128)(2,1)S(1)} collective-permute-done((bf16[2880,128]{1,0:T(8,128)(2,1)S(1)}, bf16[2880,128]{1,0:T(8,128)(2,1)S(1)}, u32[]{:S(2)}, u32[]{:S(2)}) %collective-permute-start.98) | collective-permute-done | bytes 737312 | tf_op jit(solution)/shard_map/ppermute | solution.py:427
  1057.0 9.2 collective-permute-done.102
  (970 shorter events, 590.0 us)
Async XLA Ops:
  7.2 439.9 %all-gather.2.cloned.1.call-start = ((), (), s32[]{:S(2)}) async-start(), calls=%async_computation.1 | async-start | bytes 6782976 | tf_op jit(solution)/shard_map/all_gather | solution.py:415
  44.7 84.5 %collective-permute-start.7 = (bf16[5760,128]{1,0:T(8,128)(2,1)}, bf16[5760,128]{1,0:T(8,128)(2,1)}, u32[]{:S(2)}, u32[]{:S(2)}) collective-permute-start(bf16[5760,128]{1,0:T(8,128)(2,1)} %pad_maximum_fusion.7), channel_id=1, source_target_pairs={{0,2},{1,3},{2,0},{3,1},{4,6},{5,7},{6,4},{7,5},{8,10},{9,11},{10,... | collective-permute-start | bytes 4423688 | tf_op jit(solution)/shard_map/ppermute | solution.py:427
  45.2 86.4 %collective-permute-start.6 = (bf16[5760,128]{1,0:T(8,128)(2,1)}, bf16[5760,128]{1,0:T(8,128)(2,1)}, u32[]{:S(2)}, u32[]{:S(2)}) collective-permute-start(bf16[5760,128]{1,0:T(8,128)(2,1)} %pad_maximum_fusion.7), channel_id=1, source_target_pairs={{0,1},{1,0},{2,3},{3,2},{4,5},{5,4},{6,7},{7,6},{8,9},{9,8},{10,11... | collective-permute-start | bytes 4423688 | tf_op jit(solution)/shard_map/ppermute | solution.py:423
  46.7 38.3 %collective-permute-start.9 = (bf16[32,2880]{1,0:T(8,128)(2,1)S(1)}, bf16[32,2880]{1,0:T(8,128)(2,1)S(1)}, u32[]{:S(2)}, u32[]{:S(2)}) collective-permute-start(bf16[32,2880]{1,0:T(8,128)(2,1)S(1)} %pad_maximum_fusion.19), channel_id=1, source_target_pairs={{0,1},{1,0},{2,3},{3,2},{4,5},{5,4},{6,7},{7,6},{8,9},{9,8},{10,11... | collective-permute-start | bytes 552968 | tf_op jit(solution)/shard_map/ppermute | solution.py:423
  49.8 33.5 %collective-permute-start.10 = (bf16[32,2880]{1,0:T(8,128)(2,1)S(1)}, bf16[32,2880]{1,0:T(8,128)(2,1)S(1)}, u32[]{:S(2)}, u32[]{:S(2)}) collective-permute-start(bf16[32,2880]{1,0:T(8,128)(2,1)S(1)} %pad_maximum_fusion.19), channel_id=1, source_target_pairs={{0,2},{1,3},{2,0},{3,1},{4,6},{5,7},{6,4},{7,5},{8,10},{9,11},{10,... | collective-permute-start | bytes 552968 | tf_op jit(solution)/shard_map/ppermute | solution.py:427
  51.4 47.9 %collective-permute-start.12 = (bf16[128,2880]{0,1:T(8,128)(2,1)}, bf16[128,2880]{0,1:T(8,128)(2,1)}, u32[]{:S(2)}, u32[]{:S(2)}) collective-permute-start(bf16[128,2880]{0,1:T(8,128)(2,1)} %collective-permute-done), channel_id=1, source_target_pairs={{8,16},{12,20},{16,24},{20,28},{9,17},{13,21},{17,25},{21,29},{10,... | collective-permute-start | bytes 2211848 | tf_op jit(solution)/shard_map/ppermute | solution.py:315
  297.9 23.3 %collective-permute-start.36 = (bf16[160,2944]{1,0:T(8,128)(2,1)S(1)}, bf16[160,2944]{1,0:T(8,128)(2,1)S(1)}, u32[]{:S(2)}, u32[]{:S(2)}) collective-permute-start(bf16[160,2944]{1,0:T(8,128)(2,1)S(1)} %convolution_convert_fusion.21), channel_id=1, source_target_pairs={{0,2},{1,3},{2,0},{3,1},{4,6},{5,7},{6,4},{7,5},{8,10},{9,11},{10,... | collective-permute-start | bytes 2826248 | tf_op jit(solution)/shard_map/ppermute | solution.py:427
  344.6 33.3 %collective-permute-start.42 = (bf16[160,2944]{1,0:T(8,128)(2,1)}, bf16[160,2944]{1,0:T(8,128)(2,1)}, u32[]{:S(2)}, u32[]{:S(2)}) collective-permute-start(bf16[160,2944]{1,0:T(8,128)(2,1)} %convolution_convert_fusion.19), channel_id=1, source_target_pairs={{0,2},{1,3},{2,0},{3,1},{4,6},{5,7},{6,4},{7,5},{8,10},{9,11},{10,... | collective-permute-start | bytes 2826248 | tf_op jit(solution)/shard_map/ppermute | solution.py:427
  348.6 39.8 %collective-permute-start.43 = (bf16[160,2944]{1,0:T(8,128)(2,1)}, bf16[160,2944]{1,0:T(8,128)(2,1)}, u32[]{:S(2)}, u32[]{:S(2)}) collective-permute-start(bf16[160,2944]{1,0:T(8,128)(2,1)} %convolution_convert_fusion.18), channel_id=1, source_target_pairs={{0,2},{1,3},{2,0},{3,1},{4,6},{5,7},{6,4},{7,5},{8,10},{9,11},{10,... | collective-permute-start | bytes 2826248 | tf_op jit(solution)/shard_map/ppermute | solution.py:427
  349.0 547.7 %reduce-scatter.4.cloned.1.call-start = ((), (), s32[]{:S(2)}) async-start(), calls=%async_computation.2 | async-start | bytes 6782976
  403.1 44.0 %collective-permute-start.48 = (bf16[640,2944]{1,0:T(8,128)(2,1)}, bf16[640,2944]{1,0:T(8,128)(2,1)}, u32[]{:S(2)}, u32[]{:S(2)}) collective-permute-start(bf16[640,2944]{1,0:T(8,128)(2,1)} %slice.677), channel_id=1, source_target_pairs={{0,1},{1,0},{2,3},{3,2},{4,5},{5,4},{6,7},{7,6},{8,9},{9,8},{10,11... | collective-permute-start | bytes 11304968 | tf_op jit(solution)/shard_map/ppermute | solution.py:423
  442.2 24.5 %collective-permute-start.49 = (bf16[640,2944]{1,0:T(8,128)(2,1)}, bf16[640,2944]{1,0:T(8,128)(2,1)}, u32[]{:S(2)}, u32[]{:S(2)}) collective-permute-start(bf16[640,2944]{1,0:T(8,128)(2,1)} %slice.678), channel_id=1, source_target_pairs={{0,1},{1,0},{2,3},{3,2},{4,5},{5,4},{6,7},{7,6},{8,9},{9,8},{10,11... | collective-permute-start | bytes 11304968 | tf_op jit(solution)/shard_map/ppermute | solution.py:423
  464.7 50.7 %collective-permute-start.53 = (bf16[320,2944]{1,0:T(8,128)(2,1)S(1)}, bf16[320,2944]{1,0:T(8,128)(2,1)}, u32[]{:S(2)}, u32[]{:S(2)}) collective-permute-start(bf16[320,2944]{1,0:T(8,128)(2,1)S(1)} %pad_maximum_fusion.4), channel_id=1, source_target_pairs={{0,2},{1,3},{2,0},{3,1},{4,6},{5,7},{6,4},{7,5},{8,10},{9,11},{10,... | collective-permute-start | bytes 5652488 | tf_op jit(solution)/shard_map/ppermute | solution.py:427
  466.3 82.8 %collective-permute-start.54 = (bf16[320,2944]{1,0:T(8,128)(2,1)}, bf16[320,2944]{1,0:T(8,128)(2,1)}, u32[]{:S(2)}, u32[]{:S(2)}) collective-permute-start(bf16[320,2944]{1,0:T(8,128)(2,1)} %get-tuple-element.517), channel_id=1, source_target_pairs={{0,2},{1,3},{2,0},{3,1},{4,6},{5,7},{6,4},{7,5},{8,10},{9,11},{10,... | collective-permute-start | bytes 5652488 | tf_op jit(solution)/shard_map/ppermute | solution.py:427
  472.7 158.4 %collective-permute-start.50 = (bf16[640,2944]{1,0:T(8,128)(2,1)}, bf16[640,2944]{1,0:T(8,128)(2,1)}, u32[]{:S(2)}, u32[]{:S(2)}) collective-permute-start(bf16[640,2944]{1,0:T(8,128)(2,1)} %add_convert_fusion.1), channel_id=1, source_target_pairs={{0,2},{1,3},{2,0},{3,1},{4,6},{5,7},{6,4},{7,5},{8,10},{9,11},{10,... | collective-permute-start | bytes 11304968 | tf_op jit(solution)/shard_map/ppermute | solution.py:427
  562.4 26.8 %collective-permute-start.57 = (bf16[640,2944]{1,0:T(8,128)(2,1)}, bf16[640,2944]{1,0:T(8,128)(2,1)S(1)}, u32[]{:S(2)}, u32[]{:S(2)}) collective-permute-start(bf16[640,2944]{1,0:T(8,128)(2,1)} %slice.558), channel_id=1, source_target_pairs={{0,1},{1,0},{2,3},{3,2},{4,5},{5,4},{6,7},{7,6},{8,9},{9,8},{10,11... | collective-permute-start | bytes 11304968 | tf_op jit(solution)/shard_map/ppermute | solution.py:423
  592.3 36.7 %collective-permute-start.59 = (f32[640,1]{0,1:T(1,128)S(1)}, f32[640,1]{0,1:T(1,128)S(1)}, u32[]{:S(2)}, u32[]{:S(2)}) collective-permute-start(f32[640,1]{0,1:T(1,128)S(1)} %slice.699), channel_id=1, source_target_pairs={{0,2},{1,3},{2,0},{3,1},{4,6},{5,7},{6,4},{7,5},{8,10},{9,11},{10,... | collective-permute-start | bytes 7688 | tf_op jit(solution)/shard_map/ppermute | solution.py:427
  631.1 36.5 %collective-permute-start.60 = (bf16[640,2944]{1,0:T(8,128)(2,1)}, bf16[640,2944]{1,0:T(8,128)(2,1)}, u32[]{:S(2)}, u32[]{:S(2)}) collective-permute-start(bf16[640,2944]{1,0:T(8,128)(2,1)} %slice.565), channel_id=1, source_target_pairs={{0,1},{1,0},{2,3},{3,2},{4,5},{5,4},{6,7},{7,6},{8,9},{9,8},{10,11... | collective-permute-start | bytes 11304968 | tf_op jit(solution)/shard_map/ppermute | solution.py:423
  674.0 40.1 %collective-permute-start.61 = (bf16[160,2944]{1,0:T(8,128)(2,1)}, bf16[160,2944]{1,0:T(8,128)(2,1)}, u32[]{:S(2)}, u32[]{:S(2)}) collective-permute-start(bf16[160,2944]{1,0:T(8,128)(2,1)} %get-tuple-element.498), channel_id=1, source_target_pairs={{0,2},{1,3},{2,0},{3,1},{4,6},{5,7},{6,4},{7,5},{8,10},{9,11},{10,... | collective-permute-start | bytes 2826248 | tf_op jit(solution)/shard_map/ppermute | solution.py:427
  675.6 47.7 %collective-permute-start.63 = (bf16[160,2944]{1,0:T(8,128)(2,1)}, bf16[160,2944]{1,0:T(8,128)(2,1)}, u32[]{:S(2)}, u32[]{:S(2)}) collective-permute-start(bf16[160,2944]{1,0:T(8,128)(2,1)} %get-tuple-element.497), channel_id=1, source_target_pairs={{0,2},{1,3},{2,0},{3,1},{4,6},{5,7},{6,4},{7,5},{8,10},{9,11},{10,... | collective-permute-start | bytes 2826248 | tf_op jit(solution)/shard_map/ppermute | solution.py:427
  676.0 77.6 %collective-permute-start.66 = (bf16[160,2944]{1,0:T(8,128)(2,1)}, bf16[160,2944]{1,0:T(8,128)(2,1)}, u32[]{:S(2)}, u32[]{:S(2)}) collective-permute-start(bf16[160,2944]{1,0:T(8,128)(2,1)} %get-tuple-element.496), channel_id=1, source_target_pairs={{0,2},{1,3},{2,0},{3,1},{4,6},{5,7},{6,4},{7,5},{8,10},{9,11},{10,... | collective-permute-start | bytes 2826248 | tf_op jit(solution)/shard_map/ppermute | solution.py:427
  677.6 118.0 %collective-permute-start.70 = (bf16[160,2944]{1,0:T(8,128)(2,1)}, bf16[160,2944]{1,0:T(8,128)(2,1)}, u32[]{:S(2)}, u32[]{:S(2)}) collective-permute-start(bf16[160,2944]{1,0:T(8,128)(2,1)} %get-tuple-element.495), channel_id=1, source_target_pairs={{0,2},{1,3},{2,0},{3,1},{4,6},{5,7},{6,4},{7,5},{8,10},{9,11},{10,... | collective-permute-start | bytes 2826248 | tf_op jit(solution)/shard_map/ppermute | solution.py:427
  721.8 24.4 %collective-permute-start.62 = (bf16[128,2944]{0,1:T(8,128)(2,1)}, bf16[128,2944]{0,1:T(8,128)(2,1)}, u32[]{:S(2)}, u32[]{:S(2)}) collective-permute-start(bf16[128,2944]{0,1:T(8,128)(2,1)} %constant_dynamic-slice_fusion.26), channel_id=1, source_target_pairs={{0,4},{4,0},{8,12},{12,8},{16,20},{20,16},{24,28},{28,24},{1,5},{5... | collective-permute-start | bytes 2261000 | tf_op jit(solution)/shard_map/ppermute | solution.py:319
  748.7 35.7 %collective-permute-start.64 = (bf16[128,2944]{0,1:T(8,128)(2,1)}, bf16[128,2944]{0,1:T(8,128)(2,1)}, u32[]{:S(2)}, u32[]{:S(2)}) collective-permute-start(bf16[128,2944]{0,1:T(8,128)(2,1)} %fusion.136), channel_id=1, source_target_pairs={{0,8},{4,12},{24,16},{28,20},{1,9},{5,13},{25,17},{29,21},{2,10},{... | collective-permute-start | bytes 2261000 | tf_op jit(solution)/shard_map/ppermute | solution.py:315
  752.2 32.1 %collective-permute-start.65 = (bf16[128,2944]{0,1:T(8,128)(2,1)}, bf16[128,2944]{0,1:T(8,128)(2,1)}, u32[]{:S(2)}, u32[]{:S(2)}) collective-permute-start(bf16[128,2944]{0,1:T(8,128)(2,1)} %get-tuple-element.327), channel_id=1, source_target_pairs={{0,4},{4,0},{8,12},{12,8},{16,20},{20,16},{24,28},{28,24},{1,5},{5... | collective-permute-start | bytes 2261000 | tf_op jit(solution)/shard_map/ppermute | solution.py:319
  863.4 23.6 %collective-permute-start.78 = (bf16[128,2880]{0,1:T(8,128)(2,1)}, bf16[128,2880]{0,1:T(8,128)(2,1)S(1)}, u32[]{:S(2)}, u32[]{:S(2)}) collective-permute-start(bf16[128,2880]{0,1:T(8,128)(2,1)} %collective-permute-done.75), channel_id=1, source_target_pairs={{16,8},{20,12},{8,0},{12,4},{17,9},{21,13},{9,1},{13,5},{18,10},{2... | collective-permute-start | bytes 2211848 | tf_op jit(solution)/shard_map/ppermute | solution.py:315
  977.9 42.8 %collective-permute-start.89 = (bf16[2,2880,128]{2,1,0:T(8,128)(2,1)}, bf16[2,2880,128]{2,1,0:T(8,128)(2,1)}, u32[]{:S(2)}, u32[]{:S(2)}) collective-permute-start(bf16[2,2880,128]{2,1,0:T(8,128)(2,1)} %pad_maximum_fusion.15), channel_id=1, source_target_pairs={{0,1},{1,0},{2,3},{3,2},{4,5},{5,4},{6,7},{7,6},{8,9},{9,8},{10,11... | collective-permute-start | bytes 4423688 | tf_op jit(solution)/shard_map/ppermute | solution.py:423
  989.6 34.1 %collective-permute-start.86 = (bf16[128,2880]{0,1:T(8,128)(2,1)}, bf16[128,2880]{0,1:T(8,128)(2,1)}, u32[]{:S(2)}, u32[]{:S(2)}) collective-permute-start(bf16[128,2880]{0,1:T(8,128)(2,1)} %select_convert_fusion.3), channel_id=1, source_target_pairs={{0,8},{4,12},{8,16},{12,20},{1,9},{5,13},{9,17},{13,21},{2,10},{6,... | collective-permute-start | bytes 2211848 | tf_op jit(solution)/shard_map/ppermute | solution.py:315
  992.3 31.3 %collective-permute-start.87 = (bf16[128,2880]{0,1:T(8,128)(2,1)}, bf16[128,2880]{0,1:T(8,128)(2,1)}, u32[]{:S(2)}, u32[]{:S(2)}) collective-permute-start(bf16[128,2880]{0,1:T(8,128)(2,1)} %select_convert_fusion.3), channel_id=1, source_target_pairs={{24,16},{28,20},{16,8},{20,12},{25,17},{29,21},{17,9},{21,13},{26,... | collective-permute-start | bytes 2211848 | tf_op jit(solution)/shard_map/ppermute | solution.py:315
  995.5 28.2 %collective-permute-start.88 = (bf16[128,2880]{0,1:T(8,128)(2,1)}, bf16[128,2880]{0,1:T(8,128)(2,1)}, u32[]{:S(2)}, u32[]{:S(2)}) collective-permute-start(bf16[128,2880]{0,1:T(8,128)(2,1)} %get-tuple-element.379), channel_id=1, source_target_pairs={{0,4},{4,0},{8,12},{12,8},{16,20},{20,16},{24,28},{28,24},{1,5},{5... | collective-permute-start | bytes 2211848 | tf_op jit(solution)/shard_map/ppermute | solution.py:319
  1026.2 24.9 %collective-permute-start.98 = (bf16[2880,128]{1,0:T(8,128)(2,1)S(1)}, bf16[2880,128]{1,0:T(8,128)(2,1)S(1)}, u32[]{:S(2)}, u32[]{:S(2)}) collective-permute-start(bf16[2880,128]{1,0:T(8,128)(2,1)S(1)} %get-tuple-element.396), channel_id=1, source_target_pairs={{0,2},{1,3},{2,0},{3,1},{4,6},{5,7},{6,4},{7,5},{8,10},{9,11},{10,... | collective-permute-start | bytes 2211848 | tf_op jit(solution)/shard_map/ppermute | solution.py:427
  1035.3 30.9 %collective-permute-start.102 = (bf16[2880,128]{1,0:T(8,128)(2,1)S(1)}, bf16[2880,128]{1,0:T(8,128)(2,1)S(1)}, u32[]{:S(2)}, u32[]{:S(2)}) collective-permute-start(bf16[2880,128]{1,0:T(8,128)(2,1)S(1)} %get-tuple-element.403), channel_id=1, source_target_pairs={{0,2},{1,3},{2,0},{3,1},{4,6},{5,7},{6,4},{7,5},{8,10},{9,11},{10,... | collective-permute-start | bytes 2211848 | tf_op jit(solution)/shard_map/ppermute | solution.py:427
  (278 other events, 4243.5 us)
Sparse Core Ops, SparseCore 0:
  349.2 97.6 all-gather.1
  653.4 134.9 reduce-scatter.3

commit v4 on v3

--- a/solution.py
+++ b/solution.py
@@ -367,16 +367,18 @@
         other = lax.dynamic_slice_in_dim(pair, (1 - self.side) * rows, rows, 0)
         return own, other
 
-    def scatter(self, term, counts=(0, 0, 0, 0)):
+    def scatter(self, term, counts=(0, 0, 0, 0), pools=((), (), (), ())):
         tie = self.work.tie
         own_3, other_3 = self.halves(term(3))
         side_3 = self.across(other_3)
         own_2, other_2 = self.halves(term(2))
-        side_3, other_2, own_2 = tie(side_3, other_2, own_2, count=counts[0])
+        side_3, other_2, own_2 = tie(side_3, other_2, own_2, count=counts[0], pool=pools[0])
         sum_3 = own_3.astype(F32) + side_3.astype(F32)
         step_1, side_2 = self.along(sum_3.astype(BF), [(0, 1), (3, 2)]), self.across(other_2)
         own_1, other_1 = self.halves(term(1))
-        step_1, side_2, other_1, own_1 = tie(step_1, side_2, other_1, own_1, count=counts[1])
+        step_1, side_2, other_1, own_1 = tie(
+            step_1, side_2, other_1, own_1, count=counts[1], pool=pools[1]
+        )
         sum_2 = own_2.astype(F32) + side_2.astype(F32)
         sent = jnp.where(self.at_end, sum_2, sum_3 + step_1.astype(F32)).astype(BF)
         up, down, side_1 = (
@@ -385,7 +387,9 @@
             self.across(other_1),
         )
         own_0, other_0 = self.halves(term(0))
-        up, down, side_1, own_0, other_0 = tie(up, down, side_1, own_0, other_0, count=counts[2])
+        up, down, side_1, own_0, other_0 = tie(
+            up, down, side_1, own_0, other_0, count=counts[2], pool=pools[2]
+        )
         sum_1 = own_1.astype(F32) + side_1.astype(F32)
         sent_up = jnp.where(self.at_low, sum_1, sum_2 + up.astype(F32)).astype(BF)
         sent_down = (sum_1 + down.astype(F32)).astype(BF)
@@ -394,8 +398,8 @@
             self.along(sent_down, [(1, 0), (2, 1), (3, 2)]),
             self.across(other_0),
         )
-        if counts[3]:
-            up, down, side_0 = tie(up, down, side_0, count=counts[3])
+        if counts[3] is not None:
+            up, down, side_0 = tie(up, down, side_0, count=counts[3], pool=pools[3])
         return own_0.astype(F32) + side_0.astype(F32) + up.astype(F32) + down.astype(F32)
 
 
@@ -407,7 +411,7 @@
         used = use(0, gather_seq(block))
         return [used], [later(0, used) if later else ()]
 
-    def scatter(self, term, counts=()):
+    def scatter(self, term, counts=(), pools=()):
         return scatter_seq(term(0)).astype(F32)
 
 
@@ -509,38 +513,27 @@
 
     kv_head = seq_index // max(1, seq_count // KEY_VALUE_HEADS)
 
-    def parameters(
-        attn_gain,
-        ffn_gain,
-        output_bias_vector,
-        sink_logit_values,
-        router_bias,
-        query_bias_vector,
-        key_bias_vector,
-        value_bias_vector,
-        expert_down_bias,
-        router_weight,
-        query_matrix,
-        output_matrix,
-        key_matrix,
-        value_matrix,
-    ):
-        tiny = jnp.concatenate(
-            [sink_logit_values, router_bias, query_bias_vector, key_bias_vector, value_bias_vector]
-        )
-        tiny = jnp.concatenate([tiny, jnp.zeros((part - tiny.shape[0],), BF)])
-        small = jnp.concatenate(
-            [
-                attn_gain[None],
-                ffn_gain[None],
-                output_bias_vector[None],
-                tiny[None],
-                expert_down_bias,
-                router_weight.T,
-            ],
-            axis=0,
-        )
-        small_all = jnp.stack(in_order(from_all(small)))
+    tiny = jnp.concatenate(
+        [sink_logit_values, router_bias, query_bias_vector, key_bias_vector, value_bias_vector]
+    )
+    tiny = jnp.concatenate([tiny, jnp.zeros((part - tiny.shape[0],), BF)])
+    small = jnp.concatenate(
+        [
+            attn_gain[None],
+            ffn_gain[None],
+            output_bias_vector[None],
+            tiny[None],
+            expert_down_bias,
+            router_weight.T,
+        ],
+        axis=0,
+    )
+    work.pool["small"] = to_core(small), to_chip(small)
+    work.pool["wo"] = output_matrix.T
+
+    def parameters(query_matrix, key_matrix, value_matrix):
+        small_core, small_chip = work.pool["small"]
+        small_all = jnp.stack(in_order([small, small_core, small_chip, to_core(small_chip)]))
         wide = jnp.swapaxes(small_all, 0, 1).reshape(small.shape[0], width).astype(F32)
         attn_gain_f, ffn_gain_f, out_bias_f = wide[0], wide[1], wide[2]
         down_bias_f = wide[4 : 4 + expert_count]
@@ -557,9 +550,7 @@
         q_bias = jnp.concatenate(
             [lax.dynamic_slice_in_dim(q_bias, at, 1, 0)[0] for at in near_first]
         )
-        pieces = from_all(jnp.concatenate([query_matrix, output_matrix.T], axis=0))
-        w_query = jnp.concatenate([piece[:width] for piece in pieces], axis=1)
-        wo_t = jnp.concatenate([piece[width:] for piece in pieces], axis=1)
+        w_query = jnp.concatenate(from_all(query_matrix), axis=1)
         if shared_kv:
 
             def own_head(piece):
@@ -585,29 +576,11 @@
             sinks_f,
             router_bias_f,
             w_query,
-            wo_t,
             w_pair,
             lin_bias,
         )
 
-    work.add(
-        "parameters",
-        parameters,
-        attn_gain,
-        ffn_gain,
-        output_bias_vector,
-        sink_logit_values,
-        router_bias,
-        query_bias_vector,
-        key_bias_vector,
-        value_bias_vector,
-        expert_down_bias,
-        router_weight,
-        query_matrix,
-        output_matrix,
-        key_matrix,
-        value_matrix,
-    )
+    work.add("parameters", parameters, query_matrix, key_matrix, value_matrix)
 
     columns = jnp.concatenate(
         [
@@ -633,7 +606,12 @@
         pairs.append(pair)
         return pair
 
-    line.gather(layer_input[0], lambda at, pair: (work.take("parameters"), arrive(at, pair))[1])
+    line.gather(
+        layer_input[0],
+        lambda at, pair: (work.take("parameters"), arrive(at, pair))[1],
+        pools=(("small",), (), ("wo",), ()),
+    )
+    wo_t = jnp.concatenate(from_all(work.pool["wo"]), axis=1)
     (
         attn_gain_f,
         ffn_gain_f,
@@ -643,7 +621,6 @@
         sinks_f,
         router_bias_f,
         w_query,
-        wo_t,
         w_pair,
         lin_bias,
     ) = work.take("parameters")
@@ -705,12 +682,13 @@
     def send_rows(at, used):
         return to_core(used[1]), to_chip(used[1])
 
-    picked, sent = line.gather(mid_packed, pick_rows, send_rows)
+    spare = padded - width
+    work.pool["cot"] = jnp.concatenate([cot_here, jnp.zeros((tokens_here, spare), BF)], axis=1)
+    picked, sent = line.gather(mid_packed, pick_rows, send_rows, pools=((), ("cot",), (), ()))
     selects = [select for select, _ in picked]
     own_rows = [rows for _, rows in picked]
     core_rows = [core for core, _ in sent]
     chip_rows = [chip for _, chip in sent]
-    spare = padded - width
     units_w = jnp.pad(jnp.swapaxes(expert_gate_up[0], 1, 2), ((0, 0), (0, 0), (0, spare)))
     down_w = jnp.pad(expert_down[0], ((0, 0), (0, spare)))
     units_b = expert_gate_up_bias[0].astype(F32)[:, None, :]
@@ -749,33 +727,31 @@
         return score, jnp.stack([grad_gate_pre.astype(BF), grad_up_pre.astype(BF)])
 
     def row_step(made):
-        return einsum("krh,khd->rd", made[1], units_w).astype(BF)
-
-    cot_block = jnp.concatenate([cot_here, jnp.zeros((tokens_here, spare), BF)], axis=1)
-    cot_block, own_rows = work.tie(cot_block, own_rows)
-    cot_rows = gather_seq(cot_block)
+        return einsum("krh,khd->rd", made, units_w).astype(BF)
+
+    cot_rows = gather_seq(work.pool["cot"])
     near = joined(own_rows + core_rows)
+    select_all = jnp.zeros((capacity, length), BF)
+    for at, (select, start) in enumerate(zip(selects, starts)):
+        select_all = lax.dynamic_update_slice(select_all, select, (at * slots, start))
     made_n = hidden_step(near)
-    made_n, chip_rows = work.tie(made_n, chip_rows)
+    select_chip = to_chip(select_all)
+    mix_n = mix_step(made_n)
+    made_n, chip_rows, mix_n = work.tie(made_n, chip_rows, mix_n)
     far = joined(chip_rows + [to_core(chip) for chip in chip_rows])
-    mix_n = mix_step(made_n)
     made_o = hidden_step(far)
     mix_o = mix_step(made_o)
-    mix_core_n = to_core(mix_n[capacity:])
-    mix_core_o = to_core(mix_o[capacity:])
-    cot_rows, made_o, mix_n, mix_o, mix_core_n = work.tie(
-        cot_rows, made_o, mix_n, mix_o, mix_core_n
-    )
-    cot_own = [dot(select, taken(cot_rows, at), 1, 0).astype(BF) for select, at in zip(selects, starts)]
-    half = (len(cot_own) + 1) // 2
-    cot_own = [jnp.concatenate(cot_own[:half])] + (
-        [jnp.concatenate(cot_own[half:])] if cot_own[half:] else []
-    )
-    cot_chip = [to_chip(rows) for rows in cot_own]
+    mix_core_n, mix_core_o = to_core(mix_n[capacity:]), to_core(mix_o[capacity:])
+    cot_rows, made_n, made_o, mix_n, mix_o, mix_core_n, select_chip = work.tie(
+        cot_rows, made_n, made_o, mix_n, mix_o, mix_core_n, select_chip
+    )
+    cot_own = dot(select_all, cot_rows, 1, 0).astype(BF)
+    half = (len(selects) + 1) // 2 * slots
+    cot_own = [cot_own[:half], cot_own[half:]] if half < capacity else [cot_own]
+    cot_first = to_chip(cot_own[0])
     cot_near = joined(cot_own + [to_core(rows) for rows in cot_own])
-
     def core_sum(part, from_core):
-        return (part[:capacity].astype(F32) + from_core.astype(F32)).astype(part.dtype)
+        return (part[:capacity].astype(F32) + from_core.astype(F32)).astype(BF)
 
     def total(near_part, from_core, arrived, at):
         return (
@@ -787,15 +763,23 @@
     def slot_rows(rows, at):
         return rows[at * slots : (at + 1) * slots]
 
-    def from_chip(far_sum):
-        return [to_chip(slot_rows(far_sum, at)) for at in reversed(range(len(starts)))][::-1]
+    low_rows = (len(starts) // 2) * slots
 
     def score_step(back_n, back_o):
         scores = jnp.concatenate([back_n[0], back_o[0]], axis=1)
         return scores[:capacity] + to_core(scores[capacity:])
 
+    mix_own = dot(select_all, core_sum(mix_n, mix_core_n), 0, 0).astype(BF)
+    mix_other = dot(select_chip, core_sum(mix_o, mix_core_o), 0, 0).astype(BF)
+    mix_own, mix_other, cot_near, cot_first, cot_own = work.tie(
+        mix_own, mix_other, cot_near, cot_first, cot_own
+    )
+    cot_chip = [cot_first] + [to_chip(rows) for rows in cot_own[1:]]
+    mix_own, mix_other = scatter_seq(mix_own), scatter_seq(mix_other)
+
     back_n = back_step(made_n, cot_near)
-    row_n = row_step(back_n)
+    row_n = row_step(back_n[1])
+
     back_n, row_n, cot_chip = work.tie(back_n, row_n, cot_chip)
     row_near_core = to_core(row_n[capacity:])
     cot_far = joined(cot_chip + [to_core(rows) for rows in cot_chip])
@@ -803,10 +787,18 @@
     back_n, back_o, row_near_core = work.tie(back_n, back_o, row_near_core)
     score = score_step(back_n, back_o)
     score = score[:, :1] + to_chip(score[:, 1:])
-    row_o = row_step(back_o)
-    row_o, score = work.tie(row_o, score)
+    row_o_core = row_step(back_o[1][:, capacity:])
+    row_o_core, back_o, score = work.tie(row_o_core, back_o, score)
+    row_far_core = to_core(row_o_core)
+    row_o = row_step(back_o[1][:, :capacity])
     (score_n, low_n), (score_o, low_o) = back_n, back_o
-    row_far_core = to_core(row_o[capacity:])
+
+
+    def chunk_of(low, high, at):
+        first = at * slots
+        if first < low_rows:
+            return low[first : first + slots]
+        return high[first - low_rows : first - low_rows + slots]
 
     def units_step(low_n, rows_n, low_o, rows_o):
         return einsum("krh,rd->khd", low_n, rows_n[:, :width]) + einsum(
@@ -818,11 +810,13 @@
 
     work.add("units", units_step, low_n, near, low_o, far)
     work.add("down", down_step, made_n[3], cot_near, made_o[3], cot_far)
-    (row_far_core,) = work.tie(row_far_core)
-    arrivals = from_chip(core_sum(row_o, row_far_core))
-
+    row_far_core, row_o, mix_own = work.tie(row_far_core, row_o, mix_own)
+    row_sum_far = core_sum(row_o, row_far_core)
+    row_high, row_low = to_chip(row_sum_far[low_rows:]), row_sum_far[:low_rows]
+    row_high, row_low = work.tie(row_high, row_low, count=1)
+    row_low = to_chip(row_low)
     def back_term(at):
-        row_sum = total(row_n, row_near_core, arrivals[at], at)
+        row_sum = total(row_n, row_near_core, chunk_of(row_low, row_high, at), at)
         grad_high, grad_low = split_low(slot_rows(score, at) * expert_lane)
         back_packed = jnp.concatenate(
             [
@@ -835,19 +829,8 @@
         )
         return dot(selects[at], back_packed, 0, 0).astype(BF)
 
+    work.pool["mix"] = mix_other
     back = line.scatter(back_term, counts=(1, 0, 0, 0))
-
-    mix_far = core_sum(mix_o, mix_core_o)
-    mix_far, arrivals_end = lax.optimization_barrier((mix_far, arrivals[0][:8]))
-    mix_chip = to_chip(mix_far)
-
-    def mix_place(mix_chip):
-        whole = jnp.zeros((length, width), BF)
-        for at, start in enumerate(starts):
-            mix_sum = total(mix_n, mix_core_n, slot_rows(mix_chip, at), at)
-            term = dot(selects[at], mix_sum[:, :width].astype(BF), 0, 0).astype(BF)
-            whole = place_rows(whole, term, start)
-        return whole
 
     cot_f = cot_here.astype(F32)
     grad_gates = (
@@ -879,97 +862,107 @@
         own, chip = sums
         return own + to_chip(chip).astype(F32)
 
-    def seq_sum(values):
-        step = 1
-        while step < seq_count:
-            values = values + lax.ppermute(values, "seq", [(i, i ^ step) for i in range(seq_count)])
-            step *= 2
-        return values
-
-    def small_step(rows):
-        blocks = [lax.dynamic_slice_in_dim(rows, at * part, part, 1) for at in near_first]
-        return to_core_owners(blocks, F32)
-
-    tiny_grad = jnp.zeros((fsdp_count, part), F32)
-    tiny_grad = lax.dynamic_update_slice(
-        tiny_grad, router_bias_grad.reshape(fsdp_count, -1), (0, 0)
-    ).reshape(1, width)
+    def fsdp_sum(values):
+        values = values + to_core(values)
+        return values + to_chip(values)
+
+    def seq_step(step):
+        def add_other(values):
+            return values + lax.ppermute(values, "seq", [(i, i ^ step) for i in range(seq_count)])
+
+        return add_other
+
+    def own_part(whole_array, axis_number):
+        piece_size = whole_array.shape[axis_number] // fsdp_count
+        return lax.dynamic_slice_in_dim(
+            whole_array, fsdp_index * piece_size, piece_size, axis_number
+        )
+
+    tiny_grad = jnp.concatenate([router_bias_grad, jnp.zeros((width - expert_count,), F32)])[None]
     small_grad = jnp.concatenate(
         [out_bias_grad[None], ffn_gain_grad[None], tiny_grad, down_bias_grad, router_grad_t],
         axis=0,
     )
 
+    work.add("small_fsdp", fsdp_sum, small_grad)
+
     attn_rows = jnp.zeros((length, width), BF)
     grad_heads = jnp.zeros((length, q_width), BF)
 
     def head_grads(at, pair):
         return pair, dot(pair, wo_t, 1, 0).astype(BF)
 
-    work.take("units")
-    grads, _ = line.gather(grad_attn, head_grads, counts=(1, 0, 0, 0))
-    mixture = scatter_seq(mix_place(mix_chip)).astype(F32)
+    grads, _ = line.gather(
+        grad_attn, head_grads, counts=(0, 0, 1, 0), pools=(("mix",), (), (), ())
+    )
+    mixture = (mix_own.astype(F32) + to_chip(work.pool["mix"]).astype(F32))[:, :width]
     mixture = mixture + dot(gates, down_bias_f, 1, 0, EXACT)
     layer_output = (resid_mid + mixture).astype(BF)[None]
     for start, (pair, grad_part) in zip(starts, grads):
         attn_rows = place_rows(attn_rows, pair, start)
         grad_heads = place_rows(grad_heads, grad_part, start)
 
-    lin_grad, lin_sums, sink_here_grad = attend_back(
-        turned, cosine_table, sine_table, doc_ends, sinks_here, grad_heads
-    )
-
-    order = None if whole_heads else jnp.argsort(columns)
-    back_order = None if whole_heads else jnp.argsort(order)
-
     def column_blocks(whole):
         if back_order is not None:
             whole = whole[:, back_order]
         return [whole[:, at * q_part : (at + 1) * q_part] for at in range(fsdp_count)]
 
+    order = None if whole_heads else jnp.argsort(columns)
+    back_order = None if whole_heads else jnp.argsort(order)
+    out_sums = to_core_owners(column_blocks(dot(attn_rows, heads, 0, 0)))
+    lin_grad, lin_sums, sink_here_grad = attend_back(
+        turned, cosine_table, sine_table, doc_ends, sinks_here, grad_heads
+    )
+
+    lin_grad, lin_sums, out_sums = work.tie(lin_grad, lin_sums, out_sums)
+
     def query_step(rows, grads):
         return dot(rows, grads[:, :q_width], 0, 0)
 
     def pair_step(rows, grads):
         return dot(grads[:, q_width:], rows, 0, 0)
 
-    sink_all_grad = jnp.sum(head_lane * sink_here_grad[:, None], axis=0)
-
-    def row_blocks(query_w_part, pair_w_part):
+    def gain_step(query_w_part, pair_w_part):
         attn_gain_grad = (
             jnp.sum(query_w_part * w_query.astype(F32), axis=1)
             + jnp.sum(pair_w_part * w_pair.astype(F32), axis=0)
         ) / attn_gain_f
+        sink_all_grad = jnp.sum(head_lane * sink_here_grad[:, None], axis=0)
+        sink_row = jnp.concatenate([sink_all_grad, jnp.zeros((width - QUERY_HEADS,), F32)])
+        return jnp.stack([attn_gain_grad, sink_row])
+
+    def sums_step(lin_sums):
         query_sums = lin_sums[:q_width]
         if back_order is not None:
             query_sums = query_sums[back_order]
-        pair_sums = lin_sums[q_width:]
-        blocks = []
-        for turn, at in enumerate(near_first):
-            gain = lax.dynamic_slice_in_dim(attn_gain_grad, at * part, part, 0)
-            row = [gain, sink_all_grad, query_sums[turn * q_part : (turn + 1) * q_part]]
-            block = []
-            if not shared_kv:
-                for first in (0, HEAD_DIM):
-                    row.append(lax.dynamic_slice_in_dim(pair_sums, first + at * kv_part, kv_part, 0))
-                    block.append(
-                        lax.dynamic_slice_in_dim(pair_w_part, first + at * kv_part, kv_part, 0)
-                    )
-            row = jnp.concatenate(row)
-            row = jnp.concatenate([row, jnp.zeros((width - row.shape[0],), F32)])
-            block.append(jnp.broadcast_to(row[None], (16, width)))
-            blocks.append(jnp.concatenate(block, axis=0))
-        return to_core_owners(blocks)
+        pieces = [query_sums[at * q_part : (at + 1) * q_part] for at in range(fsdp_count)]
+        return fsdp_sum(jnp.concatenate(in_order(pieces) + [lin_sums[q_width:]])[None])[0]
+
+    def pair_sum(pair_w_part):
+        if shared_kv:
+            return ()
+        summed = pair_w_part + to_core(pair_w_part.astype(BF)).astype(F32)
+        return summed + to_chip(summed.astype(BF)).astype(F32)
 
     work.add("query_w", query_step, normed_rows, lin_grad)
-    work.add("out_w", lambda a, b: dot(a, b, 0, 0), attn_rows, heads)
     work.add("pair_w", pair_step, normed_rows, lin_grad)
+    work.add("out_chip", lambda own, chip: to_owners((own, chip)), *out_sums)
     work.add("query_core", lambda whole: to_core_owners(column_blocks(whole)), "query_w")
-    work.add("out_core", lambda whole: to_core_owners(column_blocks(whole)), "out_w")
-    work.add("small_core", small_step, small_grad)
-    work.add("row_core", row_blocks, "query_w", "pair_w")
-    work.add("small_chip", to_owners, "small_core")
-    work.add("row_chip", to_owners, "row_core")
+    work.add("gain", gain_step, "query_w", "pair_w")
     work.add("query_chip", to_owners, "query_core")
+    work.add("gain_core", lambda values: values + to_core(values), "gain")
+    work.add("sums", sums_step, lin_sums)
+    work.add("pair_sum", pair_sum, "pair_w")
+    work.add(
+        "all_1",
+        lambda values, small: jnp.concatenate([values + to_chip(values), small]),
+        "gain_core",
+        "small_fsdp",
+    )
+    step = 1
+    while step < seq_count:
+        work.add("all_%d" % (2 * step), seq_step(step), "all_%d" % step)
+        step *= 2
 
     def input_term(at):
         grad_part = taken(lin_grad, starts[at])
@@ -977,10 +970,11 @@
             dot(grad_part[:, :q_width], w_query, 1, 1) + dot(grad_part[:, q_width:], w_pair, 1, 0)
         ).astype(BF)
 
-    grad_normed_in = line.scatter(input_term, counts=(1, 2, 4, 3))
+    grad_normed_in = line.scatter(input_term, counts=(1, 3, 2, 4))
     query_w_own = work.take("query_chip")
-    out_w_own = to_owners(work.take("out_core")).T
-    owned, small_own = work.take("row_chip"), seq_sum(work.take("small_chip"))
+    out_w_own = work.take("out_chip").T
+    pair_all, small_sum = work.take("pair_sum"), work.take("all_%d" % seq_count)
+    small_own = own_part(small_sum, 1)
     down_grad = work.take("down")
     gate_up_grad = jnp.swapaxes(work.take("units"), 1, 2)
     gate_up_bias_grad = jnp.sum(low_n.astype(F32), axis=1) + jnp.sum(low_o.astype(F32), axis=1)
@@ -994,13 +988,8 @@
         + grad_mid
     )
 
-    owned_row = owned[-1]
-    gain_own = seq_sum(owned_row[None, : part + QUERY_HEADS])[0]
-    sink_own = lax.dynamic_slice_in_dim(
-        gain_own[part:], fsdp_index * sink_logit_values.shape[0], sink_logit_values.shape[0], 0
-    )
-    at = part + QUERY_HEADS
-    query_b_own = owned_row[at : at + q_part]
+    sums = work.take("sums")
+    query_b_own = own_part(sums[: fsdp_count * q_part], 0)
     if shared_kv:
 
         def whole_sum(part_grad):
@@ -1014,30 +1003,33 @@
         key_b_own = whole_sum(lin_sums[q_width : q_width + HEAD_DIM])
         value_b_own = whole_sum(lin_sums[q_width + HEAD_DIM :])
     else:
-        key_w_own, value_w_own = owned[:kv_part].T, owned[kv_part : 2 * kv_part].T
-        at = at + q_part
-        key_b_own, value_b_own = owned_row[at : at + kv_part], owned_row[at + kv_part : at + 2 * kv_part]
+        key_w_own = own_part(pair_all[:HEAD_DIM], 0).T
+        value_w_own = own_part(pair_all[HEAD_DIM:], 0).T
+        key_b_own, value_b_own = (
+            own_part(sums[q_width : q_width + HEAD_DIM], 0),
+            own_part(sums[q_width + HEAD_DIM :], 0),
+        )
 
     return (
         layer_output,
         input_grad[None],
-        gain_own[:part],
+        small_own[0],
         query_w_own,
         query_b_own,
         key_w_own,
         key_b_own,
         value_w_own,
         value_b_own,
-        sink_own,
+        own_part(small_sum[1, :QUERY_HEADS], 0),
         out_w_own,
-        small_own[0],
-        small_own[1],
-        small_own[3 + expert_count :].T,
-        lax.dynamic_slice_in_dim(small_own[2], 0, router_bias.shape[0], 0),
+        small_own[2],
+        small_own[3],
+        small_own[5 + expert_count :].T,
+        own_part(small_sum[4, :expert_count], 0),
         gate_up_grad[None],
         gate_up_bias_grad[None],
         down_grad[None],
-        small_own[3 : 3 + expert_count],
+        small_own[5 : 5 + expert_count],
     )
 
 

time: 1100 us -> 1070 us (0.973)
  other arithmetic: 122 us -> 90.3 us
  local copies, waits for them, and re-layouts: 170 us -> 139 us
  matrix products: 256 us -> 274 us
  waiting for transfers between devices: 362 us -> 373 us
    ppermute x30, waiting for transfers between devices: 146 us -> 172 us  [along(): return lax.ppermute(block, 'seq', route)]
    slice x7 -> x3, local copies, waits for them, and re-layouts: 19 us -> 5.51 us  [slot_rows(): return rows[at * slots:(at + 1) * slots]]
    dot_general x6 -> x7, matrix products: 97.9 us -> 110 us  [einsum(): return jnp.einsum(form, left, right, preferred_element_type=F32)]
    convert_element_type x4 -> x3, other arithmetic: 16 us -> 4.36 us  [the longest x1 4.1 us: core_sum(): return (part[:capacity].astype(F32) + from_core.astype(F32)).astype(BF)]
    dynamic_slice x11 -> x5, local copies, waits for them, and re-layouts: 14.2 us -> 2.92 us  [own_part(): lax.dynamic_slice_in_dim(whole_array, fsdp_index * piece_size, piece_size...]
    ppermute x24, waiting for transfers between devices: 82.8 us -> 71.7 us  [across(): return lax.ppermute(block, 'seq', [(i, i ^ 1) for i in range(8)])]
    dot_general x55 -> x50, matrix products: 158 us -> 164 us  [dot(): lax.dot_general(left, right, (((left_dim,), (right_dim,)), ((), ())), pre...]
    ppermute x19 -> x21, waiting for transfers between devices: 121 us -> 117 us  [to_chip(): return lax.ppermute(block, 'fsdp', [(i, i ^ 2) for i in range(4)])]
  transfers between devices with their start and end apart: 108 -> 112, of which waited for: 43 -> 46; matrix products, arithmetic and copies ran while one was open for 45% -> 42% of each run, Pallas kernels for 0% -> 3%
where the time goes in v4:
time: 1070 us; the launch traced here: 1060 us
  waiting for transfers between devices  373 us (35%)
  matrix products  274 us (26%)
  local copies, waits for them, and re-layouts  139 us (13%)
  starting transfers between devices  137 us (13%)
  other arithmetic  90.3 us (8%)
  Pallas kernels  29.8 us (3%)
  between operations  17.1 us (2%)
    ppermute x30, waiting for transfers between devices, along(): return lax.ppermute(block, 'seq', route)  172 us
    dot_general x50, matrix products, dot(): lax.dot_general(left, right, (((left_dim,), (right_dim,)), ((), ())), pre...  164 us
    ppermute x21, waiting for transfers between devices, to_chip(): return lax.ppermute(block, 'fsdp', [(i, i ^ 2) for i in range(4)])  117 us
    dot_general x7, matrix products, einsum(): return jnp.einsum(form, left, right, preferred_element_type=F32)  110 us
    ppermute x30, starting transfers between devices, along(): return lax.ppermute(block, 'seq', route)  72.3 us
    ppermute x24, waiting for transfers between devices, across(): return lax.ppermute(block, 'seq', [(i, i ^ 1) for i in range(8)])  71.7 us
    ppermute x24, starting transfers between devices, across(): return lax.ppermute(block, 'seq', [(i, i ^ 1) for i in range(8)])  30.4 us
    dynamic_update_slice x28, local copies, waits for them, and re-layouts, place_rows(): return lax.dynamic_update_slice_in_dim(whole, piece, start, 0)  28.9 us
  transfers between devices with their start and end apart: 112, of which 46 were waited for; matrix products, arithmetic and copies ran while one was open for 42% of the time, Pallas kernels for 3%

profile of v4, /device:TPU:0, one launch (start us, length us, event | category | flops | bytes accessed | tf_op | source)
XLA Modules:
  0.0 1060.9 jit_solution(8438328161418407989)
XLA Ops:
  86.0 14.4 %collective-permute-done.15 = bf16[128,2880]{0,1:T(8,128)(2,1)S(1)} collective-permute-done((bf16[128,2880]{0,1:T(8,128)(2,1)S(1)}, bf16[128,2880]{0,1:T(8,128)(2,1)S(1)}, u32[]{:S(2)}, u32[]{:S(2)}) %collective-permute-start.15) | collective-permute-done | bytes 737312 | tf_op jit(solution)/shard_map/ppermute | solution.py:315
  114.8 12.0 %collective-permute-done.17 = bf16[128,2880]{0,1:T(8,128)(2,1)S(1)} collective-permute-done((bf16[128,2880]{0,1:T(8,128)(2,1)S(1)}, bf16[128,2880]{0,1:T(8,128)(2,1)S(1)}, u32[]{:S(2)}, u32[]{:S(2)}) %collective-permute-start.17) | collective-permute-done | bytes 737312 | tf_op jit(solution)/shard_map/ppermute | solution.py:319
  132.5 14.4 %shard_map.348 = (bf16[1024,640]{1,0:T(8,128)(2,1)}, bf16[1024,512]{1,0:T(8,128)(2,1)}) custom-call(s32[3]{0:T(128)} %bitcast.401, f32[8]{0:T(128)} %select_reduce_fusion.1.sinks_ref, f32[1024,640]{1,0:T(8,128)} %copy-done.8, f32[1024,640]{1,0:T(8,128)} %copy-done.8, f32[1024,128]{1,0:T(8,128)} %get-tuple-element.682.cos_ref.cos_before_ref, ...), custom_call_target="tpu_custom_call" | custom-call | flops 671088640 | bytes 6553600 | tf_op jit(solution)/shard_map/pallas_call | solution.py:122
  160.0 14.4 %collective-permute-done.21 = bf16[128,2880]{0,1:T(8,128)(2,1)S(1)} collective-permute-done((bf16[128,2880]{0,1:T(8,128)(2,1)S(1)}, bf16[128,2880]{0,1:T(8,128)(2,1)S(1)}, u32[]{:S(2)}, u32[]{:S(2)}) %collective-permute-start.21) | collective-permute-done | bytes 737312 | tf_op jit(solution)/shard_map/ppermute | solution.py:319
  181.2 12.9 %collective-permute-done.22 = bf16[128,2880]{0,1:T(8,128)(2,1)S(1)} collective-permute-done((bf16[128,2880]{0,1:T(8,128)(2,1)S(1)}, bf16[128,2880]{0,1:T(8,128)(2,1)S(1)}, u32[]{:S(2)}, u32[]{:S(2)}) %collective-permute-start.22) | collective-permute-done | bytes 737312 | tf_op jit(solution)/shard_map/ppermute | solution.py:315
  203.2 10.5 collective-permute-done.24
  228.4 9.4 collective-permute-done.27
  274.6 11.1 %collective-permute-done.34 = bf16[128,2944]{0,1:T(8,128)(2,1)S(1)} collective-permute-done((bf16[128,2944]{0,1:T(8,128)(2,1)S(1)}, bf16[128,2944]{0,1:T(8,128)(2,1)S(1)}, u32[]{:S(2)}, u32[]{:S(2)}) %collective-permute-start.34) | collective-permute-done | bytes 753696 | tf_op jit(solution)/shard_map/ppermute | solution.py:315
  296.0 24.7 %collective-permute-done.36 = bf16[128,2944]{0,1:T(8,128)(2,1)S(1)} collective-permute-done((bf16[128,2944]{0,1:T(8,128)(2,1)S(1)}, bf16[128,2944]{0,1:T(8,128)(2,1)S(1)}, u32[]{:S(2)}, u32[]{:S(2)}) %collective-permute-start.36) | collective-permute-done | bytes 753696 | tf_op jit(solution)/shard_map/ppermute | solution.py:315
  325.1 16.1 %collective-permute-done.40 = bf16[128,2944]{0,1:T(8,128)(2,1)S(1)} collective-permute-done((bf16[128,2944]{0,1:T(8,128)(2,1)S(1)}, bf16[128,2944]{0,1:T(8,128)(2,1)S(1)}, u32[]{:S(2)}, u32[]{:S(2)}) %collective-permute-start.40) | collective-permute-done | bytes 753696 | tf_op jit(solution)/shard_map/ppermute | solution.py:319
  351.3 16.1 %add_bitcast_fusion.1 = f32[2,1280,720]{1,2,0:T(8,128)S(1)} fusion(bf16[1280,2944]{1,0:T(8,128)(2,1)S(1)} %constant_dynamic-update-slice_fusion.38, bf16[2,720,2880]{2,1,0:T(8,128)(2,1)} %bitcast.403, f32[2,720]{1,0:T(2,128)S(1)} %bitcast_convert_fusion.7), kind=kOutput, calls=%fused_computation.33 | convolution fusion | flops 10854604800 | bytes 23209600 | tf_op jit(solution)/shard_map/rd,khd->krh/dot_general | solution.py:705
  395.9 16.5 %add_bitcast_fusion = f32[2,1280,720]{1,2,0:T(8,128)S(1)} fusion(bf16[1280,2944]{1,0:T(8,128)(2,1)S(1)} %constant_dynamic-update-slice_fusion.31, bf16[2,720,2880]{2,1,0:T(8,128)(2,1)} %bitcast.404, f32[2,720]{1,0:T(2,128)S(1)} %bitcast_convert_fusion.7), kind=kOutput, calls=%fused_computation.32 | convolution fusion | flops 10854604800 | bytes 23209600 | tf_op jit(solution)/shard_map/rd,khd->krh/dot_general | solution.py:705
  455.5 10.4 convolution_convert_fusion.2
  471.8 11.1 %collective-permute-done.56 = bf16[320,2944]{1,0:T(8,128)(2,1)} collective-permute-done((bf16[320,2944]{1,0:T(8,128)(2,1)S(1)}, bf16[320,2944]{1,0:T(8,128)(2,1)}, u32[]{:S(2)}, u32[]{:S(2)}) %collective-permute-start.56) | collective-permute-done | bytes 1884192 | tf_op jit(solution)/shard_map/ppermute | solution.py:431
  483.0 18.4 %fusion.106 = (bf16[1,1280,720]{1,2,0:T(8,128)(2,1)S(1)}, bf16[1,1280,720]{1,2,0:T(8,128)(2,1)}, f32[1280]{0:T(1024)S(1)}) fusion(f32[1280]{0:T(1024)S(1)} %reduce.3, f32[2,1280,720]{1,2,0:T(8,128)} %copy-done.26, bf16[1280,720]{0,1:T(8,128)(2,1)S(1)} %copy-done.66, bf16[1280,2944]{1,0:T(8,128)(2,1)} %constant_dynamic-update-slice_fusion.27, ...), kind=kOutput, calls=%fused_computation.187 | convolution fusion | flops 5467851776 | bytes 24596480 | tf_op jit(solution)/shard_map/dot_general | solution.py:25
  505.6 17.1 %bitcast_convert_fusion = bf16[1280,2944]{1,0:T(8,128)(2,1)} fusion(bf16[2,720,2880]{2,1,0:T(8,128)(2,1)} %bitcast.405, bf16[1,1280,720]{1,2,0:T(8,128)(2,1)S(1)} %copy-done.67, bf16[1,1280,720]{1,2,0:T(8,128)(2,1)S(1)} %get-tuple-element.546), kind=kOutput, calls=%fused_computation | convolution fusion | flops 10858373120 | bytes 19517440 | tf_op jit(solution)/shard_map/krh,khd->rd/dot_general | solution.py:705
  522.7 21.7 %collective-permute-done.57 = bf16[320,2944]{1,0:T(8,128)(2,1)} collective-permute-done((bf16[320,2944]{1,0:T(8,128)(2,1)}, bf16[320,2944]{1,0:T(8,128)(2,1)}, u32[]{:S(2)}, u32[]{:S(2)}) %collective-permute-start.57) | collective-permute-done | bytes 1884192 | tf_op jit(solution)/shard_map/ppermute | solution.py:431
  563.4 16.6 %fusion.105 = (bf16[1,1280,720]{1,2,0:T(8,128)(2,1)S(1)}, bf16[1,1280,720]{1,2,0:T(8,128)(2,1)}, f32[1280]{0:T(1024)S(1)}) fusion(f32[1280]{0:T(1024)S(1)} %reduce.4, f32[2,1280,720]{1,2,0:T(8,128)S(1)} %bitcast.375, bf16[1280,720]{0,1:T(8,128)(2,1)S(1)} %copy-done.65, bf16[1280,2944]{1,0:T(8,128)(2,1)S(1)} %constant_dynamic-update-slice_fusion.24, ...), kind=kOutput, calls=%fused_computation.186 | convolution fusion | flops 5467851776 | bytes 24596480 | tf_op jit(solution)/shard_map/dot_general | solution.py:25
  585.9 10.6 bitcast_convert_fusion.2
  605.5 10.9 %bitcast_convert_fusion.1 = bf16[640,2944]{1,0:T(8,128)(2,1)} fusion(bf16[2,720,2880]{2,1,0:T(8,128)(2,1)} %bitcast.407, bf16[2,1280,720]{1,2,0:T(8,128)(2,1)} %copy-done.11), kind=kOutput, calls=%fused_computation.15 | convolution fusion | flops 5428264960 | bytes 14090240 | tf_op jit(solution)/shard_map/krh,khd->rd/dot_general | solution.py:705
  626.5 17.4 %fusion = f32[2,720,2880]{2,1,0:T(8,128)} fusion(bf16[2,1280,720]{1,2,0:T(8,128)(2,1)S(1)} %copy-done.12, bf16[1280,2944]{1,0:T(8,128)(2,1)} %copy-done.21), kind=kOutput, calls=%fused_computation.12 | convolution fusion | flops 10616832000 | bytes 27811840 | tf_op jit(solution)/shard_map/krh,rd->khd/dot_general | solution.py:705
  643.8 21.6 %convolution_add_fusion = f32[2,720,2880]{2,1,0:T(8,128)} fusion(f32[2,720,2880]{2,1,0:T(8,128)} %fusion, bf16[2,1280,720]{1,2,0:T(8,128)(2,1)} %pad_maximum_fusion, bf16[1280,2944]{1,0:T(8,128)(2,1)} %copy-done.20), kind=kOutput, calls=%fused_computation.11 | convolution fusion | flops 10620979200 | bytes 44400640 | tf_op jit(solution)/shard_map/krh,rd->khd/dot_general | solution.py:705
  690.7 11.5 %fusion.17 = f32[720,2880]{1,0:T(8,128)} fusion(f32[720,2880]{1,0:T(8,128)S(1)} %fusion.7, bf16[1280,720]{0,1:T(8,128)(2,1)S(1)} %copy-done.62, bf16[1280,2944]{1,0:T(8,128)(2,1)} %constant_dynamic-update-slice_fusion.27), kind=kOutput, calls=%fused_computation.39 | convolution fusion | flops 5310489600 | bytes 25968640 | tf_op jit(solution)/shard_map/dot_general | solution.py:25
  713.1 10.4 collective-permute-done.68
  753.3 15.4 %collective-permute-done.69 = bf16[128,2944]{0,1:T(8,128)(2,1)} collective-permute-done((bf16[128,2944]{0,1:T(8,128)(2,1)}, bf16[128,2944]{0,1:T(8,128)(2,1)}, u32[]{:S(2)}, u32[]{:S(2)}) %collective-permute-start.69) | collective-permute-done | bytes 753696 | tf_op jit(solution)/shard_map/ppermute | solution.py:315
  780.8 9.7 collective-permute-done.72
  828.0 10.8 %collective-permute-done.80 = bf16[128,2880]{0,1:T(8,128)(2,1)S(1)} collective-permute-done((bf16[128,2880]{0,1:T(8,128)(2,1)}, bf16[128,2880]{0,1:T(8,128)(2,1)S(1)}, u32[]{:S(2)}, u32[]{:S(2)}) %collective-permute-start.80) | collective-permute-done | bytes 737312 | tf_op jit(solution)/shard_map/ppermute | solution.py:315
  858.0 13.1 %collective-permute-done.86 = bf16[128,2880]{0,1:T(8,128)(2,1)S(1)} collective-permute-done((bf16[128,2880]{0,1:T(8,128)(2,1)S(1)}, bf16[128,2880]{0,1:T(8,128)(2,1)S(1)}, u32[]{:S(2)}, u32[]{:S(2)}) %collective-permute-start.86) | collective-permute-done | bytes 737312 | tf_op jit(solution)/shard_map/ppermute | solution.py:319
  882.9 15.4 %shard_map.349 = (bf16[1024,640]{1,0:T(8,128)(2,1)}, f32[8,640]{1,0:T(8,128)}, f32[8,128]{1,0:T(8,128)}) custom-call(s32[3]{0:T(128)} %bitcast.402, f32[8]{0:T(128)} %select_reduce_fusion.1.sinks_ref, bf16[1024,640]{1,0:T(8,128)(2,1)} %get-tuple-element.358.turned_ref.before_ref, bf16[1024,640]{1,0:T(8,128)(2,1)} %get-tuple-element.358.turned_ref.before_ref, ...), custom_call_target="tpu_custom_call" | custom-call | flops 1677721600 | bytes 6553600 | tf_op jit(solution)/shard_map/pallas_call | solution.py:204
  958.7 17.1 %collective-permute-done.96 = bf16[2880,128]{1,0:T(8,128)(2,1)S(1)} collective-permute-done((bf16[2880,128]{1,0:T(8,128)(2,1)S(1)}, bf16[2880,128]{1,0:T(8,128)(2,1)S(1)}, u32[]{:S(2)}, u32[]{:S(2)}) %collective-permute-start.96) | collective-permute-done | bytes 737312 | tf_op jit(solution)/shard_map/ppermute | solution.py:431
  977.1 13.5 %collective-permute-done.104 = bf16[128,2880]{0,1:T(8,128)(2,1)S(1)} collective-permute-done((bf16[128,2880]{0,1:T(8,128)(2,1)S(1)}, bf16[128,2880]{0,1:T(8,128)(2,1)S(1)}, u32[]{:S(2)}, u32[]{:S(2)}) %collective-permute-start.104) | collective-permute-done | bytes 737312 | tf_op jit(solution)/shard_map/ppermute | solution.py:431
  1002.8 16.5 %collective-permute-done.105 = f32[2,2880]{1,0:T(2,128)S(1)} collective-permute-done((f32[2,2880]{1,0:T(2,128)S(1)}, f32[2,2880]{1,0:T(2,128)S(1)}, u32[]{:S(2)}, u32[]{:S(2)}) %collective-permute-start.105) | collective-permute-done | bytes 23072 | tf_op jit(solution)/shard_map/ppermute | solution.py:431
  (822 shorter events, 582.4 us)
Async XLA Ops:
  7.2 424.7 %all-gather.2.cloned.1.call-start = ((), (), s32[]{:S(2)}) async-start(), calls=%async_computation.2 | async-start | bytes 6782976 | tf_op jit(solution)/shard_map/all_gather | solution.py:419
  33.2 41.4 %collective-permute-start.12 = (bf16[128,2880]{0,1:T(8,128)(2,1)}, bf16[128,2880]{0,1:T(8,128)(2,1)}, u32[]{:S(2)}, u32[]{:S(2)}) collective-permute-start(bf16[128,2880]{0,1:T(8,128)(2,1)} %collective-permute-done), channel_id=1, source_target_pairs={{8,16},{12,20},{16,24},{20,28},{9,17},{13,21},{17,25},{21,29},{10,... | collective-permute-start | bytes 2211848 | tf_op jit(solution)/shard_map/ppermute | solution.py:315
  34.8 39.8 %collective-permute-start.13 = (bf16[128,2880]{0,1:T(8,128)(2,1)}, bf16[128,2880]{0,1:T(8,128)(2,1)}, u32[]{:S(2)}, u32[]{:S(2)}) collective-permute-start(bf16[128,2880]{0,1:T(8,128)(2,1)} %collective-permute-done.1), channel_id=1, source_target_pairs={{16,8},{20,12},{8,0},{12,4},{17,9},{21,13},{9,1},{13,5},{18,10},{2... | collective-permute-start | bytes 2211848 | tf_op jit(solution)/shard_map/ppermute | solution.py:315
  39.6 43.7 %collective-permute-start.6 = (bf16[2880,128]{1,0:T(8,128)(2,1)}, bf16[2880,128]{1,0:T(8,128)(2,1)}, u32[]{:S(2)}, u32[]{:S(2)}) collective-permute-start(bf16[2880,128]{1,0:T(8,128)(2,1)} %param.24), channel_id=1, source_target_pairs={{0,1},{1,0},{2,3},{3,2},{4,5},{5,4},{6,7},{7,6},{8,9},{9,8},{10,11... | collective-permute-start | bytes 2211848 | tf_op jit(solution)/shard_map/ppermute | solution.py:427
  55.4 26.1 %collective-permute-start.7 = (bf16[2880,128]{1,0:T(8,128)(2,1)}, bf16[2880,128]{1,0:T(8,128)(2,1)}, u32[]{:S(2)}, u32[]{:S(2)}) collective-permute-start(bf16[2880,128]{1,0:T(8,128)(2,1)} %param.24), channel_id=1, source_target_pairs={{0,2},{1,3},{2,0},{3,1},{4,6},{5,7},{6,4},{7,5},{8,10},{9,11},{10,... | collective-permute-start | bytes 2211848 | tf_op jit(solution)/shard_map/ppermute | solution.py:431
  100.4 46.5 %collective-permute-start.18 = (bf16[2880,128]{1,0:T(8,128)(2,1)}, bf16[2880,128]{1,0:T(8,128)(2,1)}, u32[]{:S(2)}, u32[]{:S(2)}) collective-permute-start(bf16[2880,128]{1,0:T(8,128)(2,1)} %bitcast.15), channel_id=1, source_target_pairs={{0,1},{1,0},{2,3},{3,2},{4,5},{5,4},{6,7},{7,6},{8,9},{9,8},{10,11... | collective-permute-start | bytes 2211848 | tf_op jit(solution)/shard_map/ppermute | solution.py:427
  100.4 27.0 %collective-permute-start.19 = (bf16[2880,128]{1,0:T(8,128)(2,1)}, bf16[2880,128]{1,0:T(8,128)(2,1)}, u32[]{:S(2)}, u32[]{:S(2)}) collective-permute-start(bf16[2880,128]{1,0:T(8,128)(2,1)} %bitcast.15), channel_id=1, source_target_pairs={{0,2},{1,3},{2,0},{3,1},{4,6},{5,7},{6,4},{7,5},{8,10},{9,11},{10,... | collective-permute-start | bytes 2211848 | tf_op jit(solution)/shard_map/ppermute | solution.py:431
  286.5 34.1 %collective-permute-start.38 = (bf16[160,2944]{1,0:T(8,128)(2,1)}, bf16[160,2944]{1,0:T(8,128)(2,1)}, u32[]{:S(2)}, u32[]{:S(2)}) collective-permute-start(bf16[160,2944]{1,0:T(8,128)(2,1)} %convolution_convert_fusion.16), channel_id=1, source_target_pairs={{0,1},{1,0},{2,3},{3,2},{4,5},{5,4},{6,7},{7,6},{8,9},{9,8},{10,11... | collective-permute-start | bytes 2826248 | tf_op jit(solution)/shard_map/ppermute | solution.py:427
  286.8 33.9 %collective-permute-start.39 = (bf16[160,2944]{1,0:T(8,128)(2,1)}, bf16[160,2944]{1,0:T(8,128)(2,1)}, u32[]{:S(2)}, u32[]{:S(2)}) collective-permute-start(bf16[160,2944]{1,0:T(8,128)(2,1)} %convolution_convert_fusion.16), channel_id=1, source_target_pairs={{0,2},{1,3},{2,0},{3,1},{4,6},{5,7},{6,4},{7,5},{8,10},{9,11},{10,... | collective-permute-start | bytes 2826248 | tf_op jit(solution)/shard_map/ppermute | solution.py:431
  288.3 328.1 %reduce-scatter.7.cloned.1.call-start = ((), (), s32[]{:S(2)}) async-start(), calls=%async_computation.3 | async-start | bytes 6782976
  289.9 30.7 %collective-permute-start.36 = (bf16[128,2944]{0,1:T(8,128)(2,1)S(1)}, bf16[128,2944]{0,1:T(8,128)(2,1)S(1)}, u32[]{:S(2)}, u32[]{:S(2)}) collective-permute-start(bf16[128,2944]{0,1:T(8,128)(2,1)S(1)} %get-tuple-element.268), channel_id=1, source_target_pairs={{16,24},{20,28},{8,0},{12,4},{17,25},{21,29},{9,1},{13,5},{18,26},... | collective-permute-start | bytes 2261000 | tf_op jit(solution)/shard_map/ppermute | solution.py:315
  291.4 29.3 %collective-permute-start.37 = (bf16[128,2944]{0,1:T(8,128)(2,1)S(1)}, bf16[128,2944]{0,1:T(8,128)(2,1)S(1)}, u32[]{:S(2)}, u32[]{:S(2)}) collective-permute-start(bf16[128,2944]{0,1:T(8,128)(2,1)S(1)} %get-tuple-element.269), channel_id=1, source_target_pairs={{0,4},{4,0},{8,12},{12,8},{16,20},{20,16},{24,28},{28,24},{1,5},{5... | collective-permute-start | bytes 2261000 | tf_op jit(solution)/shard_map/ppermute | solution.py:319
  344.1 37.7 %collective-permute-start.45 = (bf16[160,2944]{1,0:T(8,128)(2,1)S(1)}, bf16[160,2944]{1,0:T(8,128)(2,1)}, u32[]{:S(2)}, u32[]{:S(2)}) collective-permute-start(bf16[160,2944]{1,0:T(8,128)(2,1)S(1)} %convolution_convert_fusion.14), channel_id=1, source_target_pairs={{0,2},{1,3},{2,0},{3,1},{4,6},{5,7},{6,4},{7,5},{8,10},{9,11},{10,... | collective-permute-start | bytes 2826248 | tf_op jit(solution)/shard_map/ppermute | solution.py:431
  346.9 41.2 %collective-permute-start.46 = (bf16[160,2944]{1,0:T(8,128)(2,1)}, bf16[160,2944]{1,0:T(8,128)(2,1)}, u32[]{:S(2)}, u32[]{:S(2)}) collective-permute-start(bf16[160,2944]{1,0:T(8,128)(2,1)} %get-tuple-element.686), channel_id=1, source_target_pairs={{0,2},{1,3},{2,0},{3,1},{4,6},{5,7},{6,4},{7,5},{8,10},{9,11},{10,... | collective-permute-start | bytes 2826248 | tf_op jit(solution)/shard_map/ppermute | solution.py:431
  348.7 83.2 %collective-permute-start.52 = (bf16[640,1024]{1,0:T(8,128)(2,1)S(1)}, bf16[640,1024]{1,0:T(8,128)(2,1)}, u32[]{:S(2)}, u32[]{:S(2)}) collective-permute-start(bf16[640,1024]{1,0:T(8,128)(2,1)S(1)} %fusion.169), channel_id=1, source_target_pairs={{0,2},{1,3},{2,0},{3,1},{4,6},{5,7},{6,4},{7,5},{8,10},{9,11},{10,... | collective-permute-start | bytes 3932168 | tf_op jit(solution)/shard_map/ppermute | solution.py:431
  395.1 36.8 %collective-permute-start.51 = (bf16[640,2944]{1,0:T(8,128)(2,1)S(1)}, bf16[640,2944]{1,0:T(8,128)(2,1)}, u32[]{:S(2)}, u32[]{:S(2)}) collective-permute-start(bf16[640,2944]{1,0:T(8,128)(2,1)S(1)} %slice.427), channel_id=1, source_target_pairs={{0,1},{1,0},{2,3},{3,2},{4,5},{5,4},{6,7},{7,6},{8,9},{9,8},{10,11... | collective-permute-start | bytes 11304968 | tf_op jit(solution)/shard_map/ppermute | solution.py:427
  431.4 24.1 %collective-permute-start.53 = (bf16[640,2944]{1,0:T(8,128)(2,1)}, bf16[640,2944]{1,0:T(8,128)(2,1)}, u32[]{:S(2)}, u32[]{:S(2)}) collective-permute-start(bf16[640,2944]{1,0:T(8,128)(2,1)} %slice.546), channel_id=1, source_target_pairs={{0,1},{1,0},{2,3},{3,2},{4,5},{5,4},{6,7},{7,6},{8,9},{9,8},{10,11... | collective-permute-start | bytes 11304968 | tf_op jit(solution)/shard_map/ppermute | solution.py:427
  439.3 26.6 %collective-permute-start.54 = (bf16[320,2944]{1,0:T(8,128)(2,1)S(1)}, bf16[320,2944]{1,0:T(8,128)(2,1)}, u32[]{:S(2)}, u32[]{:S(2)}) collective-permute-start(bf16[320,2944]{1,0:T(8,128)(2,1)S(1)} %slice.547), channel_id=1, source_target_pairs={{0,1},{1,0},{2,3},{3,2},{4,5},{5,4},{6,7},{7,6},{8,9},{9,8},{10,11... | collective-permute-start | bytes 5652488 | tf_op jit(solution)/shard_map/ppermute | solution.py:427
  439.4 43.5 %collective-permute-start.56 = (bf16[320,2944]{1,0:T(8,128)(2,1)S(1)}, bf16[320,2944]{1,0:T(8,128)(2,1)}, u32[]{:S(2)}, u32[]{:S(2)}) collective-permute-start(bf16[320,2944]{1,0:T(8,128)(2,1)S(1)} %slice.547), channel_id=1, source_target_pairs={{0,2},{1,3},{2,0},{3,1},{4,6},{5,7},{6,4},{7,5},{8,10},{9,11},{10,... | collective-permute-start | bytes 5652488 | tf_op jit(solution)/shard_map/ppermute | solution.py:431
  501.4 43.0 %collective-permute-start.57 = (bf16[320,2944]{1,0:T(8,128)(2,1)}, bf16[320,2944]{1,0:T(8,128)(2,1)}, u32[]{:S(2)}, u32[]{:S(2)}) collective-permute-start(bf16[320,2944]{1,0:T(8,128)(2,1)} %get-tuple-element.302), channel_id=1, source_target_pairs={{0,2},{1,3},{2,0},{3,1},{4,6},{5,7},{6,4},{7,5},{8,10},{9,11},{10,... | collective-permute-start | bytes 5652488 | tf_op jit(solution)/shard_map/ppermute | solution.py:431
  501.7 304.9 %reduce-scatter.9.cloned.1.call-start = ((), (), s32[]{:S(2)}) async-start(), calls=%async_computation.4 | async-start | bytes 6782976
  557.3 24.7 %collective-permute-start.60 = (bf16[640,2944]{1,0:T(8,128)(2,1)}, bf16[640,2944]{1,0:T(8,128)(2,1)S(1)}, u32[]{:S(2)}, u32[]{:S(2)}) collective-permute-start(bf16[640,2944]{1,0:T(8,128)(2,1)} %slice.437), channel_id=1, source_target_pairs={{0,1},{1,0},{2,3},{3,2},{4,5},{5,4},{6,7},{7,6},{8,9},{9,8},{10,11... | collective-permute-start | bytes 11304968 | tf_op jit(solution)/shard_map/ppermute | solution.py:427
  624.9 43.8 %collective-permute-start.64 = (bf16[320,2944]{1,0:T(8,128)(2,1)}, bf16[320,2944]{1,0:T(8,128)(2,1)}, u32[]{:S(2)}, u32[]{:S(2)}) collective-permute-start(bf16[320,2944]{1,0:T(8,128)(2,1)} %get-tuple-element.563), channel_id=1, source_target_pairs={{0,2},{1,3},{2,0},{3,1},{4,6},{5,7},{6,4},{7,5},{8,10},{9,11},{10,... | collective-permute-start | bytes 5652488 | tf_op jit(solution)/shard_map/ppermute | solution.py:431
  677.9 30.6 %collective-permute-start.65 = (bf16[128,2944]{0,1:T(8,128)(2,1)}, bf16[128,2944]{0,1:T(8,128)(2,1)}, u32[]{:S(2)}, u32[]{:S(2)}) collective-permute-start(bf16[128,2944]{0,1:T(8,128)(2,1)} %constant_dynamic-slice_fusion.16), channel_id=1, source_target_pairs={{0,4},{4,0},{8,12},{12,8},{16,20},{20,16},{24,28},{28,24},{1,5},{5... | collective-permute-start | bytes 2261000 | tf_op jit(solution)/shard_map/ppermute | solution.py:319
  680.9 42.6 %collective-permute-start.68 = (bf16[320,2944]{1,0:T(8,128)(2,1)}, bf16[320,2944]{1,0:T(8,128)(2,1)}, u32[]{:S(2)}, u32[]{:S(2)}) collective-permute-start(bf16[320,2944]{1,0:T(8,128)(2,1)} %get-tuple-element.343), channel_id=1, source_target_pairs={{0,2},{1,3},{2,0},{3,1},{4,6},{5,7},{6,4},{7,5},{8,10},{9,11},{10,... | collective-permute-start | bytes 5652488 | tf_op jit(solution)/shard_map/ppermute | solution.py:431
  710.9 31.0 %collective-permute-start.66 = (bf16[128,2944]{0,1:T(8,128)(2,1)}, bf16[128,2944]{0,1:T(8,128)(2,1)}, u32[]{:S(2)}, u32[]{:S(2)}) collective-permute-start(bf16[128,2944]{0,1:T(8,128)(2,1)} %fusion.130), channel_id=1, source_target_pairs={{0,8},{4,12},{24,16},{28,20},{1,9},{5,13},{25,17},{29,21},{2,10},{... | collective-permute-start | bytes 2261000 | tf_op jit(solution)/shard_map/ppermute | solution.py:315
  713.0 28.8 %collective-permute-start.67 = (bf16[128,2944]{0,1:T(8,128)(2,1)}, bf16[128,2944]{0,1:T(8,128)(2,1)}, u32[]{:S(2)}, u32[]{:S(2)}) collective-permute-start(bf16[128,2944]{0,1:T(8,128)(2,1)} %get-tuple-element.342), channel_id=1, source_target_pairs={{0,4},{4,0},{8,12},{12,8},{16,20},{20,16},{24,28},{28,24},{1,5},{5... | collective-permute-start | bytes 2261000 | tf_op jit(solution)/shard_map/ppermute | solution.py:319
  952.3 38.9 %collective-permute-start.93 = (bf16[128,2880]{0,1:T(8,128)(2,1)S(1)}, bf16[128,2880]{0,1:T(8,128)(2,1)S(1)}, u32[]{:S(2)}, u32[]{:S(2)}) collective-permute-start(bf16[128,2880]{0,1:T(8,128)(2,1)S(1)} %select_convert_fusion.3), channel_id=1, source_target_pairs={{0,8},{4,12},{8,16},{12,20},{1,9},{5,13},{9,17},{13,21},{2,10},{6,... | collective-permute-start | bytes 2211848 | tf_op jit(solution)/shard_map/ppermute | solution.py:315
  954.4 36.8 %collective-permute-start.94 = (bf16[128,2880]{0,1:T(8,128)(2,1)S(1)}, bf16[128,2880]{0,1:T(8,128)(2,1)S(1)}, u32[]{:S(2)}, u32[]{:S(2)}) collective-permute-start(bf16[128,2880]{0,1:T(8,128)(2,1)S(1)} %select_convert_fusion.3), channel_id=1, source_target_pairs={{24,16},{28,20},{16,8},{20,12},{25,17},{29,21},{17,9},{21,13},{26,... | collective-permute-start | bytes 2211848 | tf_op jit(solution)/shard_map/ppermute | solution.py:315
  955.2 36.0 %collective-permute-start.95 = (bf16[128,2880]{0,1:T(8,128)(2,1)S(1)}, bf16[128,2880]{0,1:T(8,128)(2,1)S(1)}, u32[]{:S(2)}, u32[]{:S(2)}) collective-permute-start(bf16[128,2880]{0,1:T(8,128)(2,1)S(1)} %copy-done.83), channel_id=1, source_target_pairs={{0,4},{4,0},{8,12},{12,8},{16,20},{20,16},{24,28},{28,24},{1,5},{5... | collective-permute-start | bytes 2211848 | tf_op jit(solution)/shard_map/ppermute | solution.py:319
  957.2 33.4 %collective-permute-start.104 = (bf16[128,2880]{0,1:T(8,128)(2,1)S(1)}, bf16[128,2880]{0,1:T(8,128)(2,1)S(1)}, u32[]{:S(2)}, u32[]{:S(2)}) collective-permute-start(bf16[128,2880]{0,1:T(8,128)(2,1)S(1)} %fusion.146), channel_id=1, source_target_pairs={{0,2},{1,3},{2,0},{3,1},{4,6},{5,7},{6,4},{7,5},{8,10},{9,11},{10,... | collective-permute-start | bytes 2211848 | tf_op jit(solution)/shard_map/ppermute | solution.py:431
  992.1 27.3 %collective-permute-start.97 = (bf16[128,2880]{0,1:T(8,128)(2,1)S(1)}, bf16[128,2880]{0,1:T(8,128)(2,1)S(1)}, u32[]{:S(2)}, u32[]{:S(2)}) collective-permute-start(bf16[128,2880]{0,1:T(8,128)(2,1)S(1)} %get-tuple-element.603), channel_id=1, source_target_pairs={{0,8},{4,12},{8,16},{12,20},{16,24},{20,28},{1,9},{5,13},{9,17},{1... | collective-permute-start | bytes 2211848 | tf_op jit(solution)/shard_map/ppermute | solution.py:315
  (211 other events, 2669.1 us)
Sparse Core Ops, SparseCore 0:
  288.4 107.1 all-gather.1
  501.8 113.4 reduce-scatter.6
  619.5 139.4 reduce-scatter.8

commit v5 on v4

--- a/solution.py
+++ b/solution.py
@@ -529,9 +529,18 @@
         axis=0,
     )
     work.pool["small"] = to_core(small), to_chip(small)
-    work.pool["wo"] = output_matrix.T
-
-    def parameters(query_matrix, key_matrix, value_matrix):
+
+    def gather_columns(local):
+        whole = lax.all_gather(local, "fsdp", axis=1, tiled=True)
+        size = local.shape[1]
+        pieces = [whole[:, at * size : (at + 1) * size] for at in range(fsdp_count)]
+        return jnp.concatenate(in_order(pieces), axis=1)
+
+    w_query, wo_t = gather_columns(query_matrix), gather_columns(output_matrix.T)
+    if not shared_kv:
+        kv_all = lax.all_gather(jnp.stack([key_matrix.T, value_matrix.T]), "fsdp", axis=1, tiled=True)
+
+    def parameters():
         small_core, small_chip = work.pool["small"]
         small_all = jnp.stack(in_order([small, small_core, small_chip, to_core(small_chip)]))
         wide = jnp.swapaxes(small_all, 0, 1).reshape(small.shape[0], width).astype(F32)
@@ -550,7 +559,6 @@
         q_bias = jnp.concatenate(
             [lax.dynamic_slice_in_dim(q_bias, at, 1, 0)[0] for at in near_first]
         )
-        w_query = jnp.concatenate(from_all(query_matrix), axis=1)
         if shared_kv:
 
             def own_head(piece):
@@ -561,11 +569,7 @@
             k_bias = own_head(key_bias_vector).astype(F32)
             v_bias = own_head(value_bias_vector).astype(F32)
         else:
-            kv_pieces = in_order(from_all(jnp.concatenate([key_matrix.T, value_matrix.T], axis=0)))
-            w_pair = jnp.concatenate(
-                [piece[:kv_part] for piece in kv_pieces] + [piece[kv_part:] for piece in kv_pieces],
-                axis=0,
-            )
+            w_pair = kv_all.reshape(2 * HEAD_DIM, width)
         lin_bias = jnp.concatenate([q_bias, k_bias, v_bias])
         return (
             attn_gain_f,
@@ -575,12 +579,11 @@
             router_t,
             sinks_f,
             router_bias_f,
-            w_query,
             w_pair,
             lin_bias,
         )
 
-    work.add("parameters", parameters, query_matrix, key_matrix, value_matrix)
+    work.add("parameters", parameters)
 
     columns = jnp.concatenate(
         [
@@ -609,9 +612,8 @@
     line.gather(
         layer_input[0],
         lambda at, pair: (work.take("parameters"), arrive(at, pair))[1],
-        pools=(("small",), (), ("wo",), ()),
-    )
-    wo_t = jnp.concatenate(from_all(work.pool["wo"]), axis=1)
+        pools=(("small",), (), (), ()),
+    )
     (
         attn_gain_f,
         ffn_gain_f,
@@ -620,7 +622,6 @@
         router_t,
         sinks_f,
         router_bias_f,
-        w_query,
         w_pair,
         lin_bias,
     ) = work.take("parameters")

time: 1070 us -> 1050 us (0.981)
  local copies, waits for them, and re-layouts: 139 us -> 111 us
  blocking collectives: 0 us -> 12.9 us
    all_gather x0 -> x1, blocking collectives: none -> 12.9 us  [per_device(): lax.all_gather(jnp.stack([key_matrix.T, value_matrix.T]), 'fsdp', axis=1,...]
    ppermute x21 -> x18, waiting for transfers between devices: 117 us -> 105 us  [to_chip(): return lax.ppermute(block, 'fsdp', [(i, i ^ 2) for i in range(4)])]
    unnamed x269 -> x301, local copies, waits for them, and re-layouts: 25.8 us -> 17.8 us
    ppermute x21 -> x18, starting transfers between devices: 21.4 us -> 20.5 us  [to_chip(): return lax.ppermute(block, 'fsdp', [(i, i ^ 2) for i in range(4)])]
  transfers between devices with their start and end apart: 112 -> 105, of which waited for: 46 -> 47; matrix products, arithmetic and copies ran while one was open for 42% -> 40% of each run, Pallas kernels for 3% -> 3%
where the time goes in v5:
time: 1050 us; the launch traced here: 1040 us
  waiting for transfers between devices  378 us (36%)
  matrix products  274 us (26%)
  starting transfers between devices  127 us (12%)
  local copies, waits for them, and re-layouts  111 us (11%)
  other arithmetic  92.7 us (9%)
  Pallas kernels  30.1 us (3%)
  between operations  17.3 us (2%)
  blocking collectives  12.9 us (1%)
    ppermute x30, waiting for transfers between devices, along(): return lax.ppermute(block, 'seq', route)  180 us
    dot_general x50, matrix products, dot(): lax.dot_general(left, right, (((left_dim,), (right_dim,)), ((), ())), pre...  164 us
    dot_general x7, matrix products, einsum(): return jnp.einsum(form, left, right, preferred_element_type=F32)  110 us
    ppermute x18, waiting for transfers between devices, to_chip(): return lax.ppermute(block, 'fsdp', [(i, i ^ 2) for i in range(4)])  105 us
    ppermute x24, waiting for transfers between devices, across(): return lax.ppermute(block, 'seq', [(i, i ^ 1) for i in range(8)])  79.7 us
    ppermute x30, starting transfers between devices, along(): return lax.ppermute(block, 'seq', route)  74.2 us
    dynamic_update_slice x28, local copies, waits for them, and re-layouts, place_rows(): return lax.dynamic_update_slice_in_dim(whole, piece, start, 0)  28.1 us
  transfers between devices with their start and end apart: 105, of which 47 were waited for; matrix products, arithmetic and copies ran while one was open for 40% of the time, Pallas kernels for 3%

profile of v5, /device:TPU:0, one launch (start us, length us, event | category | flops | bytes accessed | tf_op | source)
XLA Modules:
  0.0 1043.6 jit_solution(1791496873140904119)
XLA Ops:
  29.7 12.9 %all_gather.13 = bf16[2,64,2880]{2,1,0:T(8,128)(2,1)S(1)} all-gather(bf16[2,16,2880]{2,1,0:T(8,128)(2,1)S(1)} %pad_maximum_fusion.16), channel_id=1, replica_groups=mesh['seq'=8,'fsdp'=4] {'fsdp'}, dimensions={1}, use_global_device_ids=true | all-gather | bytes 921600 | tf_op jit(solution)/shard_map/all_gather | solution.py:541
  53.1 15.2 %collective-permute-done.7 = bf16[128,2880]{0,1:T(8,128)(2,1)} collective-permute-done((bf16[128,2880]{0,1:T(8,128)(2,1)S(1)}, bf16[128,2880]{0,1:T(8,128)(2,1)}, u32[]{:S(2)}, u32[]{:S(2)}) %collective-permute-start.7) | collective-permute-done | bytes 737312 | tf_op jit(solution)/shard_map/ppermute | solution.py:315
  74.2 19.5 %collective-permute-done.9 = bf16[128,2880]{0,1:T(8,128)(2,1)S(1)} collective-permute-done((bf16[128,2880]{0,1:T(8,128)(2,1)S(1)}, bf16[128,2880]{0,1:T(8,128)(2,1)S(1)}, u32[]{:S(2)}, u32[]{:S(2)}) %collective-permute-start.9) | collective-permute-done | bytes 737312 | tf_op jit(solution)/shard_map/ppermute | solution.py:315
  95.5 15.9 %collective-permute-done.11 = bf16[128,2880]{0,1:T(8,128)(2,1)S(1)} collective-permute-done((bf16[128,2880]{0,1:T(8,128)(2,1)S(1)}, bf16[128,2880]{0,1:T(8,128)(2,1)S(1)}, u32[]{:S(2)}, u32[]{:S(2)}) %collective-permute-start.11) | collective-permute-done | bytes 737312 | tf_op jit(solution)/shard_map/ppermute | solution.py:319
  129.9 14.7 %shard_map.348 = (bf16[1024,640]{1,0:T(8,128)(2,1)}, bf16[1024,512]{1,0:T(8,128)(2,1)}) custom-call(s32[3]{0:T(128)} %bitcast.400, f32[8]{0:T(128)} %select_reduce_fusion.1.sinks_ref, f32[1024,640]{1,0:T(8,128)} %copy-done.7, f32[1024,640]{1,0:T(8,128)} %copy-done.7, f32[1024,128]{1,0:T(8,128)} %get-tuple-element.670.cos_ref.cos_before_ref, ...), custom_call_target="tpu_custom_call" | custom-call | flops 671088640 | bytes 6553600 | tf_op jit(solution)/shard_map/pallas_call | solution.py:122
  153.2 13.8 %collective-permute-done.12 = bf16[128,2880]{0,1:T(8,128)(2,1)S(1)} collective-permute-done((bf16[128,2880]{0,1:T(8,128)(2,1)}, bf16[128,2880]{0,1:T(8,128)(2,1)S(1)}, u32[]{:S(2)}, u32[]{:S(2)}) %collective-permute-start.12) | collective-permute-done | bytes 737312 | tf_op jit(solution)/shard_map/ppermute | solution.py:319
  172.2 11.1 %collective-permute-done.13 = bf16[128,2880]{0,1:T(8,128)(2,1)S(1)} collective-permute-done((bf16[128,2880]{0,1:T(8,128)(2,1)S(1)}, bf16[128,2880]{0,1:T(8,128)(2,1)S(1)}, u32[]{:S(2)}, u32[]{:S(2)}) %collective-permute-start.13) | collective-permute-done | bytes 737312 | tf_op jit(solution)/shard_map/ppermute | solution.py:315
  273.9 24.8 %collective-permute-done.27 = bf16[128,2944]{0,1:T(8,128)(2,1)S(1)} collective-permute-done((bf16[128,2944]{0,1:T(8,128)(2,1)S(1)}, bf16[128,2944]{0,1:T(8,128)(2,1)S(1)}, u32[]{:S(2)}, u32[]{:S(2)}) %collective-permute-start.27) | collective-permute-done | bytes 753696 | tf_op jit(solution)/shard_map/ppermute | solution.py:315
  302.4 17.1 %collective-permute-done.31 = bf16[128,2944]{0,1:T(8,128)(2,1)S(1)} collective-permute-done((bf16[128,2944]{0,1:T(8,128)(2,1)S(1)}, bf16[128,2944]{0,1:T(8,128)(2,1)S(1)}, u32[]{:S(2)}, u32[]{:S(2)}) %collective-permute-start.31) | collective-permute-done | bytes 753696 | tf_op jit(solution)/shard_map/ppermute | solution.py:319
  330.7 16.1 %add_bitcast_fusion.1 = f32[2,1280,720]{1,2,0:T(8,128)S(1)} fusion(bf16[1280,2944]{1,0:T(8,128)(2,1)S(1)} %constant_dynamic-update-slice_fusion.24, bf16[2,720,2880]{2,1,0:T(8,128)(2,1)} %bitcast.402, f32[2,720]{1,0:T(2,128)S(1)} %bitcast_convert_fusion.7), kind=kOutput, calls=%fused_computation.33 | convolution fusion | flops 10854604800 | bytes 23209600 | tf_op jit(solution)/shard_map/rd,khd->krh/dot_general | solution.py:706
  351.6 9.4 convolution_convert_fusion.1
  374.0 16.5 %add_bitcast_fusion = f32[2,1280,720]{1,2,0:T(8,128)S(1)} fusion(bf16[1280,2944]{1,0:T(8,128)(2,1)S(1)} %constant_dynamic-update-slice_fusion.17, bf16[2,720,2880]{2,1,0:T(8,128)(2,1)} %bitcast.403, f32[2,720]{1,0:T(2,128)S(1)} %bitcast_convert_fusion.7), kind=kOutput, calls=%fused_computation.32 | convolution fusion | flops 10854604800 | bytes 23209600 | tf_op jit(solution)/shard_map/rd,khd->krh/dot_general | solution.py:706
  395.8 9.4 convolution_convert_fusion
  434.1 10.4 convolution_convert_fusion.2
  450.4 10.6 %collective-permute-done.47 = bf16[320,2944]{1,0:T(8,128)(2,1)} collective-permute-done((bf16[320,2944]{1,0:T(8,128)(2,1)S(1)}, bf16[320,2944]{1,0:T(8,128)(2,1)}, u32[]{:S(2)}, u32[]{:S(2)}) %collective-permute-start.47) | collective-permute-done | bytes 1884192 | tf_op jit(solution)/shard_map/ppermute | solution.py:431
  461.1 18.4 %fusion.106 = (bf16[1,1280,720]{1,2,0:T(8,128)(2,1)S(1)}, bf16[1,1280,720]{1,2,0:T(8,128)(2,1)}, f32[1280]{0:T(1024)S(1)}) fusion(f32[1280]{0:T(1024)S(1)} %reduce.3, f32[2,1280,720]{1,2,0:T(8,128)} %copy-done.25, bf16[1280,720]{0,1:T(8,128)(2,1)S(1)} %copy-done.78, bf16[1280,2944]{1,0:T(8,128)(2,1)} %constant_dynamic-update-slice_fusion.13, ...), kind=kOutput, calls=%fused_computation.189 | convolution fusion | flops 5467851776 | bytes 24596480 | tf_op jit(solution)/shard_map/dot_general | solution.py:25
  484.9 17.1 %bitcast_convert_fusion = bf16[1280,2944]{1,0:T(8,128)(2,1)} fusion(bf16[2,720,2880]{2,1,0:T(8,128)(2,1)} %bitcast.404, bf16[1,1280,720]{1,2,0:T(8,128)(2,1)S(1)} %copy-done.79, bf16[1,1280,720]{1,2,0:T(8,128)(2,1)S(1)} %get-tuple-element.538), kind=kOutput, calls=%fused_computation | convolution fusion | flops 10858373120 | bytes 19517440 | tf_op jit(solution)/shard_map/krh,khd->rd/dot_general | solution.py:706
  502.0 20.5 %collective-permute-done.48 = bf16[320,2944]{1,0:T(8,128)(2,1)} collective-permute-done((bf16[320,2944]{1,0:T(8,128)(2,1)}, bf16[320,2944]{1,0:T(8,128)(2,1)}, u32[]{:S(2)}, u32[]{:S(2)}) %collective-permute-start.48) | collective-permute-done | bytes 1884192 | tf_op jit(solution)/shard_map/ppermute | solution.py:431
  542.7 16.6 %fusion.105 = (bf16[1,1280,720]{1,2,0:T(8,128)(2,1)S(1)}, bf16[1,1280,720]{1,2,0:T(8,128)(2,1)}, f32[1280]{0:T(1024)S(1)}) fusion(f32[1280]{0:T(1024)S(1)} %reduce.4, f32[2,1280,720]{1,2,0:T(8,128)S(1)} %bitcast.373, bf16[1280,720]{0,1:T(8,128)(2,1)S(1)} %copy-done.77, bf16[1280,2944]{1,0:T(8,128)(2,1)S(1)} %constant_dynamic-update-slice_fusion.10, ...), kind=kOutput, calls=%fused_computation.188 | convolution fusion | flops 5467851776 | bytes 24596480 | tf_op jit(solution)/shard_map/dot_general | solution.py:25
  566.3 10.4 bitcast_convert_fusion.2
  585.7 10.8 %bitcast_convert_fusion.1 = bf16[640,2944]{1,0:T(8,128)(2,1)} fusion(bf16[2,720,2880]{2,1,0:T(8,128)(2,1)} %bitcast.406, bf16[2,1280,720]{1,2,0:T(8,128)(2,1)} %copy-done.10), kind=kOutput, calls=%fused_computation.15 | convolution fusion | flops 5428264960 | bytes 14090240 | tf_op jit(solution)/shard_map/krh,khd->rd/dot_general | solution.py:706
  606.5 17.3 %fusion = f32[2,720,2880]{2,1,0:T(8,128)} fusion(bf16[2,1280,720]{1,2,0:T(8,128)(2,1)S(1)} %copy-done.11, bf16[1280,2944]{1,0:T(8,128)(2,1)} %copy-done.20), kind=kOutput, calls=%fused_computation.12 | convolution fusion | flops 10616832000 | bytes 27811840 | tf_op jit(solution)/shard_map/krh,rd->khd/dot_general | solution.py:706
  623.8 21.5 %convolution_add_fusion = f32[2,720,2880]{2,1,0:T(8,128)} fusion(f32[2,720,2880]{2,1,0:T(8,128)} %fusion, bf16[2,1280,720]{1,2,0:T(8,128)(2,1)} %pad_maximum_fusion, bf16[1280,2944]{1,0:T(8,128)(2,1)} %copy-done.19), kind=kOutput, calls=%fused_computation.11 | convolution fusion | flops 10620979200 | bytes 44400640 | tf_op jit(solution)/shard_map/krh,rd->khd/dot_general | solution.py:706
  667.1 11.7 %fusion.17 = f32[720,2880]{1,0:T(8,128)} fusion(f32[720,2880]{1,0:T(8,128)S(1)} %fusion.7, bf16[1280,720]{0,1:T(8,128)(2,1)S(1)} %copy-done.74, bf16[1280,2944]{1,0:T(8,128)(2,1)} %constant_dynamic-update-slice_fusion.13), kind=kOutput, calls=%fused_computation.39 | convolution fusion | flops 5310489600 | bytes 25968640 | tf_op jit(solution)/shard_map/dot_general | solution.py:25
  710.3 12.1 %collective-permute-done.57 = bf16[128,2944]{0,1:T(8,128)(2,1)} collective-permute-done((bf16[128,2944]{0,1:T(8,128)(2,1)}, bf16[128,2944]{0,1:T(8,128)(2,1)}, u32[]{:S(2)}, u32[]{:S(2)}) %collective-permute-start.57) | collective-permute-done | bytes 753696 | tf_op jit(solution)/shard_map/ppermute | solution.py:315
  735.9 11.6 %collective-permute-done.60 = bf16[128,2944]{0,1:T(8,128)(2,1)} collective-permute-done((bf16[128,2944]{0,1:T(8,128)(2,1)}, bf16[128,2944]{0,1:T(8,128)(2,1)}, u32[]{:S(2)}, u32[]{:S(2)}) %collective-permute-start.60) | collective-permute-done | bytes 753696 | tf_op jit(solution)/shard_map/ppermute | solution.py:315
  807.4 11.1 %collective-permute-done.71 = bf16[128,2880]{0,1:T(8,128)(2,1)S(1)} collective-permute-done((bf16[128,2880]{0,1:T(8,128)(2,1)}, bf16[128,2880]{0,1:T(8,128)(2,1)S(1)}, u32[]{:S(2)}, u32[]{:S(2)}) %collective-permute-start.71) | collective-permute-done | bytes 737312 | tf_op jit(solution)/shard_map/ppermute | solution.py:315
  836.4 13.4 %collective-permute-done.77 = bf16[128,2880]{0,1:T(8,128)(2,1)S(1)} collective-permute-done((bf16[128,2880]{0,1:T(8,128)(2,1)S(1)}, bf16[128,2880]{0,1:T(8,128)(2,1)S(1)}, u32[]{:S(2)}, u32[]{:S(2)}) %collective-permute-start.77) | collective-permute-done | bytes 737312 | tf_op jit(solution)/shard_map/ppermute | solution.py:319
  861.7 15.4 %shard_map.349 = (bf16[1024,640]{1,0:T(8,128)(2,1)}, f32[8,640]{1,0:T(8,128)}, f32[8,128]{1,0:T(8,128)}) custom-call(s32[3]{0:T(128)} %bitcast.401, f32[8]{0:T(128)} %select_reduce_fusion.1.sinks_ref, bf16[1024,640]{1,0:T(8,128)(2,1)} %get-tuple-element.350.turned_ref.before_ref, bf16[1024,640]{1,0:T(8,128)(2,1)} %get-tuple-element.350.turned_ref.before_ref, ...), custom_call_target="tpu_custom_call" | custom-call | flops 1677721600 | bytes 6553600 | tf_op jit(solution)/shard_map/pallas_call | solution.py:204
  941.0 17.1 %collective-permute-done.87 = bf16[2880,128]{1,0:T(8,128)(2,1)S(1)} collective-permute-done((bf16[2880,128]{1,0:T(8,128)(2,1)S(1)}, bf16[2880,128]{1,0:T(8,128)(2,1)S(1)}, u32[]{:S(2)}, u32[]{:S(2)}) %collective-permute-start.87) | collective-permute-done | bytes 737312 | tf_op jit(solution)/shard_map/ppermute | solution.py:431
  959.4 13.5 %collective-permute-done.95 = bf16[128,2880]{0,1:T(8,128)(2,1)S(1)} collective-permute-done((bf16[128,2880]{0,1:T(8,128)(2,1)S(1)}, bf16[128,2880]{0,1:T(8,128)(2,1)S(1)}, u32[]{:S(2)}, u32[]{:S(2)}) %collective-permute-start.95) | collective-permute-done | bytes 737312 | tf_op jit(solution)/shard_map/ppermute | solution.py:431
  985.6 16.6 %collective-permute-done.96 = f32[2,2880]{1,0:T(2,128)S(1)} collective-permute-done((f32[2,2880]{1,0:T(2,128)S(1)}, f32[2,2880]{1,0:T(2,128)S(1)}, u32[]{:S(2)}, u32[]{:S(2)}) %collective-permute-start.96) | collective-permute-done | bytes 23072 | tf_op jit(solution)/shard_map/ppermute | solution.py:431
  (836 shorter events, 553.7 us)
Async XLA Ops:
  7.2 105.7 %all-gather.4.cloned.1.call-start = ((), (), s32[]{:S(2)}) async-start(), calls=%async_computation.2 | async-start | bytes 3686400 | tf_op jit(solution)/shard_map/all_gather | solution.py:534
  8.0 136.7 %all-gather.6.cloned.1.call-start = ((), (), s32[]{:S(2)}) async-start(), calls=%async_computation.3 | async-start | bytes 3686400 | tf_op jit(solution)/shard_map/all_gather | solution.py:534
  8.0 35.4 %collective-permute-start = (bf16[128,2880]{0,1:T(8,128)(2,1)}, bf16[128,2880]{0,1:T(8,128)(2,1)}, u32[]{:S(2)}, u32[]{:S(2)}) collective-permute-start(bf16[128,2880]{0,1:T(8,128)(2,1)} %bitcast.365), channel_id=1, source_target_pairs={{0,8},{4,12},{8,16},{12,20},{16,24},{20,28},{1,9},{5,13},{9,17},{1... | collective-permute-start | bytes 2211848 | tf_op jit(solution)/shard_map/ppermute | solution.py:315
  13.9 29.5 %collective-permute-start.1 = (bf16[128,2880]{0,1:T(8,128)(2,1)}, bf16[128,2880]{0,1:T(8,128)(2,1)S(1)}, u32[]{:S(2)}, u32[]{:S(2)}) collective-permute-start(bf16[128,2880]{0,1:T(8,128)(2,1)} %bitcast.366), channel_id=1, source_target_pairs={{8,0},{12,4},{16,8},{20,12},{24,16},{28,20},{9,1},{13,5},{17,9},{2... | collective-permute-start | bytes 2211848 | tf_op jit(solution)/shard_map/ppermute | solution.py:315
  15.2 28.2 %collective-permute-start.2 = (bf16[128,2880]{0,1:T(8,128)(2,1)}, bf16[128,2880]{0,1:T(8,128)(2,1)}, u32[]{:S(2)}, u32[]{:S(2)}) collective-permute-start(bf16[128,2880]{0,1:T(8,128)(2,1)} %bitcast.367), channel_id=1, source_target_pairs={{0,4},{4,0},{8,12},{12,8},{16,20},{20,16},{24,28},{28,24},{1,5},{5... | collective-permute-start | bytes 2211848 | tf_op jit(solution)/shard_map/ppermute | solution.py:319
  25.7 384.3 %all-gather.8.cloned.1.call-start = ((), (), s32[]{:S(2)}) async-start(), calls=%async_computation.4 | async-start | bytes 6782976 | tf_op jit(solution)/shard_map/all_gather | solution.py:419
  69.9 23.9 %collective-permute-start.9 = (bf16[128,2880]{0,1:T(8,128)(2,1)S(1)}, bf16[128,2880]{0,1:T(8,128)(2,1)S(1)}, u32[]{:S(2)}, u32[]{:S(2)}) collective-permute-start(bf16[128,2880]{0,1:T(8,128)(2,1)S(1)} %get-tuple-element.229), channel_id=1, source_target_pairs={{16,24},{20,28},{8,0},{12,4},{17,25},{21,29},{9,1},{13,5},{18,26},... | collective-permute-start | bytes 2211848 | tf_op jit(solution)/shard_map/ppermute | solution.py:315
  266.5 32.3 %collective-permute-start.29 = (bf16[160,2944]{1,0:T(8,128)(2,1)}, bf16[160,2944]{1,0:T(8,128)(2,1)}, u32[]{:S(2)}, u32[]{:S(2)}) collective-permute-start(bf16[160,2944]{1,0:T(8,128)(2,1)} %convolution_convert_fusion.16), channel_id=1, source_target_pairs={{0,1},{1,0},{2,3},{3,2},{4,5},{5,4},{6,7},{7,6},{8,9},{9,8},{10,11... | collective-permute-start | bytes 2826248 | tf_op jit(solution)/shard_map/ppermute | solution.py:427
  266.7 32.1 %collective-permute-start.30 = (bf16[160,2944]{1,0:T(8,128)(2,1)}, bf16[160,2944]{1,0:T(8,128)(2,1)}, u32[]{:S(2)}, u32[]{:S(2)}) collective-permute-start(bf16[160,2944]{1,0:T(8,128)(2,1)} %convolution_convert_fusion.16), channel_id=1, source_target_pairs={{0,2},{1,3},{2,0},{3,1},{4,6},{5,7},{6,4},{7,5},{8,10},{9,11},{10,... | collective-permute-start | bytes 2826248 | tf_op jit(solution)/shard_map/ppermute | solution.py:431
  267.2 329.3 %reduce-scatter.7.cloned.1.call-start = ((), (), s32[]{:S(2)}) async-start(), calls=%async_computation.5 | async-start | bytes 6782976
  268.8 29.9 %collective-permute-start.27 = (bf16[128,2944]{0,1:T(8,128)(2,1)S(1)}, bf16[128,2944]{0,1:T(8,128)(2,1)S(1)}, u32[]{:S(2)}, u32[]{:S(2)}) collective-permute-start(bf16[128,2944]{0,1:T(8,128)(2,1)S(1)} %get-tuple-element.260), channel_id=1, source_target_pairs={{16,24},{20,28},{8,0},{12,4},{17,25},{21,29},{9,1},{13,5},{18,26},... | collective-permute-start | bytes 2261000 | tf_op jit(solution)/shard_map/ppermute | solution.py:315
  270.3 28.5 %collective-permute-start.28 = (bf16[128,2944]{0,1:T(8,128)(2,1)S(1)}, bf16[128,2944]{0,1:T(8,128)(2,1)S(1)}, u32[]{:S(2)}, u32[]{:S(2)}) collective-permute-start(bf16[128,2944]{0,1:T(8,128)(2,1)S(1)} %get-tuple-element.261), channel_id=1, source_target_pairs={{0,4},{4,0},{8,12},{12,8},{16,20},{20,16},{24,28},{28,24},{1,5},{5... | collective-permute-start | bytes 2261000 | tf_op jit(solution)/shard_map/ppermute | solution.py:319
  322.2 38.9 %collective-permute-start.36 = (bf16[160,2944]{1,0:T(8,128)(2,1)S(1)}, bf16[160,2944]{1,0:T(8,128)(2,1)}, u32[]{:S(2)}, u32[]{:S(2)}) collective-permute-start(bf16[160,2944]{1,0:T(8,128)(2,1)S(1)} %convolution_convert_fusion.14), channel_id=1, source_target_pairs={{0,2},{1,3},{2,0},{3,1},{4,6},{5,7},{6,4},{7,5},{8,10},{9,11},{10,... | collective-permute-start | bytes 2826248 | tf_op jit(solution)/shard_map/ppermute | solution.py:431
  326.2 40.0 %collective-permute-start.37 = (bf16[160,2944]{1,0:T(8,128)(2,1)}, bf16[160,2944]{1,0:T(8,128)(2,1)}, u32[]{:S(2)}, u32[]{:S(2)}) collective-permute-start(bf16[160,2944]{1,0:T(8,128)(2,1)} %get-tuple-element.674), channel_id=1, source_target_pairs={{0,2},{1,3},{2,0},{3,1},{4,6},{5,7},{6,4},{7,5},{8,10},{9,11},{10,... | collective-permute-start | bytes 2826248 | tf_op jit(solution)/shard_map/ppermute | solution.py:431
  326.8 83.2 %collective-permute-start.43 = (bf16[640,1024]{1,0:T(8,128)(2,1)S(1)}, bf16[640,1024]{1,0:T(8,128)(2,1)}, u32[]{:S(2)}, u32[]{:S(2)}) collective-permute-start(bf16[640,1024]{1,0:T(8,128)(2,1)S(1)} %fusion.173), channel_id=1, source_target_pairs={{0,2},{1,3},{2,0},{3,1},{4,6},{5,7},{6,4},{7,5},{8,10},{9,11},{10,... | collective-permute-start | bytes 3932168 | tf_op jit(solution)/shard_map/ppermute | solution.py:431
  373.2 36.8 %collective-permute-start.42 = (bf16[640,2944]{1,0:T(8,128)(2,1)S(1)}, bf16[640,2944]{1,0:T(8,128)(2,1)}, u32[]{:S(2)}, u32[]{:S(2)}) collective-permute-start(bf16[640,2944]{1,0:T(8,128)(2,1)S(1)} %slice.427), channel_id=1, source_target_pairs={{0,1},{1,0},{2,3},{3,2},{4,5},{5,4},{6,7},{7,6},{8,9},{9,8},{10,11... | collective-permute-start | bytes 11304968 | tf_op jit(solution)/shard_map/ppermute | solution.py:427
  409.5 24.6 %collective-permute-start.44 = (bf16[640,2944]{1,0:T(8,128)(2,1)}, bf16[640,2944]{1,0:T(8,128)(2,1)}, u32[]{:S(2)}, u32[]{:S(2)}) collective-permute-start(bf16[640,2944]{1,0:T(8,128)(2,1)} %slice.546), channel_id=1, source_target_pairs={{0,1},{1,0},{2,3},{3,2},{4,5},{5,4},{6,7},{7,6},{8,9},{9,8},{10,11... | collective-permute-start | bytes 11304968 | tf_op jit(solution)/shard_map/ppermute | solution.py:427
  417.4 27.1 %collective-permute-start.45 = (bf16[320,2944]{1,0:T(8,128)(2,1)S(1)}, bf16[320,2944]{1,0:T(8,128)(2,1)}, u32[]{:S(2)}, u32[]{:S(2)}) collective-permute-start(bf16[320,2944]{1,0:T(8,128)(2,1)S(1)} %slice.547), channel_id=1, source_target_pairs={{0,1},{1,0},{2,3},{3,2},{4,5},{5,4},{6,7},{7,6},{8,9},{9,8},{10,11... | collective-permute-start | bytes 5652488 | tf_op jit(solution)/shard_map/ppermute | solution.py:427
  417.5 43.5 %collective-permute-start.47 = (bf16[320,2944]{1,0:T(8,128)(2,1)S(1)}, bf16[320,2944]{1,0:T(8,128)(2,1)}, u32[]{:S(2)}, u32[]{:S(2)}) collective-permute-start(bf16[320,2944]{1,0:T(8,128)(2,1)S(1)} %slice.547), channel_id=1, source_target_pairs={{0,2},{1,3},{2,0},{3,1},{4,6},{5,7},{6,4},{7,5},{8,10},{9,11},{10,... | collective-permute-start | bytes 5652488 | tf_op jit(solution)/shard_map/ppermute | solution.py:431
  479.4 43.0 %collective-permute-start.48 = (bf16[320,2944]{1,0:T(8,128)(2,1)}, bf16[320,2944]{1,0:T(8,128)(2,1)}, u32[]{:S(2)}, u32[]{:S(2)}) collective-permute-start(bf16[320,2944]{1,0:T(8,128)(2,1)} %get-tuple-element.294), channel_id=1, source_target_pairs={{0,2},{1,3},{2,0},{3,1},{4,6},{5,7},{6,4},{7,5},{8,10},{9,11},{10,... | collective-permute-start | bytes 5652488 | tf_op jit(solution)/shard_map/ppermute | solution.py:431
  481.0 305.4 %reduce-scatter.9.cloned.1.call-start = ((), (), s32[]{:S(2)}) async-start(), calls=%async_computation.6 | async-start | bytes 6782976
  536.5 24.8 %collective-permute-start.51 = (bf16[640,2944]{1,0:T(8,128)(2,1)}, bf16[640,2944]{1,0:T(8,128)(2,1)S(1)}, u32[]{:S(2)}, u32[]{:S(2)}) collective-permute-start(bf16[640,2944]{1,0:T(8,128)(2,1)} %slice.437), channel_id=1, source_target_pairs={{0,1},{1,0},{2,3},{3,2},{4,5},{5,4},{6,7},{7,6},{8,9},{9,8},{10,11... | collective-permute-start | bytes 11304968 | tf_op jit(solution)/shard_map/ppermute | solution.py:427
  605.1 43.8 %collective-permute-start.55 = (bf16[320,2944]{1,0:T(8,128)(2,1)}, bf16[320,2944]{1,0:T(8,128)(2,1)}, u32[]{:S(2)}, u32[]{:S(2)}) collective-permute-start(bf16[320,2944]{1,0:T(8,128)(2,1)} %get-tuple-element.555), channel_id=1, source_target_pairs={{0,2},{1,3},{2,0},{3,1},{4,6},{5,7},{6,4},{7,5},{8,10},{9,11},{10,... | collective-permute-start | bytes 5652488 | tf_op jit(solution)/shard_map/ppermute | solution.py:431
  658.1 28.1 %collective-permute-start.56 = (bf16[128,2944]{0,1:T(8,128)(2,1)}, bf16[128,2944]{0,1:T(8,128)(2,1)}, u32[]{:S(2)}, u32[]{:S(2)}) collective-permute-start(bf16[128,2944]{0,1:T(8,128)(2,1)} %constant_dynamic-slice_fusion.16), channel_id=1, source_target_pairs={{0,4},{4,0},{8,12},{12,8},{16,20},{20,16},{24,28},{28,24},{1,5},{5... | collective-permute-start | bytes 2261000 | tf_op jit(solution)/shard_map/ppermute | solution.py:319
  658.6 42.6 %collective-permute-start.59 = (bf16[320,2944]{1,0:T(8,128)(2,1)}, bf16[320,2944]{1,0:T(8,128)(2,1)}, u32[]{:S(2)}, u32[]{:S(2)}) collective-permute-start(bf16[320,2944]{1,0:T(8,128)(2,1)} %get-tuple-element.335), channel_id=1, source_target_pairs={{0,2},{1,3},{2,0},{3,1},{4,6},{5,7},{6,4},{7,5},{8,10},{9,11},{10,... | collective-permute-start | bytes 5652488 | tf_op jit(solution)/shard_map/ppermute | solution.py:431
  688.5 33.8 %collective-permute-start.57 = (bf16[128,2944]{0,1:T(8,128)(2,1)}, bf16[128,2944]{0,1:T(8,128)(2,1)}, u32[]{:S(2)}, u32[]{:S(2)}) collective-permute-start(bf16[128,2944]{0,1:T(8,128)(2,1)} %fusion.130), channel_id=1, source_target_pairs={{0,8},{4,12},{24,16},{28,20},{1,9},{5,13},{25,17},{29,21},{2,10},{... | collective-permute-start | bytes 2261000 | tf_op jit(solution)/shard_map/ppermute | solution.py:315
  692.0 30.3 %collective-permute-start.58 = (bf16[128,2944]{0,1:T(8,128)(2,1)}, bf16[128,2944]{0,1:T(8,128)(2,1)}, u32[]{:S(2)}, u32[]{:S(2)}) collective-permute-start(bf16[128,2944]{0,1:T(8,128)(2,1)} %get-tuple-element.334), channel_id=1, source_target_pairs={{0,4},{4,0},{8,12},{12,8},{16,20},{20,16},{24,28},{28,24},{1,5},{5... | collective-permute-start | bytes 2261000 | tf_op jit(solution)/shard_map/ppermute | solution.py:319
  935.0 38.5 %collective-permute-start.84 = (bf16[128,2880]{0,1:T(8,128)(2,1)S(1)}, bf16[128,2880]{0,1:T(8,128)(2,1)S(1)}, u32[]{:S(2)}, u32[]{:S(2)}) collective-permute-start(bf16[128,2880]{0,1:T(8,128)(2,1)S(1)} %select_convert_fusion.3), channel_id=1, source_target_pairs={{0,8},{4,12},{8,16},{12,20},{1,9},{5,13},{9,17},{13,21},{2,10},{6,... | collective-permute-start | bytes 2211848 | tf_op jit(solution)/shard_map/ppermute | solution.py:315
  937.2 36.3 %collective-permute-start.85 = (bf16[128,2880]{0,1:T(8,128)(2,1)S(1)}, bf16[128,2880]{0,1:T(8,128)(2,1)S(1)}, u32[]{:S(2)}, u32[]{:S(2)}) collective-permute-start(bf16[128,2880]{0,1:T(8,128)(2,1)S(1)} %select_convert_fusion.3), channel_id=1, source_target_pairs={{24,16},{28,20},{16,8},{20,12},{25,17},{29,21},{17,9},{21,13},{26,... | collective-permute-start | bytes 2211848 | tf_op jit(solution)/shard_map/ppermute | solution.py:315
  937.9 35.6 %collective-permute-start.86 = (bf16[128,2880]{0,1:T(8,128)(2,1)S(1)}, bf16[128,2880]{0,1:T(8,128)(2,1)S(1)}, u32[]{:S(2)}, u32[]{:S(2)}) collective-permute-start(bf16[128,2880]{0,1:T(8,128)(2,1)S(1)} %get-tuple-element.388), channel_id=1, source_target_pairs={{0,4},{4,0},{8,12},{12,8},{16,20},{20,16},{24,28},{28,24},{1,5},{5... | collective-permute-start | bytes 2211848 | tf_op jit(solution)/shard_map/ppermute | solution.py:319
  940.0 32.9 %collective-permute-start.95 = (bf16[128,2880]{0,1:T(8,128)(2,1)S(1)}, bf16[128,2880]{0,1:T(8,128)(2,1)S(1)}, u32[]{:S(2)}, u32[]{:S(2)}) collective-permute-start(bf16[128,2880]{0,1:T(8,128)(2,1)S(1)} %fusion.146), channel_id=1, source_target_pairs={{0,2},{1,3},{2,0},{3,1},{4,6},{5,7},{6,4},{7,5},{8,10},{9,11},{10,... | collective-permute-start | bytes 2211848 | tf_op jit(solution)/shard_map/ppermute | solution.py:431
  974.3 27.9 %collective-permute-start.88 = (bf16[128,2880]{0,1:T(8,128)(2,1)S(1)}, bf16[128,2880]{0,1:T(8,128)(2,1)S(1)}, u32[]{:S(2)}, u32[]{:S(2)}) collective-permute-start(bf16[128,2880]{0,1:T(8,128)(2,1)S(1)} %get-tuple-element.599), channel_id=1, source_target_pairs={{0,8},{4,12},{8,16},{12,20},{16,24},{20,28},{1,9},{5,13},{9,17},{1... | collective-permute-start | bytes 2211848 | tf_op jit(solution)/shard_map/ppermute | solution.py:315
  (223 other events, 2795.8 us)
Sparse Core Ops, SparseCore 0:
  9.6 35.3 all-gather.3
  46.5 27.8 all-gather.5
  267.3 109.1 all-gather.7
  481.1 113.3 reduce-scatter.6
  598.5 137.7 reduce-scatter.8
